TPU v7x, 32 devices: a whole 2x2x4 slice. The times are simulated.
32 devices in a mesh: elem: 8 (over y, x, core), mode: 4 (over z).
Axes of the slice: x: 2, y: 2, z: 4, core: 2. Of those that a mesh axis runs over, the one named last changes fastest.
Arguments:
- u_spec: bfloat16 [1024, 16384], P('mode', 'elem'), may hold values from -6 to 6
- dir_spec: bfloat16 [1024, 16384], P('mode', 'elem'), may hold values from -6 to 6
- advecting: bfloat16 [3, 1024, 16384], P(None, None, ('elem', 'mode')), may hold values from -6 to 6
- viscosity: bfloat16 [1024, 16384], P(None, ('elem', 'mode')), may hold values from 0.099609375 to 2
- degrees: int32 [2, 256], P(None, 'elem'), may hold values from 2 to 7
- edge_side: int32 [1024], P('elem'), may hold values from 0 to 127, as said below
- edge_link: int32 [3, 1024], P(None, 'elem'), may hold values from -1 to 127, as said below
Outputs:
- advect: float32 [1024, 16384], P('mode', 'elem')
- helm_velocity: float32 [1024, 16384], P('mode', 'elem')
- helm_direction: float32 [1024, 16384], P('mode', 'elem')
Inputs may be any that keep to these rules, and one draw needn't show every extreme that they name: `edge_side`: within each partition's 128 slots, no element side appears twice. `edge_link`: A slot with peer -1 is empty and has flag 0 and peer slot 0. Pairing is symmetric: a live slot's partner is live, names it back and has the same flag. A peer is the partition itself (another slot) or a partition one or two places away around the closed loop of 8 partitions. At most 24 live slots of one partition name any one other partition as peer, and some partition has exactly that many with each of its four neighbours. Some partition has all 128 slots live.
All inputs are finite; a program needn't handle non-finite values.
Results may differ from a plain program's by a relative error of at most 0.0055.
Values may be sent and summed in bfloat16 or wider, within the bound.
No kernel may reach another device: no remote copies, remote signals or barrier semaphores. Data moves between devices by JAX's collectives and lax.ppermute only.
A program may use at most 128 MiB of HBM per device.

v0:
```python
import math

import jax
import jax.numpy as jnp
import numpy as np
from jax import lax
from jax.sharding import PartitionSpec as P

NQ = 8


METRIC = 0.125
AREA_SCALE = 64.0
LENGTH = 8.0
HELM_LAMBDA = 4.0
PENALTY = 0.02


def from_behind(block, axis, distance):
    devices = range(lax.axis_size(axis))
    route = [((i - distance) % len(devices), i) for i in devices]
    return lax.ppermute(block, axis, route)


def cheb_tables():
    degree_top = 7
    angles = np.pi * np.arange(degree_top + 1) / degree_top
    cheb_points = np.cos(angles)
    signs_scale = np.ones(degree_top + 1)
    signs_scale[0] = 2.0
    signs_scale[degree_top] = 2.0
    signs_scale = signs_scale * (-1.0) ** np.arange(degree_top + 1)
    differences = cheb_points[:, None] - cheb_points[None, :]
    derivative = (
        signs_scale[:, None] / signs_scale[None, :] / (differences + np.eye(degree_top + 1))
    )
    derivative = derivative - np.eye(degree_top + 1) * derivative.sum(axis=1)[:, None]
    weights = np.zeros(degree_top + 1)
    interior = np.ones(degree_top - 1)
    for k in range(1, (degree_top - 1) // 2 + 1):
        interior = interior - 2.0 * np.cos(2 * k * angles[1:degree_top]) / (4 * k * k - 1)
    weights[0] = 1.0 / (degree_top * degree_top)
    weights[degree_top] = weights[0]
    weights[1:degree_top] = 2.0 * interior / degree_top
    return (derivative, weights)


def node_tables():
    derivative, weights = cheb_tables()
    identity_eight = np.eye(8)
    node_x = np.kron(METRIC * derivative, identity_eight)
    node_y = np.kron(identity_eight, METRIC * derivative)
    mass = AREA_SCALE * np.outer(weights, weights).reshape(-1)
    edge_weight = LENGTH * weights
    return (
        jnp.asarray(node_x, dtype=jnp.float32),
        jnp.asarray(node_y, dtype=jnp.float32),
        jnp.asarray(mass, dtype=jnp.float32),
        jnp.asarray(edge_weight, dtype=jnp.float32),
    )


def synthesis_table(total_count):
    planes = jnp.arange(total_count, dtype=jnp.int32)
    wave_index = planes // 2
    turn_count = planes[:, None] * wave_index[None, :] % total_count
    angles = 2.0 * math.pi / total_count * turn_count.astype(jnp.float32)
    level_scale = math.sqrt(2.0 / total_count)
    parity = (planes % 2)[None, :]
    synthesis = jnp.where(parity == 0, jnp.cos(angles), jnp.sin(angles)) * level_scale
    alternating = (1 - 2 * (planes % 2)).astype(jnp.float32)[:, None] / math.sqrt(total_count)
    column = planes[None, :]
    synthesis = jnp.where(column == 0, jnp.float32(1.0 / math.sqrt(total_count)), synthesis)
    synthesis = jnp.where(column == 1, alternating, synthesis)
    return synthesis.astype(jnp.bfloat16)


def z_derivative(coeffs):
    total_count = coeffs.shape[-2]
    paired = coeffs.reshape(coeffs.shape[:-2] + (total_count // 2, 2, coeffs.shape[-1]))
    rate_table = (4.0 / total_count * jnp.arange(total_count // 2, dtype=jnp.float32))[:, None]
    even_part = rate_table * paired[..., 1, :]
    odd_part = -rate_table * paired[..., 0, :]
    return jnp.stack([even_part, odd_part], axis=-2).reshape(coeffs.shape)


def side_nodes(side_code, position):
    return jnp.where(
        side_code == 0,
        position,
        jnp.where(
            side_code == 1,
            8 * position + 7,
            jnp.where(side_code == 2, 63 - position, 8 * (7 - position)),
        ),
    )


def on_device(u_spec, dir_spec, advecting, viscosity, degrees, edge_side, edge_link):
    node_x, node_y, mass, edge_weight = node_tables()
    modes_count = lax.axis_size("mode")
    local_elements = degrees.shape[1]
    block_elements = local_elements // modes_count
    block_width = NQ * NQ * block_elements
    synthesis = synthesis_table(viscosity.shape[0])
    identity_block = jnp.eye(block_elements, dtype=jnp.float32)
    kron_x = jnp.kron(node_x, identity_block)
    kron_y = jnp.kron(node_y, identity_block)
    mass_block = jnp.repeat(mass, block_elements)
    mass_local = jnp.tile(mass_block, modes_count)
    velocity = advecting.astype(jnp.float32)
    weighted = mass_block[None, :] * viscosity.astype(jnp.float32)
    both_fields = jnp.stack([u_spec, dir_spec], axis=0)
    gathered = lax.all_to_all(both_fields, "mode", split_axis=2, concat_axis=1, tiled=True)
    fields = gathered.shape[0]
    slope_hat = z_derivative(gathered.astype(jnp.float32)).astype(jnp.bfloat16)
    stacked = jnp.concatenate([gathered, slope_hat], axis=0)
    values = jnp.einsum("zk,fkc->fzc", synthesis, stacked, preferred_element_type=jnp.float32)
    plain_phys = values[:fields]
    along_z = values[fields:]
    grad_x = jnp.einsum("fzc,dc->fzd", plain_phys, kron_x, precision=lax.Precision.HIGHEST)
    grad_y = jnp.einsum("fzc,dc->fzd", plain_phys, kron_y, precision=lax.Precision.HIGHEST)
    flat_sum = jnp.einsum(
        "fzd,dc->fzc", weighted[None] * grad_x, kron_x, precision=lax.Precision.HIGHEST
    ) + jnp.einsum("fzd,dc->fzc", weighted[None] * grad_y, kron_y, precision=lax.Precision.HIGHEST)
    pieces = [flat_sum.astype(jnp.bfloat16), (weighted[None] * along_z).astype(jnp.bfloat16)]
    moved_phys = velocity[0] * grad_x[0] + velocity[1] * grad_y[0] + velocity[2] * along_z[0]
    pieces = [moved_phys.astype(jnp.bfloat16)[None]] + pieces
    back_stack = jnp.concatenate(pieces, axis=0)
    coeff_back = jnp.einsum(
        "zk,fzc->fkc", synthesis, back_stack, preferred_element_type=jnp.float32
    )
    leading = 1
    co_flat = coeff_back[leading : leading + fields]
    co_span = coeff_back[leading + fields :]
    volume = co_flat - z_derivative(co_span)
    returned = lax.all_to_all(
        jnp.concatenate([coeff_back[0:1], volume], axis=0).astype(jnp.bfloat16),
        "mode",
        split_axis=1,
        concat_axis=2,
        tiled=True,
    ).astype(jnp.float32)
    advect_out = returned[0]
    volume_velocity = returned[1]
    volume_direction = returned[2]
    fields_spec = jnp.stack([u_spec, dir_spec], axis=0)
    slot_count = edge_side.shape[0]
    local_element = edge_side // 4
    side_code = edge_side % 4
    position = jnp.arange(NQ, dtype=jnp.int32)
    side_node = side_nodes(side_code[:, None], position[None, :])
    slot_columns = (
        (local_element // block_elements)[:, None] * block_width
        + side_node * block_elements
        + (local_element % block_elements)[:, None]
    ).reshape(-1)
    column_ids = jnp.arange(fields_spec.shape[2], dtype=jnp.int32)
    picker = (column_ids[:, None] == slot_columns[None, :]).astype(jnp.bfloat16)
    traces = jnp.einsum(
        "fzc,cs->fzs", fields_spec, picker, preferred_element_type=jnp.float32
    ).astype(jnp.bfloat16)
    element_match = local_element[:, None] == jnp.arange(local_elements, dtype=jnp.int32)[None, :]
    degree_rows = jnp.where((side_code % 2 == 0)[:, None], degrees[0][None, :], degrees[1][None, :])
    normal_degree = jnp.sum(jnp.where(element_match, degree_rows, 0), axis=1).astype(jnp.float32)
    degree_wire = jnp.repeat(normal_degree, NQ).astype(jnp.bfloat16)[None, None, :]
    flip_flag = edge_link[0]
    peer_part = edge_link[1]
    peer_slot = edge_link[2]
    live_slot = peer_part >= 0
    turned = jnp.where(flip_flag[:, None] == 1, NQ - 1 - position[None, :], position[None, :])
    part_count = lax.axis_size("elem")
    my_part = lax.axis_index("elem")
    blocks = [traces]
    degree_blocks = [degree_wire]
    for offset in (1, 2, -1, -2):
        near_block, near_degree = from_behind((traces, degree_wire), "elem", -offset)
        blocks.append(near_block)
        degree_blocks.append(near_degree)
    joined = jnp.concatenate(blocks, axis=2)
    joined_degree = jnp.concatenate(degree_blocks, axis=2)
    distance = (peer_part - my_part) % part_count
    block_code = jnp.where(
        distance == 0,
        0,
        jnp.where(
            distance == 1,
            1,
            jnp.where(distance == 2, 2, jnp.where(distance == part_count - 1, 3, 4)),
        ),
    )
    target = ((block_code * slot_count + peer_slot)[:, None] * NQ + turned).reshape(-1)
    others = jnp.take(joined, target, axis=2)
    other_degree = jnp.take(joined_degree, target, axis=2)
    joint_degree = jnp.maximum(degree_wire, other_degree).astype(jnp.float32)[0, 0]
    strength = PENALTY * (joint_degree + 1.0) * (joint_degree + 1.0)
    factor = jnp.where(jnp.repeat(live_slot, NQ), strength, jnp.float32(0.0)) * jnp.tile(
        edge_weight, slot_count
    )
    factor_columns = jnp.dot(picker.astype(jnp.float32), factor, precision=lax.Precision.HIGHEST)
    others_columns = jnp.einsum("fzs,cs->fzc", others, picker, preferred_element_type=jnp.float32)
    penalty = factor_columns[None, None, :] * (fields_spec.astype(jnp.float32) - others_columns)
    local_part = HELM_LAMBDA * mass_local[None, None, :] * fields_spec.astype(jnp.float32) + penalty
    helm_velocity = local_part[0] + volume_velocity
    helm_direction = local_part[1] + volume_direction
    return (advect_out, helm_velocity, helm_direction)


def solution(mesh):
    in_specs = (
        P("mode", "elem"),
        P("mode", "elem"),
        P(None, None, ("elem", "mode")),
        P(None, ("elem", "mode")),
        P(None, "elem"),
        P("elem"),
        P(None, "elem"),
    )
    out_specs = (P("mode", "elem"), P("mode", "elem"), P("mode", "elem"))
    return jax.shard_map(
        on_device, mesh=mesh, in_specs=in_specs, out_specs=out_specs, check_vma=False
    )
```

profile of v0, /device:TPU:0, one launch (start us, length us, event | category | flops | bytes accessed | tf_op | source)
XLA Modules:
  0.0 353.8 jit_solution(12351588935201045884)
XLA Ops:
  2.3 5.4 %constant_dynamic-update-slice_fusion.9 = (bf16[2,256,5120]{2,1,0:T(8,128)(2,1)}, bf16[2,256,1024]{2,1,0:T(8,128)(2,1)}) fusion(s32[1024]{0:T(1024)S(1)} %reshape.363, bf16[1,256,2048]{2,1,0:T(8,128)(2,1)} %bitcast.101, bf16[1,256,2048]{2,1,0:T(8,128)(2,1)} %bitcast.104), kind=kOutput, calls=%fused_computation.89 | convolution fusion | flops 2151153664 | bytes 4198400 | tf_op jit(solution)/shard_map/fzc,cs->fzs/dot_general | solution.py:160
  17.2 5.1 %all-to-all-start = ((bf16[2,256,2048]{1,0,2:T(2,128)(2,1)}), bf16[2,256,2048]{1,0,2:T(2,128)(2,1)}, u32[]{:S(2)}, u32[]{:S(2)}) async-start(bf16[2,256,2048]{1,0,2:T(2,128)(2,1)} %copy.67), calls=%async_computation | async-start | bytes 4194304 | tf_op jit(solution)/shard_map/all_to_all | solution.py:114
  22.3 12.0 %broadcast_multiply_fusion.1 = (f32[64,8,64,8]{3,2,1,0:T(8,128)}, f32[64,8,64,8]{3,2,1,0:T(8,128)}) fusion(f32[8,8]{1,0:T(8,128)S(1)} %fusion.68, f32[64,64]{1,0:T(8,128)S(1)} %copy-done.11, f32[64,64]{1,0:T(8,128)S(1)} %copy-done.12), kind=kLoop, calls=%fused_computation.8 | loop fusion | flops 524288 | bytes 2130176 | tf_op jit(solution)/shard_map/jit(kron)/mul | solution.py:107
  34.3 13.4 %reshape.389 = f32[512,512,1]{1,0,2:T(8,128)} reshape(f32[64,8,64,8]{3,2,1,0:T(8,128)} %get-tuple-element.18) | data formatting | bytes 2097152 | tf_op jit(solution)/shard_map/jit(kron)/mul | solution.py:107
  47.7 13.4 %reshape.390 = f32[512,512,1]{1,0,2:T(8,128)} reshape(f32[64,8,64,8]{3,2,1,0:T(8,128)} %get-tuple-element.19) | data formatting | bytes 2097152 | tf_op jit(solution)/shard_map/jit(kron)/mul | solution.py:108
  72.7 18.3 %fusion.113 = bf16[1024,1024,1]{1,0,2:T(8,128)(2,1)} fusion(s32[1024]{0:T(1024)S(1)} %add_select_fusion.1, bf16[1024]{0:T(1024)(128)(2,1)S(1)} %convert_multiply_fusion.2, pred[1024]{0:T(1024)(128)(4,1)S(1)} %get-tuple-element.32, pred[1024]{0:T(1024)(128)(4,1)S(1)} %get-tuple-element.31, pred[1024]{0:T(1024)(128)(4,1)S(1)} %iota_compare_fusion.5), kind=kLoop, calls=%fused_computation.50.clone.clone.2 | loop fusion | flops 18874368 | bytes 2106368 | tf_op jit(solution)/shard_map/zk,fzc->fkc/dot_general | solution.py:130
  91.0 10.4 %copy.68 = bf16[2,256,4,512]{3,0,1,2:T(2,128)(2,1)} copy(bf16[2,256,4,512]{1,0,3,2:T(2,128)(2,1)} %bitcast.2) | data formatting | bytes 4194304 | tf_op jit(solution)/shard_map/all_to_all | solution.py:114
  106.9 4.0 %pad_maximum_fusion.3 = bf16[2,512,2,512]{3,0,2,1:T(2,128)(2,1)} fusion(bf16[2,512,1,512]{3,0,2,1:T(2,128)(2,1)S(1)} %get-tuple-element.17, bf16[2,512,1,512]{3,0,2,1:T(2,128)(2,1)S(1)} %get-tuple-element.16), kind=kLoop, calls=%fused_computation.69 | loop fusion | flops 1048576 | bytes 4194304 | tf_op jit(solution)/shard_map/stack | solution.py:84
  110.9 6.1 %copy.70 = bf16[2,1024,512]{1,2,0:T(8,128)(2,1)} copy(bf16[2,1024,512]{2,0,1:T(2,128)(2,1)} %bitcast.98) | data formatting | bytes 4194304 | tf_op jit(solution)/shard_map/convert_element_type | solution.py:116
  117.0 4.5 %copy.69 = bf16[2,4,256,512]{2,1,3,0:T(4,128)(2,1)} copy(bf16[2,4,256,512]{2,0,3,1:T(2,128)(2,1)} %bitcast.4) | data formatting | bytes 4194304 | tf_op jit(solution)/shard_map/all_to_all | solution.py:114
  121.6 4.8 %all_to_all.23 = bf16[2,1024,512]{1,2,0:T(8,128)(2,1)} reshape(bf16[2,4,256,512]{2,1,3,0:T(4,128)(2,1)} %copy.69) | data formatting | bytes 4194304 | tf_op jit(solution)/shard_map/all_to_all | solution.py:114
  129.0 19.7 %fusion.36 = f32[4,1024,512]{1,2,0:T(8,128)S(1)} fusion(s32[1024]{0:T(1024)S(1)} %add_select_fusion.1, bf16[1024]{0:T(1024)(128)(2,1)S(1)} %convert_multiply_fusion.2, pred[1024]{0:T(1024)(128)(4,1)S(1)} %get-tuple-element.32, pred[1024]{0:T(1024)(128)(4,1)S(1)} %get-tuple-element.31, pred[1024]{0:T(1024)(128)(4,1)S(1)} %iota_compare_fusion.5, ...), kind=kOutput, calls=%fused_computation.48 | convolution fusion | flops 4313841664 | bytes 12592128 | tf_op jit(solution)/shard_map/zk,fkc->fzc/dot_general | solution.py:118
  148.8 7.5 %fusion.92 = f32[2,1024,512]{1,2,0:T(8,128)S(1)} fusion(f32[4,1024,512]{1,2,0:T(8,128)S(1)} %fusion.36, f32[512,512,1]{1,0,2:T(8,128)S(1)} %copy-done), kind=kOutput, calls=%fused_computation.172 | convolution fusion | flops 6442450944 | bytes 13631488 | tf_op jit(solution)/shard_map/fzc,dc->fzd/dot_general | solution.py:121
  156.2 7.2 %fusion.93 = f32[2,1024,512]{1,2,0:T(8,128)S(1)} fusion(f32[4,1024,512]{1,2,0:T(8,128)S(1)} %fusion.36, f32[512,512,1]{1,0,2:T(8,128)S(1)} %copy-done.1), kind=kOutput, calls=%fused_computation.173 | convolution fusion | flops 6442450944 | bytes 13631488 | tf_op jit(solution)/shard_map/fzc,dc->fzd/dot_general | solution.py:122
  165.6 9.0 %fusion.26 = f32[2,1024,512]{1,2,0:T(8,128)} fusion(f32[512,512,1]{1,0,2:T(8,128)S(1)} %copy-done.1, f32[2,1024,512]{1,2,0:T(8,128)S(1)} %fusion.93, f32[1024,512]{0,1:T(8,128)S(1)} %copy.75), kind=kOutput, calls=%fused_computation.39 | convolution fusion | flops 6443499520 | bytes 11534336 | tf_op jit(solution)/shard_map/fzd,dc->fzc/dot_general | solution.py:125
  176.9 9.1 %add_convert_fusion = bf16[2,1024,512]{1,2,0:T(8,128)(2,1)S(1)} fusion(f32[2,1024,512]{1,2,0:T(8,128)} %fusion.26, f32[512,512,1]{1,0,2:T(8,128)S(1)} %copy-done, f32[2,1024,512]{1,2,0:T(8,128)S(1)} %fusion.92, f32[1024,512]{0,1:T(8,128)S(1)} %copy.75), kind=kOutput, calls=%fused_computation.38 | convolution fusion | flops 6445596672 | bytes 13631488 | tf_op jit(solution)/shard_map/fzd,dc->fzc/dot_general | solution.py:123
  186.0 5.7 %fusion.33 = f32[5,1024,512]{1,2,0:T(8,128)S(1)} fusion(bf16[2,1024,512]{1,2,0:T(8,128)(2,1)S(1)} %copy-done.5, bf16[2,1024,512]{1,2,0:T(8,128)(2,1)S(1)} %add_convert_fusion, bf16[1,1024,512]{1,2,0:T(8,128)(2,1)S(1)} %copy-done.10, bf16[1024,1024,1]{1,0,2:T(8,128)(2,1)S(1)} %copy-done.17), kind=kOutput, calls=%fused_computation.47 | convolution fusion | flops 5373952000 | bytes 17825792 | tf_op jit(solution)/shard_map/zk,fzc->fkc/dot_general | solution.py:130
  198.2 7.2 %copy.82 = f32[2,1024,512]{2,0,1:T(2,128)} copy(f32[2,1024,512]{1,2,0:T(8,128)} %slice.126) | data formatting | bytes 8388608 | tf_op jit(solution)/shard_map/slice | solution.py:135
  205.4 4.1 %slice_multiply_fusion.2 = (f32[2,512,1,512]{3,0,2,1:T(2,128)S(1)}, f32[2,512,1,512]{3,0,2,1:T(2,128)S(1)}) fusion(f32[2,512,2,512]{3,0,2,1:T(2,128)} %bitcast.96, f32[512]{0:T(512)S(1)} %get-tuple-element.29, f32[512]{0:T(512)S(1)} %get-tuple-element.30), kind=kLoop, calls=%fused_computation.56 | loop fusion | flops 1048576 | bytes 8392704 | tf_op jit(solution)/shard_map/mul | solution.py:82
  213.4 7.2 %copy.83 = f32[2,1024,512]{1,2,0:T(8,128)} copy(f32[2,1024,512]{2,0,1:T(2,128)} %bitcast.95) | data formatting | bytes 8388608 | tf_op jit(solution)/shard_map/reshape | solution.py:84
  220.6 4.3 %fusion.17 = bf16[2,1024,512]{1,2,0:T(8,128)(2,1)S(1)} fusion(f32[2,1024,512]{1,2,0:T(8,128)} %copy.83, f32[5,1024,512]{1,2,0:T(8,128)} %copy-done.2), kind=kLoop, calls=%fused_computation.27 | loop fusion | flops 2097152 | bytes 10485760 | tf_op jit(solution)/shard_map/convert.4
  225.2 5.7 %copy.84 = bf16[3,1024,512]{2,0,1:T(4,128)(2,1)} copy(bf16[3,1024,512]{1,2,0:T(8,128)(2,1)S(1)} %pad_maximum_fusion.1) | data formatting | bytes 6291456 | tf_op jit(solution)/shard_map/concatenate | solution.py:138
  231.0 5.2 %all-to-all-start.1 = ((bf16[3,1024,512]{2,0,1:T(4,128)(2,1)}), bf16[3,1024,512]{2,0,1:T(4,128)(2,1)}, u32[]{:S(2)}, u32[]{:S(2)}) async-start(bf16[3,1024,512]{2,0,1:T(4,128)(2,1)} %copy.84), calls=%async_computation.1 | async-start | bytes 8388608 | tf_op jit(solution)/shard_map/all_to_all | solution.py:137
  243.3 4.0 %collective-permute-done.2 = bf16[1,1,1024]{2,1,0:T(2,128)(2,1)S(1)} collective-permute-done((bf16[1,1,1024]{2,1,0:T(2,128)(2,1)S(1)}, bf16[1,1,1024]{2,1,0:T(2,128)(2,1)S(1)}, u32[]{:S(2)}, u32[]{:S(2)}) %collective-permute-start.2) | collective-permute-done | bytes 2080 | tf_op jit(solution)/shard_map/ppermute | solution.py:22
  247.4 4.5 %collective-permute-done.3 = bf16[1,1,1024]{2,1,0:T(2,128)(2,1)S(1)} collective-permute-done((bf16[1,1,1024]{2,1,0:T(2,128)(2,1)S(1)}, bf16[1,1,1024]{2,1,0:T(2,128)(2,1)S(1)}, u32[]{:S(2)}, u32[]{:S(2)}) %collective-permute-start.3) | collective-permute-done | bytes 2080 | tf_op jit(solution)/shard_map/ppermute | solution.py:22
  251.9 7.0 %gather_fusion = bf16[1024]{0:T(1024)(128)(2,1)S(1)} fusion(bf16[5120]{0:T(1024)(128)(2,1)S(1)} %reduce, s32[1024]{0:T(1024)S(1)} %broadcast_clamp_fusion), kind=kCustom, calls=%fused_computation | custom fusion | bytes 8192 | tf_op jit(solution)/shard_map/jit(_take)/gather | solution.py:194
  272.0 13.6 %copy.86 = bf16[2,256,5120]{1,0,2:T(2,128)(2,1)} copy(bf16[2,256,5120]{2,1,0:T(8,128)(2,1)} %constant_dynamic-update-slice_fusion.5) | data formatting | bytes 10485760 | tf_op jit(solution)/shard_map/concatenate | solution.py:180
  285.6 6.8 %gather_fusion.1 = bf16[1024,2,256]{2,1,0:T(2,128)(2,1)S(1)} fusion(bf16[2,256,5120]{1,0,2:T(2,128)(2,1)} %copy.86, s32[1024]{0:T(1024)S(1)} %broadcast_clamp_fusion), kind=kCustom, calls=%fused_computation.1 | custom fusion | bytes 2101248 | tf_op jit(solution)/shard_map/jit(_take)/gather | solution.py:193
  296.3 5.0 %fusion.12 = f32[2,256,2048]{2,1,0:T(8,128)} fusion(s32[1024]{0:T(1024)S(1)} %reshape.363, f32[2048]{0:T(1024)S(1)} %bitcast.110, f32[2048]{0:T(1024)S(1)} %bitcast.108, bf16[2,256,1024]{1,0,2:T(2,128)(2,1)S(1)} %fusion.59, bf16[1,256,2048]{2,1,0:T(8,128)(2,1)S(1)} %bitcast.103, bf16[1,256,2048]{2,1,0:T(8,128)(2,1)S(1)} %bitcast.106), kind=kOutput, calls=%fused_computation.21 | convolution fusion | flops 2155872256 | bytes 7360512 | tf_op jit(solution)/shard_map/fzs,cs->fzc/dot_general | solution.py:201
  301.3 28.4 %all-to-all-done.1 = bf16[3,1024,512]{2,0,1:T(4,128)(2,1)} async-done(((bf16[3,1024,512]{2,0,1:T(4,128)(2,1)}), bf16[3,1024,512]{2,0,1:T(4,128)(2,1)}, u32[]{:S(2)}, u32[]{:S(2)}) %all-to-all-start.1) | async-done | bytes 3145760 | tf_op jit(solution)/shard_map/all_to_all | solution.py:137
  329.7 5.2 %copy.102 = f32[3,4,256,512]{3,1,2,0:T(4,128)S(1)} copy(bf16[3,4,256,512]{3,0,2,1:T(4,128)(2,1)} %bitcast.30) | data formatting | bytes 9437184 | tf_op jit(solution)/shard_map/convert_element_type | solution.py:143
  348.6 5.0 %fusion.42 = (f32[256,2048]{1,0:T(8,128)}, f32[256,2048]{1,0:T(8,128)}) fusion(f32[1,256,2048]{2,1,0:T(8,128)S(1)} %copy-done.3, f32[2,256,2048]{2,1,0:T(8,128)} %fusion.12, f32[1,256,2048]{2,1,0:T(8,128)S(1)} %slice.107), kind=kLoop, calls=%fused_computation.52 | loop fusion | flops 1048576 | bytes 12582912 | tf_op jit(solution)/shard_map/add | solution.py:205
  (125 shorter events, 83.3 us)
Async XLA Ops:
  2.3 10.8 %copy-start.6 = (bf16[256,2048]{1,0:T(8,128)(2,1)S(1)}, bf16[256,2048]{1,0:T(8,128)(2,1)}, u32[]{:S(2)}) copy-start(bf16[256,2048]{1,0:T(8,128)(2,1)} %param.12) | copy-start | bytes 3145732
  2.3 10.8 %copy-start.8 = (bf16[256,2048]{1,0:T(8,128)(2,1)S(1)}, bf16[256,2048]{1,0:T(8,128)(2,1)}, u32[]{:S(2)}) copy-start(bf16[256,2048]{1,0:T(8,128)(2,1)} %param.11) | copy-start | bytes 3145732
  7.7 255.0 %collective-permute-start.4 = (bf16[2,256,1024]{2,1,0:T(8,128)(2,1)}, bf16[2,256,1024]{2,1,0:T(8,128)(2,1)}, u32[]{:S(2)}, u32[]{:S(2)}) collective-permute-start(bf16[2,256,1024]{2,1,0:T(8,128)(2,1)} %get-tuple-element.28), channel_id=1, source_target_pairs={{4,0},{8,4},{12,8},{16,12},{20,16},{24,20},{28,24},{0,28},{5,1},{9... | collective-permute-start | bytes 3145736 | tf_op jit(solution)/shard_map/ppermute | solution.py:22
  11.1 254.0 %collective-permute-start.5 = (bf16[2,256,1024]{2,1,0:T(8,128)(2,1)}, bf16[2,256,1024]{2,1,0:T(8,128)(2,1)}, u32[]{:S(2)}, u32[]{:S(2)}) collective-permute-start(bf16[2,256,1024]{2,1,0:T(8,128)(2,1)} %get-tuple-element.28), channel_id=1, source_target_pairs={{8,0},{12,4},{16,8},{20,12},{24,16},{28,20},{0,24},{4,28},{9,1},{1... | collective-permute-start | bytes 3145736 | tf_op jit(solution)/shard_map/ppermute | solution.py:22
  11.6 255.8 %collective-permute-start.6 = (bf16[2,256,1024]{2,1,0:T(8,128)(2,1)}, bf16[2,256,1024]{2,1,0:T(8,128)(2,1)}, u32[]{:S(2)}, u32[]{:S(2)}) collective-permute-start(bf16[2,256,1024]{2,1,0:T(8,128)(2,1)} %get-tuple-element.28), channel_id=1, source_target_pairs={{28,0},{0,4},{4,8},{8,12},{12,16},{16,20},{20,24},{24,28},{29,1},{... | collective-permute-start | bytes 3145736 | tf_op jit(solution)/shard_map/ppermute | solution.py:22
  11.8 257.8 %collective-permute-start.7 = (bf16[2,256,1024]{2,1,0:T(8,128)(2,1)}, bf16[2,256,1024]{2,1,0:T(8,128)(2,1)}, u32[]{:S(2)}, u32[]{:S(2)}) collective-permute-start(bf16[2,256,1024]{2,1,0:T(8,128)(2,1)} %get-tuple-element.28), channel_id=1, source_target_pairs={{24,0},{28,4},{0,8},{4,12},{8,16},{12,20},{16,24},{20,28},{25,1},{... | collective-permute-start | bytes 3145736 | tf_op jit(solution)/shard_map/ppermute | solution.py:22
  13.3 9.0 %copy-start.11 = (f32[64,64]{1,0:T(8,128)S(1)}, f32[64,64]{1,0:T(8,128)}, u32[]{:S(2)}) copy-start(f32[64,64]{1,0:T(8,128)} %constant.185.clone) | copy-start | bytes 49156
  13.3 8.9 %copy-start.12 = (f32[64,64]{1,0:T(8,128)S(1)}, f32[64,64]{1,0:T(8,128)}, u32[]{:S(2)}) copy-start(f32[64,64]{1,0:T(8,128)} %constant.186.clone) | copy-start | bytes 49156
  17.2 73.8 %all-to-all-start = ((bf16[2,256,2048]{1,0,2:T(2,128)(2,1)}), bf16[2,256,2048]{1,0,2:T(2,128)(2,1)}, u32[]{:S(2)}, u32[]{:S(2)}) async-start(bf16[2,256,2048]{1,0,2:T(2,128)(2,1)} %copy.67), calls=%async_computation | async-start | bytes 4194304 | tf_op jit(solution)/shard_map/all_to_all | solution.py:114
  64.3 3.4 copy-start.16
  129.0 19.8 %copy-start = (f32[512,512,1]{1,0,2:T(8,128)S(1)}, f32[512,512,1]{1,0,2:T(8,128)}, u32[]{:S(2)}) copy-start(f32[512,512,1]{1,0,2:T(8,128)} %reshape.389) | copy-start | bytes 3145732
  148.7 7.5 %copy-start.1 = (f32[512,512,1]{1,0,2:T(8,128)S(1)}, f32[512,512,1]{1,0,2:T(8,128)}, u32[]{:S(2)}) copy-start(f32[512,512,1]{1,0,2:T(8,128)} %reshape.390) | copy-start | bytes 3145732
  163.5 11.2 %slice-start = ((s8[6291456]{0:T(1024)(128)(4,1)}), s8[4194304]{0:T(1024)(128)(4,1)S(1)}, s32[]{:S(2)}) async-start(s8[6291456]{0:T(1024)(128)(4,1)} %bitcast.93), calls=%async_computation.2 | async-start | bytes 8388608
  165.6 9.1 %slice-start.1 = ((s8[6291456]{0:T(1024)(128)(4,1)}), s8[2097152]{0:T(1024)(128)(4,1)S(1)}, s32[]{:S(2)}) async-start(s8[6291456]{0:T(1024)(128)(4,1)} %bitcast.93), calls=%async_computation.3 | async-start | bytes 4194304
  176.9 9.1 %copy-start.5 = (bf16[2,1024,512]{1,2,0:T(8,128)(2,1)S(1)}, bf16[2,1024,512]{1,2,0:T(8,128)(2,1)}, u32[]{:S(2)}) copy-start(bf16[2,1024,512]{1,2,0:T(8,128)(2,1)} %fusion.18) | copy-start | bytes 6291460
  176.9 9.1 %copy-start.10 = (bf16[1,1024,512]{1,2,0:T(8,128)(2,1)S(1)}, bf16[1,1024,512]{1,2,0:T(8,128)(2,1)}, u32[]{:S(2)}) copy-start(bf16[1,1024,512]{1,2,0:T(8,128)(2,1)} %fusion.45) | copy-start | bytes 3145732
  176.9 9.1 %copy-start.17 = (bf16[1024,1024,1]{1,0,2:T(8,128)(2,1)S(1)}, bf16[1024,1024,1]{1,0,2:T(8,128)(2,1)}, u32[]{:S(2)}) copy-start(bf16[1024,1024,1]{1,0,2:T(8,128)(2,1)} %fusion.113) | copy-start | bytes 6291460
  191.8 5.3 %copy-start.2 = (f32[5,1024,512]{1,2,0:T(8,128)}, f32[5,1024,512]{1,2,0:T(8,128)S(1)}, u32[]{:S(2)}) copy-start(f32[5,1024,512]{1,2,0:T(8,128)S(1)} %fusion.33) | copy-start | bytes 31457284
  220.6 4.3 %copy-start.4 = (bf16[1,1024,512]{1,2,0:T(8,128)(2,1)S(1)}, bf16[1,1024,512]{1,2,0:T(8,128)(2,1)}, u32[]{:S(2)}) copy-start(bf16[1,1024,512]{1,2,0:T(8,128)(2,1)} %slice.179) | copy-start | bytes 3145732
  230.9 5.2 %copy-start.14 = (s32[2,32]{1,0:T(2,128)S(1)}, s32[2,32]{1,0:T(2,128)}, u32[]{:S(2)}) copy-start(s32[2,32]{1,0:T(2,128)} %param.15) | copy-start | bytes 772
  230.9 7.4 %copy-start.13 = (s32[3,128]{1,0:T(4,128)S(1)}, s32[3,128]{1,0:T(4,128)}, u32[]{:S(2)}) copy-start(s32[3,128]{1,0:T(4,128)} %param.17) | copy-start | bytes 4612
  231.0 8.1 %copy-start.15 = (f32[8]{0:T(128)S(1)}, f32[8]{0:T(128)}, u32[]{:S(2)}) copy-start(f32[8]{0:T(128)} %constant.188.clone) | copy-start | bytes 100
  231.0 98.8 %all-to-all-start.1 = ((bf16[3,1024,512]{2,0,1:T(4,128)(2,1)}), bf16[3,1024,512]{2,0,1:T(4,128)(2,1)}, u32[]{:S(2)}, u32[]{:S(2)}) async-start(bf16[3,1024,512]{2,0,1:T(4,128)(2,1)} %copy.84), calls=%async_computation.1 | async-start | bytes 8388608 | tf_op jit(solution)/shard_map/all_to_all | solution.py:137
  236.5 3.2 collective-permute-start
  239.7 3.6 %collective-permute-start.1 = (bf16[1,1,1024]{2,1,0:T(2,128)(2,1)S(1)}, bf16[1,1,1024]{2,1,0:T(2,128)(2,1)S(1)}, u32[]{:S(2)}, u32[]{:S(2)}) collective-permute-start(bf16[1,1,1024]{2,1,0:T(2,128)(2,1)S(1)} %convert_element_type.123), channel_id=1, source_target_pairs={{8,0},{12,4},{16,8},{20,12},{24,16},{28,20},{0,24},{4,28},{9,1},{1... | collective-permute-start | bytes 6152 | tf_op jit(solution)/shard_map/ppermute | solution.py:22
  243.3 4.0 %collective-permute-start.2 = (bf16[1,1,1024]{2,1,0:T(2,128)(2,1)S(1)}, bf16[1,1,1024]{2,1,0:T(2,128)(2,1)S(1)}, u32[]{:S(2)}, u32[]{:S(2)}) collective-permute-start(bf16[1,1,1024]{2,1,0:T(2,128)(2,1)S(1)} %convert_element_type.123), channel_id=1, source_target_pairs={{28,0},{0,4},{4,8},{8,12},{12,16},{16,20},{20,24},{24,28},{29,1},{... | collective-permute-start | bytes 6152 | tf_op jit(solution)/shard_map/ppermute | solution.py:22
  247.4 4.5 %collective-permute-start.3 = (bf16[1,1,1024]{2,1,0:T(2,128)(2,1)S(1)}, bf16[1,1,1024]{2,1,0:T(2,128)(2,1)S(1)}, u32[]{:S(2)}, u32[]{:S(2)}) collective-permute-start(bf16[1,1,1024]{2,1,0:T(2,128)(2,1)S(1)} %convert_element_type.123), channel_id=1, source_target_pairs={{24,0},{28,4},{0,8},{4,12},{8,16},{12,20},{16,24},{20,28},{25,1},{... | collective-permute-start | bytes 6152 | tf_op jit(solution)/shard_map/ppermute | solution.py:22
  285.6 10.7 %copy-start.7 = (bf16[256,2048]{1,0:T(8,128)(2,1)S(1)}, bf16[256,2048]{1,0:T(8,128)(2,1)}, u32[]{:S(2)}) copy-start(bf16[256,2048]{1,0:T(8,128)(2,1)} %param.12) | copy-start | bytes 3145732
  285.6 10.7 %copy-start.9 = (bf16[256,2048]{1,0:T(8,128)(2,1)S(1)}, bf16[256,2048]{1,0:T(8,128)(2,1)}, u32[]{:S(2)}) copy-start(bf16[256,2048]{1,0:T(8,128)(2,1)} %param.11) | copy-start | bytes 3145732
  344.6 3.9 %copy-start.3 = (f32[1,256,2048]{2,1,0:T(8,128)S(1)}, f32[1,256,2048]{2,1,0:T(8,128)}, u32[]{:S(2)}) copy-start(f32[1,256,2048]{2,1,0:T(8,128)} %slice.110) | copy-start | bytes 6291460
where the time goes:
time: 359 us; the launch traced here: 354 us
  local copies, waits for them, and re-layouts  145 us (40%)
  other arithmetic  76.4 us (21%)
  matrix products  72.4 us (20%)
  waiting for transfers between devices  40.5 us (11%)
  starting transfers between devices  18.1 us (5%)
    all_to_all x1, waiting for transfers between devices, on_device(): lax.all_to_all(jnp.concatenate([coeff_back[0:1], volume], axis=0).astype(...  28.4 us
    all_to_all x3, local copies, waits for them, and re-layouts, on_device(): lax.all_to_all(both_fields, 'mode', split_axis=2, concat_axis=1, tiled=True)  19.7 us
    dot_general x1, matrix products, on_device(): jnp.einsum('zk,fkc->fzc', synthesis, stacked, preferred_element_type=jnp....  19.7 us
    dot_general x1, other arithmetic, on_device(): jnp.einsum('zk,fzc->fkc', synthesis, back_stack, preferred_element_type=j...  18.3 us
    unnamed x51, local copies, waits for them, and re-layouts  16.8 us
    concatenate x2, local copies, waits for them, and re-layouts, on_device(): joined = jnp.concatenate(blocks, axis=2)  15.9 us
    mul x1, local copies, waits for them, and re-layouts, on_device(): kron_x = jnp.kron(node_x, identity_block)  13.4 us
    mul x1, local copies, waits for them, and re-layouts, on_device(): kron_y = jnp.kron(node_y, identity_block)  13.4 us
  transfers between devices with their start and end apart: 10, of which 5 were waited for; matrix products, arithmetic and copies ran while one was open for 72% of the time, Pallas kernels for 0%

commit v1 on v0

v1 whole, which is shorter than its diff:
```python
import functools
import math

import jax
import jax.numpy as jnp
import ml_dtypes
import numpy as np
from jax import lax
from jax.experimental import pallas as pl
from jax.experimental.pallas import tpu as pltpu
from jax.sharding import PartitionSpec as P

NQ = 8
METRIC = 0.125
AREA_SCALE = 64.0
LENGTH = 8.0
HELM_LAMBDA = 4.0
PENALTY = 0.02
OFFSETS = (1, 2, -1, -2)
MSG = 256
VMEM_LIMIT = 56 * 1024 * 1024

F32 = jnp.float32
BF16 = jnp.bfloat16
VMEM = pl.BlockSpec(memory_space=pltpu.VMEM)
SMEM = pl.BlockSpec(memory_space=pltpu.SMEM)
NT = (((1,), (1,)), ((), ()))


def cheb_tables():
    degree_top = 7
    angles = np.pi * np.arange(degree_top + 1) / degree_top
    cheb_points = np.cos(angles)
    signs_scale = np.ones(degree_top + 1)
    signs_scale[0] = 2.0
    signs_scale[degree_top] = 2.0
    signs_scale = signs_scale * (-1.0) ** np.arange(degree_top + 1)
    differences = cheb_points[:, None] - cheb_points[None, :]
    derivative = (
        signs_scale[:, None] / signs_scale[None, :] / (differences + np.eye(degree_top + 1))
    )
    derivative = derivative - np.eye(degree_top + 1) * derivative.sum(axis=1)[:, None]
    weights = np.zeros(degree_top + 1)
    interior = np.ones(degree_top - 1)
    for k in range(1, (degree_top - 1) // 2 + 1):
        interior = interior - 2.0 * np.cos(2 * k * angles[1:degree_top]) / (4 * k * k - 1)
    weights[0] = 1.0 / (degree_top * degree_top)
    weights[degree_top] = weights[0]
    weights[1:degree_top] = 2.0 * interior / degree_top
    return (derivative, weights)


def split_pair(matrix):
    matrix = matrix.astype(np.float32)
    high = matrix.astype(ml_dtypes.bfloat16)
    low = (matrix - high.astype(np.float32)).astype(ml_dtypes.bfloat16)
    return np.concatenate([high, high, low], axis=0)


def synthesis_tables(total):
    planes = np.arange(total)
    turn = (planes[:, None] * (planes // 2)[None, :]) % total
    angles = np.float32(2.0 * math.pi / total) * turn.astype(np.float32)
    angles = angles.astype(np.float64)
    table = np.where(planes[None, :] % 2 == 0, np.cos(angles), np.sin(angles))
    table = table * math.sqrt(2.0 / total)
    table[:, 0] = 1.0 / math.sqrt(total)
    table[:, 1] = (1 - 2 * (planes % 2)) / math.sqrt(total)
    rounded = table.astype(np.float32).astype(ml_dtypes.bfloat16)
    exact = rounded.astype(np.float64)
    rate = 4.0 / total * (planes[::2] // 2)
    sloped = np.zeros_like(exact)
    sloped[:, 1::2] = exact[:, 0::2] * rate[None, :]
    sloped[:, 0::2] = -exact[:, 1::2] * rate[None, :]
    return rounded, sloped.astype(np.float32).astype(ml_dtypes.bfloat16)


def shift_of(number):
    assert number & (number - 1) == 0
    return number.bit_length() - 1


def dot(a, b):
    return jnp.dot(a, b, preferred_element_type=F32)


def dot_split(value, table):
    high = value.astype(BF16)
    low = (value - high.astype(F32)).astype(BF16)
    return dot(jnp.concatenate([high, low, high], axis=1), table)


def planes_kernel(
    modes, advected, me_ref, *refs
):
    pieces = refs[:modes]
    (s_ref, sz_ref, t_ref, tz_ref, visc_ref, mass_ref, rx_ref, ry_ref, kx_ref, ky_ref) = refs[
        modes : modes + 10
    ]
    refs = refs[modes + 10 :]
    if advected:
        adv_ref = refs[0]
        refs = refs[1:]
    outs = refs[:modes]
    spec, flat, flux = refs[modes : modes + 3]
    moved = refs[modes + 3] if advected else None
    me = me_ref[0]
    rows = pieces[0].shape[0]
    total, width = visc_ref.shape
    group = ry_ref.shape[1]
    for d in range(modes):
        block = lax.rem(me - d + modes, modes)
        spec[pl.ds(pl.multiple_of(block * rows, rows), rows), :] = pieces[d][...]
    chunk = min(256, total)

    def grouped(value, ref):
        parts = [
            dot_split(value[:, g : g + group], ref[...]) for g in range(0, width, group)
        ]
        return parts[0] if len(parts) == 1 else jnp.concatenate(parts, axis=1)

    def forward(step, carry):
        at = pl.ds(pl.multiple_of(step * chunk, chunk), chunk)
        coeffs = spec[...]
        plain = dot(s_ref[at, :], coeffs)
        along = dot(sz_ref[at, :], coeffs)
        grad_x = dot_split(plain, rx_ref[...])
        grad_y = grouped(plain, ry_ref)
        weighted = mass_ref[...] * visc_ref[at, :].astype(F32)
        if advected:
            moved[at, :] = (
                adv_ref[0, at, :].astype(F32) * grad_x
                + adv_ref[1, at, :].astype(F32) * grad_y
                + adv_ref[2, at, :].astype(F32) * along
            ).astype(BF16)
        flux[at, :] = (weighted * along).astype(BF16)
        flat_sum = dot_split(weighted * grad_x, kx_ref[...]) + grouped(weighted * grad_y, ky_ref)
        flat[at, :] = flat_sum.astype(BF16)
        return carry

    lax.fori_loop(0, total // chunk, forward, 0)

    for d in range(modes):
        block = lax.rem(me + d, modes)
        at = pl.ds(pl.multiple_of(block * rows, rows), rows)
        volume = dot(t_ref[at, :], flat[...]) + dot(tz_ref[at, :], flux[...])
        if advected:
            outs[d][0] = dot(t_ref[at, :], moved[...]).astype(BF16)
            outs[d][1] = volume.astype(BF16)
        else:
            outs[d][0] = volume.astype(BF16)


def planes(pieces, tables, visc, adv, me):
    modes = len(pieces)
    rows, width = pieces[0].shape
    total = visc.shape[0]
    advected = adv is not None
    fields = 2 if advected else 1
    operands = [me, *pieces, *tables[:4], visc, *tables[4:]]
    if advected:
        operands.append(adv)
    scratch = [pltpu.VMEM((total, width), BF16)] * (4 if advected else 3)
    flops = 2 * total * total * width * (2 + 2 + (1 if advected else 0))
    flops += 2 * total * width * width * 9
    return pl.pallas_call(
        functools.partial(planes_kernel, modes, advected),
        out_shape=[jax.ShapeDtypeStruct((fields, rows, width), BF16)] * modes,
        in_specs=[SMEM] + [VMEM] * (len(operands) - 1),
        out_specs=[VMEM] * modes,
        scratch_shapes=scratch,
        compiler_params=pltpu.CompilerParams(vmem_limit_bytes=VMEM_LIMIT),
        cost_estimate=pl.CostEstimate(
            flops=flops, bytes_accessed=12 * total * total, transcendentals=0
        ),
        name="planes_moved" if advected else "planes_plain",
    )(*operands)


def slot_line(side, block_elements):
    element = lax.shift_right_logical(side, 2)
    code = jnp.bitwise_and(side, 3)
    first = jnp.where(code == 0, 0, jnp.where(code == 1, 7, jnp.where(code == 2, 63, 56)))
    step = jnp.where(code == 0, 1, jnp.where(code == 1, 8, jnp.where(code == 2, -1, -8)))
    block = lax.shift_right_logical(element, shift_of(block_elements))
    inner = jnp.bitwise_and(element, block_elements - 1)
    base = block * (NQ * NQ * block_elements) + first * block_elements + inner
    return base, step * block_elements


def across(values):
    return jnp.sum(values.astype(F32), axis=1, keepdims=True)


def down(values):
    return jnp.sum(values.astype(F32), axis=0, keepdims=True)


def degree_column(side_col, degrees):
    slots = side_col.shape[0]
    elements = degrees.shape[1]
    lanes = lax.broadcasted_iota(jnp.int32, (slots, elements), 1)
    mine = lanes == lax.shift_right_logical(side_col, 2)
    along_x = jnp.bitwise_and(side_col, 1) == 0
    value = jnp.where(along_x, degrees[0:1, :], degrees[1:2, :])
    return across(jnp.where(mine, value, 0))


def traces_kernel(parts, block_elements, me_ref, u_ref, d_ref, row_ref, col_ref, deg_ref, *outs):
    me = me_ref[0]
    rows, columns = u_ref.shape
    side_col = col_ref[:, 0:1]
    peer_col = col_ref[:, 2:3]
    peer_row = row_ref[2:3, :]
    slots = side_col.shape[0]
    base, step = slot_line(side_col, block_elements)
    degree = degree_column(side_col, deg_ref[...])
    before = lax.broadcasted_iota(jnp.int32, (slots, slots), 1) < lax.broadcasted_iota(
        jnp.int32, (slots, slots), 0
    )
    lane = lax.broadcasted_iota(jnp.int32, (slots, MSG), 1)
    place = lax.shift_right_logical(lane, 3)
    line = base + step * jnp.bitwise_and(lane, 7) + 1
    chunk = min(512, columns)
    for out, offset in zip(outs, OFFSETS):
        peer = lax.rem(me + offset + parts, parts)
        rank = across(jnp.where((peer_row == peer) & before, 1, 0)).astype(jnp.int32)
        chosen = (peer_col == peer) & (rank == place)
        target = down(jnp.where(chosen, line, 0)).astype(jnp.int32) - 1
        total_u = jnp.zeros((rows, MSG), F32)
        total_d = jnp.zeros((rows, MSG), F32)
        for start in range(0, columns, chunk):
            here = lax.broadcasted_iota(jnp.int32, (chunk, MSG), 0) + start
            pick = jnp.where(here == target, 1.0, 0.0).astype(BF16)
            total_u += dot(u_ref[:, start : start + chunk], pick)
            total_d += dot(d_ref[:, start : start + chunk], pick)
        out[0:rows, :] = total_u.astype(BF16)
        out[rows : 2 * rows, :] = total_d.astype(BF16)
        degrees = down(jnp.where(chosen, degree, 0.0))
        out[2 * rows :, :] = jnp.broadcast_to(degrees, (16, MSG)).astype(BF16)


def penalty_kernel(
    parts,
    block_elements,
    me_ref,
    u_ref,
    d_ref,
    row_ref,
    col_ref,
    deg_ref,
    degt_ref,
    weight_ref,
    mass_ref,
    near0,
    near1,
    near2,
    near3,
    out_u,
    out_d,
    others,
):
    near = (near0, near1, near2, near3)
    me = me_ref[0]
    rows, columns = u_ref.shape
    side_col, flag_col, peer_col, slot_col = (col_ref[:, i : i + 1] for i in range(4))
    side_row, peer_row, slot_row = row_ref[0:1, :], row_ref[2:3, :], row_ref[3:4, :]
    slots = side_col.shape[0]
    nodes = slots * NQ
    base_col, step_col = slot_line(side_col, block_elements)
    base_row, step_row = slot_line(side_row, block_elements)
    degree_col = degree_column(side_col, deg_ref[...])
    elements = degt_ref.shape[0]
    level = lax.broadcasted_iota(jnp.int32, (elements, slots), 0)
    mine = level == lax.shift_right_logical(side_row, 2)
    value = jnp.where(jnp.bitwise_and(side_row, 1) == 0, degt_ref[:, 0:1], degt_ref[:, 1:2])
    degree_row = down(jnp.where(mine, value, 0))

    lane_slot = lax.broadcasted_iota(jnp.int32, (slots, slots), 1)
    partner = lane_slot == slot_col
    partner_base = across(jnp.where(partner, base_row, 0)).astype(jnp.int32)
    partner_step = across(jnp.where(partner, step_row, 0)).astype(jnp.int32)
    inner_degree = across(jnp.where(partner, degree_row, 0.0))
    rank = across(jnp.where((peer_row == peer_col) & (slot_row < slot_col), 1, 0)).astype(
        jnp.int32
    )
    source = partner_base
    source_step = partner_step
    other_degree = inner_degree
    lane_msg = lax.broadcasted_iota(jnp.int32, (slots, MSG), 1)
    at_rank = lane_msg == rank * NQ
    for index, offset in enumerate(OFFSETS):
        from_here = peer_col == lax.rem(me + offset + parts, parts)
        far_degree = near[index][2 * rows : 2 * rows + 16, :].astype(F32)[0:1, :]
        source = jnp.where(from_here, columns + index * MSG + rank * NQ, source)
        source_step = jnp.where(from_here, 1, source_step)
        other_degree = jnp.where(
            from_here, across(jnp.where(at_rank, far_degree, 0.0)), other_degree
        )
    live = peer_col >= 0
    turned = flag_col == 1
    source = jnp.where(turned, source + 7 * source_step, source)
    source_step = jnp.where(turned, -source_step, source_step)
    source = jnp.where(live, source, -1)
    source_step = jnp.where(live, source_step, 0)
    joint = jnp.maximum(degree_col, other_degree) + 1.0
    strength = jnp.where(live, PENALTY * joint * joint, 0.0)

    lane = lax.broadcasted_iota(jnp.int32, (slots, nodes), 1)
    owner = lax.shift_right_logical(lane, 3) == lax.broadcasted_iota(jnp.int32, (slots, nodes), 0)
    node = jnp.bitwise_and(lane, 7)
    own_line = down(jnp.where(owner, base_col + step_col * node, 0)).astype(jnp.int32)
    far_line = down(jnp.where(owner, source + source_step * node, 0)).astype(jnp.int32)
    factor = down(jnp.where(owner, strength, 0.0)) * weight_ref[...]
    factor_high = factor.astype(BF16).astype(F32)
    factor_low = factor - factor_high

    chunk = min(512, columns)
    total_u = jnp.zeros((rows, nodes), F32)
    total_d = jnp.zeros((rows, nodes), F32)
    for start in range(0, columns, chunk):
        here = lax.broadcasted_iota(jnp.int32, (chunk, nodes), 0) + start
        pick = jnp.where(here == far_line, 1.0, 0.0).astype(BF16)
        total_u += dot(u_ref[:, start : start + chunk], pick)
        total_d += dot(d_ref[:, start : start + chunk], pick)
    for index in range(len(OFFSETS)):
        here = lax.broadcasted_iota(jnp.int32, (MSG, nodes), 0) + (columns + index * MSG)
        pick = jnp.where(here == far_line, 1.0, 0.0).astype(BF16)
        total_u += dot(near[index][0:rows, :], pick)
        total_d += dot(near[index][rows : 2 * rows, :], pick)
    others[0:rows, :] = total_u.astype(BF16)
    others[rows : 2 * rows, :] = total_d.astype(BF16)
    others[2 * rows :, :] = jnp.ones((16, nodes), BF16)

    for start in range(0, columns, chunk):
        here = lax.broadcasted_iota(jnp.int32, (chunk, nodes), 0) + start
        match = here == own_line
        spread_high = jnp.where(match, factor_high, 0.0).astype(BF16)
        spread_low = jnp.where(match, factor_low, 0.0).astype(BF16)
        pulled = lax.dot_general(
            others[...], spread_high, NT, preferred_element_type=F32
        ) + lax.dot_general(others[...], spread_low, NT, preferred_element_type=F32)
        at = slice(start, start + chunk)
        scale = HELM_LAMBDA * mass_ref[:, at] + pulled[2 * rows : 2 * rows + 1, :]
        out_u[:, at] = scale * u_ref[:, at].astype(F32) - pulled[0:rows, :]
        out_d[:, at] = scale * d_ref[:, at].astype(F32) - pulled[rows : 2 * rows, :]


def finish_kernel(modes, plane, me_ref, *refs):
    pieces = refs[:modes]
    local = refs[modes] if len(refs) == modes + 2 else None
    out = refs[-1]
    me = me_ref[0]
    width = pieces[0].shape[2]
    for d in range(modes):
        block = lax.rem(me - d + modes, modes)
        at = pl.ds(pl.multiple_of(block * width, width), width)
        value = pieces[d][plane].astype(F32)
        if local is not None:
            value = value + local[:, at]
        out[:, at] = value


def finish(pieces, plane, local, me):
    modes = len(pieces)
    rows, width = pieces[0].shape[1:]
    operands = [me, *pieces] + ([] if local is None else [local])
    return pl.pallas_call(
        functools.partial(finish_kernel, modes, plane),
        out_shape=jax.ShapeDtypeStruct((rows, modes * width), F32),
        in_specs=[SMEM] + [VMEM] * (len(operands) - 1),
        out_specs=VMEM,
        compiler_params=pltpu.CompilerParams(vmem_limit_bytes=VMEM_LIMIT),
        name="finish",
    )(*operands)


def pass_kernel(*refs):
    del refs


def after(values, others):
    anywhere = pl.BlockSpec(memory_space=pl.ANY)
    return pl.pallas_call(
        pass_kernel,
        out_shape=[jax.ShapeDtypeStruct(v.shape, v.dtype) for v in values],
        in_specs=[anywhere] * (len(values) + len(others)),
        out_specs=[anywhere] * len(values),
        input_output_aliases={i: i for i in range(len(values))},
        name="after",
    )(*values, *others)


def shift_by(block, axis, distance):
    count = lax.axis_size(axis)
    return lax.ppermute(block, axis, [(i, (i + distance) % count) for i in range(count)])


def on_device(u_spec, dir_spec, advecting, viscosity, degrees, edge_side, edge_link):
    modes = lax.axis_size("mode")
    parts = lax.axis_size("elem")
    total, width = viscosity.shape
    rows, columns = u_spec.shape
    block_elements = degrees.shape[1] // modes
    slots = edge_side.shape[0]
    my_mode = lax.axis_index("mode")
    mode_id = my_mode.astype(jnp.int32).reshape(1)
    part_id = lax.axis_index("elem").astype(jnp.int32).reshape(1)

    derivative, weights = cheb_tables()
    identity = np.eye(block_elements)
    kron_x = np.kron(METRIC * derivative, np.eye(NQ * block_elements))
    group = width
    if width % 256 == 0 and 256 % (NQ * block_elements) == 0:
        group = 256
    kron_y = np.kron(np.eye(group // (NQ * block_elements)), np.kron(METRIC * derivative, identity))
    mass = np.repeat(AREA_SCALE * np.outer(weights, weights).reshape(-1), block_elements)
    synthesis, sloped = synthesis_tables(total)
    tables = [
        jnp.asarray(t)
        for t in (
            synthesis,
            sloped,
            np.ascontiguousarray(synthesis.T),
            np.ascontiguousarray(sloped.T),
            mass.astype(np.float32)[None, :],
            split_pair(kron_x.T),
            split_pair(kron_y.T),
            split_pair(kron_x),
            split_pair(kron_y),
        )
    ]

    def cut(field):
        return [
            lax.dynamic_slice_in_dim(field, lax.rem(my_mode + d, modes) * width, width, axis=1)
            for d in range(modes)
        ]

    u_cut = cut(u_spec)
    u_pieces = [u_cut[0]] + [shift_by(u_cut[d], "mode", d) for d in range(1, modes)]
    d_cut = cut(dir_spec)
    d_send = after(d_cut[1:], u_pieces[1:])
    d_pieces = [d_cut[0]] + [shift_by(d_send[d - 1], "mode", d) for d in range(1, modes)]

    table_row = jnp.concatenate([edge_side[None, :], edge_link], axis=0)
    table_col = table_row.T
    near = pl.pallas_call(
        functools.partial(traces_kernel, parts, block_elements),
        out_shape=[jax.ShapeDtypeStruct((2 * rows + 16, MSG), BF16)] * len(OFFSETS),
        in_specs=[SMEM] + [VMEM] * 5,
        out_specs=[VMEM] * len(OFFSETS),
        compiler_params=pltpu.CompilerParams(vmem_limit_bytes=VMEM_LIMIT),
        name="traces",
    )(part_id, u_spec, dir_spec, table_row, table_col, degrees)
    by_offset = {o: shift_by(block, "elem", o) for o, block in zip(OFFSETS, near)}
    near = [by_offset[-o] for o in OFFSETS]

    u_back = planes(u_pieces, tables, viscosity, advecting, mode_id)
    d_back = planes(d_pieces, tables, viscosity, None, mode_id)

    edge_weight = np.tile(LENGTH * weights, slots).astype(np.float32)[None, :]
    mass_local = np.tile(mass, modes).astype(np.float32)[None, :]
    local_u, local_d = pl.pallas_call(
        functools.partial(penalty_kernel, parts, block_elements),
        out_shape=[jax.ShapeDtypeStruct((rows, columns), F32)] * 2,
        in_specs=[SMEM] + [VMEM] * 12,
        out_specs=[VMEM] * 2,
        scratch_shapes=[pltpu.VMEM((2 * rows + 16, slots * NQ), BF16)],
        compiler_params=pltpu.CompilerParams(vmem_limit_bytes=VMEM_LIMIT),
        cost_estimate=pl.CostEstimate(
            flops=2 * 2 * rows * slots * NQ * 3 * columns,
            bytes_accessed=20 * rows * columns,
            transcendentals=0,
        ),
        name="penalty",
    )(
        part_id,
        u_spec,
        dir_spec,
        table_row,
        table_col,
        degrees,
        degrees.T,
        jnp.asarray(edge_weight),
        jnp.asarray(mass_local),
        *near,
    )

    def returned(back):
        return [back[0]] + [shift_by(back[d], "mode", d) for d in range(1, modes)]

    u_returned = returned(u_back)
    d_returned = returned(d_back)
    advect = finish(u_returned, 0, None, mode_id)
    helm_velocity = finish(u_returned, 1, local_u, mode_id)
    helm_direction = finish(d_returned, 0, local_d, mode_id)
    return (advect, helm_velocity, helm_direction)


def solution(mesh):
    in_specs = (
        P("mode", "elem"),
        P("mode", "elem"),
        P(None, None, ("elem", "mode")),
        P(None, ("elem", "mode")),
        P(None, "elem"),
        P("elem"),
        P(None, "elem"),
    )
    out_specs = (P("mode", "elem"), P("mode", "elem"), P("mode", "elem"))
    return jax.shard_map(
        on_device, mesh=mesh, in_specs=in_specs, out_specs=out_specs, check_vma=False
    )
```

time: 359 us -> 136 us (0.38)
  the two profiles are of different devices: /device:TPU:0 before, /device:TPU:10 now
where the time goes in v1:
time: 136 us; the launch traced here: 135 us
  Pallas kernels  63.6 us (47%)
  waiting for transfers between devices  44.7 us (33%)
  starting transfers between devices  18.7 us (14%)
  local copies, waits for them, and re-layouts  7.48 us (6%)
    ppermute x16, waiting for transfers between devices, shift_by(): lax.ppermute(block, axis, [(i, (i + distance) % count) for i in range(cou...  44.7 us
    pallas_call x2, Pallas kernels, planes(): pl.pallas_call(functools.partial(planes_kernel, modes, advected), out_sha...  35.2 us
    ppermute x16, starting transfers between devices, shift_by(): lax.ppermute(block, axis, [(i, (i + distance) % count) for i in range(cou...  18.7 us
    pallas_call x1, Pallas kernels, on_device(): pl.pallas_call(functools.partial(penalty_kernel, parts, block_elements),...  13.4 us
    pallas_call x3, Pallas kernels, finish(): pl.pallas_call(functools.partial(finish_kernel, modes, plane), out_shape=...  10.1 us
    pallas_call x1, Pallas kernels, on_device(): pl.pallas_call(functools.partial(traces_kernel, parts, block_elements), o...  4.9 us
    unnamed x51, local copies, waits for them, and re-layouts  3.65 us
    dynamic_slice x2, local copies, waits for them, and re-layouts, cut(): lax.dynamic_slice_in_dim(field, lax.rem(my_mode + d, modes) * width, widt...  3.1 us
  transfers between devices with their start and end apart: 16, of which 8 were waited for; matrix products, arithmetic and copies ran while one was open for 2% of the time, Pallas kernels for 44%

profile of v1, /device:TPU:10, one launch (start us, length us, event | category | flops | bytes accessed | tf_op | source)
XLA Modules:
  0.0 135.4 jit_solution(15750626959191071033)
XLA Ops:
  0.7 2.1 %constant_dynamic-slice_fusion.4 = (bf16[256,512]{1,0:T(8,128)(2,1)S(1)}, bf16[256,512]{1,0:T(8,128)(2,1)S(1)}, bf16[256,512]{1,0:T(8,128)(2,1)S(1)}, bf16[256,512]{1,0:T(8,128)(2,1)}) fusion(bf16[256,2048]{1,0:T(8,128)(2,1)} %u_ref.3, s32[]{:T(128)S(6)} %select_n.19, s32[]{:T(128)S(6)} %select_n.18, s32[]{:T(128)S(6)} %select_n.17, s32[]{:T(128)S(6)} %select_n.16), kind=kLoop, calls=%fused_computation.5 | loop fusion | bytes 2097168 | tf_op jit(solution)/shard_map/dynamic_slice | solution.py:436
  2.8 1.6 %collective-permute-start = (bf16[256,512]{1,0:T(8,128)(2,1)S(1)}, bf16[256,512]{1,0:T(8,128)(2,1)S(1)}, u32[]{:S(2)}, u32[]{:S(2)}) collective-permute-start(bf16[256,512]{1,0:T(8,128)(2,1)S(1)} %get-tuple-element.43), channel_id=1, source_target_pairs={{0,1},{1,2},{2,3},{3,0},{4,5},{5,6},{6,7},{7,4},{8,9},{9,10},{10,1... | collective-permute-start | bytes 786440 | tf_op jit(solution)/shard_map/ppermute | solution.py:396
  4.4 1.2 collective-permute-start.1
  5.6 1.8 %collective-permute-start.2 = (bf16[256,512]{1,0:T(8,128)(2,1)S(1)}, bf16[256,512]{1,0:T(8,128)(2,1)S(1)}, u32[]{:S(2)}, u32[]{:S(2)}) collective-permute-start(bf16[256,512]{1,0:T(8,128)(2,1)S(1)} %get-tuple-element.41), channel_id=1, source_target_pairs={{0,3},{1,0},{2,1},{3,2},{4,7},{5,4},{6,5},{7,6},{8,11},{9,8},{10,9... | collective-permute-start | bytes 786440 | tf_op jit(solution)/shard_map/ppermute | solution.py:396
  7.4 0.7 copy.29
  8.2 4.9 %traces.1 = (bf16[528,256]{1,0:T(8,128)(2,1)}, bf16[528,256]{1,0:T(8,128)(2,1)}, bf16[528,256]{1,0:T(8,128)(2,1)}, bf16[528,256]{1,0:T(8,128)(2,1)}) custom-call(s32[1]{0:T(128)} %bitcast.1.me_ref, bf16[256,2048]{1,0:T(8,128)(2,1)} %u_ref.3, bf16[256,2048]{1,0:T(8,128)(2,1)} %d_ref.3, s32[4,128]{1,0:T(4,128)} %copy-done.10, s32[128,4]{1,0:T(8,128)} %bitcast.5, ...), custom_call_target="tpu_custom_call" | custom-call | tf_op jit(solution)/shard_map/traces/pallas_call | solution.py:448
  13.1 1.6 %collective-permute-start.7 = (bf16[528,256]{1,0:T(8,128)(2,1)}, bf16[528,256]{1,0:T(8,128)(2,1)S(1)}, u32[]{:S(2)}, u32[]{:S(2)}) collective-permute-start(bf16[528,256]{1,0:T(8,128)(2,1)} %get-tuple-element.25), channel_id=1, source_target_pairs={{0,24},{4,28},{8,0},{12,4},{16,8},{20,12},{24,16},{28,20},{1,25},{... | collective-permute-start | bytes 811016 | tf_op jit(solution)/shard_map/ppermute | solution.py:396
  15.3 1.0 constant_dynamic-slice_fusion
  16.4 6.0 %collective-permute-done.refs_1_.refs_3_ = bf16[256,512]{1,0:T(8,128)(2,1)S(1)} collective-permute-done((bf16[256,512]{1,0:T(8,128)(2,1)S(1)}, bf16[256,512]{1,0:T(8,128)(2,1)S(1)}, u32[]{:S(2)}, u32[]{:S(2)}) %collective-permute-start) | collective-permute-done | bytes 262176 | tf_op jit(solution)/shard_map/ppermute | solution.py:396
  22.3 4.5 %collective-permute-done.1.refs_2_.refs_4_ = bf16[256,512]{1,0:T(8,128)(2,1)S(1)} collective-permute-done((bf16[256,512]{1,0:T(8,128)(2,1)S(1)}, bf16[256,512]{1,0:T(8,128)(2,1)S(1)}, u32[]{:S(2)}, u32[]{:S(2)}) %collective-permute-start.1) | collective-permute-done | bytes 262176 | tf_op jit(solution)/shard_map/ppermute | solution.py:396
  26.8 1.8 %collective-permute-done.2.refs_3_.refs_5_ = bf16[256,512]{1,0:T(8,128)(2,1)S(1)} collective-permute-done((bf16[256,512]{1,0:T(8,128)(2,1)S(1)}, bf16[256,512]{1,0:T(8,128)(2,1)S(1)}, u32[]{:S(2)}, u32[]{:S(2)}) %collective-permute-start.2) | collective-permute-done | bytes 262176 | tf_op jit(solution)/shard_map/ppermute | solution.py:396
  28.6 0.7 copy-done.6
  29.3 1.7 %collective-permute-start.11 = (bf16[256,512]{1,0:T(8,128)(2,1)}, bf16[256,512]{1,0:T(8,128)(2,1)S(1)}, u32[]{:S(2)}, u32[]{:S(2)}) collective-permute-start(bf16[256,512]{1,0:T(8,128)(2,1)} %get-tuple-element.30), channel_id=1, source_target_pairs={{0,2},{1,3},{2,0},{3,1},{4,6},{5,7},{6,4},{7,5},{8,10},{9,11},{10,... | collective-permute-start | bytes 786440 | tf_op jit(solution)/shard_map/ppermute | solution.py:396
  31.0 2.0 %collective-permute-start.12 = (bf16[256,512]{1,0:T(8,128)(2,1)}, bf16[256,512]{1,0:T(8,128)(2,1)S(1)}, u32[]{:S(2)}, u32[]{:S(2)}) collective-permute-start(bf16[256,512]{1,0:T(8,128)(2,1)} %get-tuple-element.31), channel_id=1, source_target_pairs={{0,3},{1,0},{2,1},{3,2},{4,7},{5,4},{6,5},{7,6},{8,11},{9,8},{10,9... | collective-permute-start | bytes 786440 | tf_op jit(solution)/shard_map/ppermute | solution.py:396
  33.0 18.8 %planes_moved.1 = (bf16[2,256,512]{2,1,0:T(8,128)(2,1)}, bf16[2,256,512]{2,1,0:T(8,128)(2,1)}, bf16[2,256,512]{2,1,0:T(8,128)(2,1)}, bf16[2,256,512]{2,1,0:T(8,128)(2,1)}) custom-call(s32[1]{0:T(128)} %bitcast.me_ref, bf16[256,512]{1,0:T(8,128)(2,1)} %get-tuple-element.44.refs_0_, bf16[256,512]{1,0:T(8,128)(2,1)} %copy-done.4, bf16[256,512]{1,0:T(8,128)(2,1)} %copy-done.5, ...), custom_call_target="tpu_custom_call" | custom-call | flops 10200547328 | bytes 12582912 | tf_op jit(solution)/shard_map/planes_moved/pallas_call | solution.py:166
  52.5 1.5 %collective-permute-start.9 = (bf16[528,256]{1,0:T(8,128)(2,1)S(1)}, bf16[528,256]{1,0:T(8,128)(2,1)S(1)}, u32[]{:S(2)}, u32[]{:S(2)}) collective-permute-start(bf16[528,256]{1,0:T(8,128)(2,1)S(1)} %copy-done.18), channel_id=1, source_target_pairs={{0,8},{4,12},{8,16},{12,20},{16,24},{20,28},{24,0},{28,4},{1,9},{5... | collective-permute-start | bytes 811016 | tf_op jit(solution)/shard_map/ppermute | solution.py:396
  54.0 0.7 copy-done.24
  54.7 16.3 %planes_plain.1 = (bf16[1,256,512]{2,1,0:T(8,128)(2,1)}, bf16[1,256,512]{2,1,0:T(8,128)(2,1)}, bf16[1,256,512]{2,1,0:T(8,128)(2,1)}, bf16[1,256,512]{2,1,0:T(8,128)(2,1)}) custom-call(s32[1]{0:T(128)} %bitcast.me_ref, bf16[256,512]{1,0:T(8,128)(2,1)} %get-tuple-element.39.refs_0_, bf16[256,512]{1,0:T(8,128)(2,1)} %copy-done.22, bf16[256,512]{1,0:T(8,128)(2,1)} %copy-done.23, ...), custom_call_target="tpu_custom_call" | custom-call | flops 9126805504 | bytes 12582912 | tf_op jit(solution)/shard_map/planes_plain/pallas_call | solution.py:166
  71.0 3.3 %collective-permute-start.4 = (bf16[2,256,512]{2,1,0:T(8,128)(2,1)S(1)}, bf16[2,256,512]{2,1,0:T(8,128)(2,1)S(1)}, u32[]{:S(2)}, u32[]{:S(2)}) collective-permute-start(bf16[2,256,512]{2,1,0:T(8,128)(2,1)S(1)} %copy-done.15), channel_id=1, source_target_pairs={{0,2},{1,3},{2,0},{3,1},{4,6},{5,7},{6,4},{7,5},{8,10},{9,11},{10,... | collective-permute-start | bytes 1572872 | tf_op jit(solution)/shard_map/ppermute | solution.py:396
  74.4 1.4 %collective-permute-start.5 = (bf16[2,256,512]{2,1,0:T(8,128)(2,1)S(1)}, bf16[2,256,512]{2,1,0:T(8,128)(2,1)S(1)}, u32[]{:S(2)}, u32[]{:S(2)}) collective-permute-start(bf16[2,256,512]{2,1,0:T(8,128)(2,1)S(1)} %copy-done.14), channel_id=1, source_target_pairs={{0,3},{1,0},{2,1},{3,2},{4,7},{5,4},{6,5},{7,6},{8,11},{9,8},{10,9... | collective-permute-start | bytes 1572872 | tf_op jit(solution)/shard_map/ppermute | solution.py:396
  75.8 0.7 collective-permute-start.13
  76.5 1.8 %collective-permute-start.14 = (bf16[1,256,512]{2,1,0:T(8,128)(2,1)}, bf16[1,256,512]{2,1,0:T(8,128)(2,1)S(1)}, u32[]{:S(2)}, u32[]{:S(2)}) collective-permute-start(bf16[1,256,512]{2,1,0:T(8,128)(2,1)} %get-tuple-element.34), channel_id=1, source_target_pairs={{0,2},{1,3},{2,0},{3,1},{4,6},{5,7},{6,4},{7,5},{8,10},{9,11},{10,... | collective-permute-start | bytes 786440 | tf_op jit(solution)/shard_map/ppermute | solution.py:396
  78.4 13.4 %penalty.1 = (f32[256,2048]{1,0:T(8,128)}, f32[256,2048]{1,0:T(8,128)}) custom-call(s32[1]{0:T(128)} %bitcast.1.me_ref, bf16[256,2048]{1,0:T(8,128)(2,1)} %u_ref.3, bf16[256,2048]{1,0:T(8,128)(2,1)} %d_ref.3, s32[4,128]{1,0:T(4,128)} %copy-done.10, s32[128,4]{1,0:T(8,128)} %bitcast.6, s32[2,32]{1,0:T(2,128)} %deg_ref.3, s32[32,2]{1,0:T(8,128)} %bitcast.7, ...), custom_call_target="tpu_custom_call" | custom-call | flops 6442450944 | bytes 10485760 | tf_op jit(solution)/shard_map/penalty/pallas_call | solution.py:464
  91.8 27.5 %collective-permute-done.4.refs_2_ = bf16[2,256,512]{2,1,0:T(8,128)(2,1)S(1)} collective-permute-done((bf16[2,256,512]{2,1,0:T(8,128)(2,1)S(1)}, bf16[2,256,512]{2,1,0:T(8,128)(2,1)S(1)}, u32[]{:S(2)}, u32[]{:S(2)}) %collective-permute-start.4) | collective-permute-done | bytes 524320 | tf_op jit(solution)/shard_map/ppermute | solution.py:396
  119.2 1.2 collective-permute-done.5.refs_3_
  120.5 0.8 copy-done.3
  121.3 3.0 %finish.3 = f32[256,2048]{1,0:T(8,128)} custom-call(s32[1]{0:T(128)} %bitcast.me_ref, bf16[2,256,512]{2,1,0:T(8,128)(2,1)} %get-tuple-element.20.refs_0_, bf16[2,256,512]{2,1,0:T(8,128)(2,1)} %copy-done.1, bf16[2,256,512]{2,1,0:T(8,128)(2,1)} %copy-done.2, bf16[2,256,512]{2,1,0:T(8,128)(2,1)} %copy-done.3), custom_call_target="tpu_custom_call" | custom-call | tf_op jit(solution)/shard_map/finish/pallas_call | solution.py:368
  124.2 3.7 %finish.4 = f32[256,2048]{1,0:T(8,128)} custom-call(s32[1]{0:T(128)} %bitcast.me_ref, bf16[2,256,512]{2,1,0:T(8,128)(2,1)} %get-tuple-element.20.refs_0_, bf16[2,256,512]{2,1,0:T(8,128)(2,1)} %copy-done.1, bf16[2,256,512]{2,1,0:T(8,128)(2,1)} %copy-done.2, bf16[2,256,512]{2,1,0:T(8,128)(2,1)} %copy-done.3, f32[256,2048]{1,0:T(8,128)} %get-tuple-element.28.refs_4_), custom_call_target="tpu_custom_call" | custom-call | tf_op jit(solution)/shard_map/finish/pallas_call | solution.py:368
  128.0 2.4 %collective-permute-done.14.refs_2_ = bf16[1,256,512]{2,1,0:T(8,128)(2,1)S(1)} collective-permute-done((bf16[1,256,512]{2,1,0:T(8,128)(2,1)}, bf16[1,256,512]{2,1,0:T(8,128)(2,1)S(1)}, u32[]{:S(2)}, u32[]{:S(2)}) %collective-permute-start.14) | collective-permute-done | bytes 262176 | tf_op jit(solution)/shard_map/ppermute | solution.py:396
  130.4 0.8 collective-permute-done.15.refs_3_
  131.2 0.7 copy-done.9
  131.9 3.4 %finish.5 = f32[256,2048]{1,0:T(8,128)} custom-call(s32[1]{0:T(128)} %bitcast.me_ref, bf16[1,256,512]{2,1,0:T(8,128)(2,1)} %get-tuple-element.32.refs_0_, bf16[1,256,512]{2,1,0:T(8,128)(2,1)} %copy-done.7, bf16[1,256,512]{2,1,0:T(8,128)(2,1)} %copy-done.8, bf16[1,256,512]{2,1,0:T(8,128)(2,1)} %copy-done.9, f32[256,2048]{1,0:T(8,128)} %get-tuple-element.36.refs_4_), custom_call_target="tpu_custom_call" | custom-call | tf_op jit(solution)/shard_map/finish/pallas_call | solution.py:368
  (63 shorter events, 1.4 us)
Async XLA Ops:
  0.6 6.8 %copy-start.13 = (s32[128]{0:T(128)S(1)}, s32[128]{0:T(128)}, u32[]{:S(2)}) copy-start(s32[128]{0:T(128)} %param.23) | copy-start | bytes 1540
  0.6 6.8 %copy-start.12 = (s32[3,128]{1,0:T(4,128)S(1)}, s32[3,128]{1,0:T(4,128)}, u32[]{:S(2)}) copy-start(s32[3,128]{1,0:T(4,128)} %param.24) | copy-start | bytes 4612
  0.7 14.0 %copy-start.11 = (s32[2,32]{1,0:T(2,128)S(1)}, s32[2,32]{1,0:T(2,128)}, u32[]{:S(2)}) copy-start(s32[2,32]{1,0:T(2,128)} %deg_ref.3) | copy-start | bytes 772
  0.7 14.6 %copy-start = (bf16[256,2048]{1,0:T(8,128)(2,1)S(1)}, bf16[256,2048]{1,0:T(8,128)(2,1)}, u32[]{:S(2)}) copy-start(bf16[256,2048]{1,0:T(8,128)(2,1)} %d_ref.3) | copy-start | bytes 3145732
  2.8 19.5 %collective-permute-start = (bf16[256,512]{1,0:T(8,128)(2,1)S(1)}, bf16[256,512]{1,0:T(8,128)(2,1)S(1)}, u32[]{:S(2)}, u32[]{:S(2)}) collective-permute-start(bf16[256,512]{1,0:T(8,128)(2,1)S(1)} %get-tuple-element.43), channel_id=1, source_target_pairs={{0,1},{1,2},{2,3},{3,0},{4,5},{5,6},{6,7},{7,4},{8,9},{9,10},{10,1... | collective-permute-start | bytes 786440 | tf_op jit(solution)/shard_map/ppermute | solution.py:396
  4.4 22.4 %collective-permute-start.1 = (bf16[256,512]{1,0:T(8,128)(2,1)S(1)}, bf16[256,512]{1,0:T(8,128)(2,1)S(1)}, u32[]{:S(2)}, u32[]{:S(2)}) collective-permute-start(bf16[256,512]{1,0:T(8,128)(2,1)S(1)} %get-tuple-element.42), channel_id=1, source_target_pairs={{0,2},{1,3},{2,0},{3,1},{4,6},{5,7},{6,4},{7,5},{8,10},{9,11},{10,... | collective-permute-start | bytes 786440 | tf_op jit(solution)/shard_map/ppermute | solution.py:396
  5.6 23.0 %collective-permute-start.2 = (bf16[256,512]{1,0:T(8,128)(2,1)S(1)}, bf16[256,512]{1,0:T(8,128)(2,1)S(1)}, u32[]{:S(2)}, u32[]{:S(2)}) collective-permute-start(bf16[256,512]{1,0:T(8,128)(2,1)S(1)} %get-tuple-element.41), channel_id=1, source_target_pairs={{0,3},{1,0},{2,1},{3,2},{4,7},{5,4},{6,5},{7,6},{8,11},{9,8},{10,9... | collective-permute-start | bytes 786440 | tf_op jit(solution)/shard_map/ppermute | solution.py:396
  13.1 58.0 %collective-permute-start.6 = (bf16[528,256]{1,0:T(8,128)(2,1)}, bf16[528,256]{1,0:T(8,128)(2,1)S(1)}, u32[]{:S(2)}, u32[]{:S(2)}) collective-permute-start(bf16[528,256]{1,0:T(8,128)(2,1)} %get-tuple-element.24), channel_id=1, source_target_pairs={{0,28},{4,0},{8,4},{12,8},{16,12},{20,16},{24,20},{28,24},{1,29},{... | collective-permute-start | bytes 811016 | tf_op jit(solution)/shard_map/ppermute | solution.py:396
  13.1 61.3 %collective-permute-start.7 = (bf16[528,256]{1,0:T(8,128)(2,1)}, bf16[528,256]{1,0:T(8,128)(2,1)S(1)}, u32[]{:S(2)}, u32[]{:S(2)}) collective-permute-start(bf16[528,256]{1,0:T(8,128)(2,1)} %get-tuple-element.25), channel_id=1, source_target_pairs={{0,24},{4,28},{8,0},{12,4},{16,8},{20,12},{24,16},{28,20},{1,25},{... | collective-permute-start | bytes 811016 | tf_op jit(solution)/shard_map/ppermute | solution.py:396
  22.3 6.3 %copy-start.4 = (bf16[256,512]{1,0:T(8,128)(2,1)}, bf16[256,512]{1,0:T(8,128)(2,1)S(1)}, u32[]{:S(2)}) copy-start(bf16[256,512]{1,0:T(8,128)(2,1)S(1)} %collective-permute-done.refs_1_.refs_3_) | copy-start | bytes 786436
  29.3 22.6 %collective-permute-start.10 = (bf16[256,512]{1,0:T(8,128)(2,1)}, bf16[256,512]{1,0:T(8,128)(2,1)S(1)}, u32[]{:S(2)}, u32[]{:S(2)}) collective-permute-start(bf16[256,512]{1,0:T(8,128)(2,1)} %get-tuple-element.29), channel_id=1, source_target_pairs={{0,1},{1,2},{2,3},{3,0},{4,5},{5,6},{6,7},{7,4},{8,9},{9,10},{10,1... | collective-permute-start | bytes 786440 | tf_op jit(solution)/shard_map/ppermute | solution.py:396
  29.3 23.2 %collective-permute-start.11 = (bf16[256,512]{1,0:T(8,128)(2,1)}, bf16[256,512]{1,0:T(8,128)(2,1)S(1)}, u32[]{:S(2)}, u32[]{:S(2)}) collective-permute-start(bf16[256,512]{1,0:T(8,128)(2,1)} %get-tuple-element.30), channel_id=1, source_target_pairs={{0,2},{1,3},{2,0},{3,1},{4,6},{5,7},{6,4},{7,5},{8,10},{9,11},{10,... | collective-permute-start | bytes 786440 | tf_op jit(solution)/shard_map/ppermute | solution.py:396
  31.0 23.0 %collective-permute-start.12 = (bf16[256,512]{1,0:T(8,128)(2,1)}, bf16[256,512]{1,0:T(8,128)(2,1)S(1)}, u32[]{:S(2)}, u32[]{:S(2)}) collective-permute-start(bf16[256,512]{1,0:T(8,128)(2,1)} %get-tuple-element.31), channel_id=1, source_target_pairs={{0,3},{1,0},{2,1},{3,2},{4,7},{5,4},{6,5},{7,6},{8,11},{9,8},{10,9... | collective-permute-start | bytes 786440 | tf_op jit(solution)/shard_map/ppermute | solution.py:396
  33.0 18.9 %copy-start.19 = (bf16[528,256]{1,0:T(8,128)(2,1)S(1)}, bf16[528,256]{1,0:T(8,128)(2,1)}, u32[]{:S(2)}) copy-start(bf16[528,256]{1,0:T(8,128)(2,1)} %get-tuple-element.26) | copy-start | bytes 811012
  33.0 19.5 %copy-start.18 = (bf16[528,256]{1,0:T(8,128)(2,1)S(1)}, bf16[528,256]{1,0:T(8,128)(2,1)}, u32[]{:S(2)}) copy-start(bf16[528,256]{1,0:T(8,128)(2,1)} %get-tuple-element.27) | copy-start | bytes 811012
  51.8 2.1 %copy-start.22 = (bf16[256,512]{1,0:T(8,128)(2,1)}, bf16[256,512]{1,0:T(8,128)(2,1)S(1)}, u32[]{:S(2)}) copy-start(bf16[256,512]{1,0:T(8,128)(2,1)S(1)} %collective-permute-done.10.refs_1_) | copy-start | bytes 786436
  51.9 23.9 %collective-permute-start.8 = (bf16[528,256]{1,0:T(8,128)(2,1)S(1)}, bf16[528,256]{1,0:T(8,128)(2,1)S(1)}, u32[]{:S(2)}, u32[]{:S(2)}) collective-permute-start(bf16[528,256]{1,0:T(8,128)(2,1)S(1)} %copy-done.19), channel_id=1, source_target_pairs={{0,4},{4,8},{8,12},{12,16},{16,20},{20,24},{24,28},{28,0},{1,5},{5... | collective-permute-start | bytes 811016 | tf_op jit(solution)/shard_map/ppermute | solution.py:396
  52.5 24.0 %collective-permute-start.9 = (bf16[528,256]{1,0:T(8,128)(2,1)S(1)}, bf16[528,256]{1,0:T(8,128)(2,1)S(1)}, u32[]{:S(2)}, u32[]{:S(2)}) collective-permute-start(bf16[528,256]{1,0:T(8,128)(2,1)S(1)} %copy-done.18), channel_id=1, source_target_pairs={{0,8},{4,12},{8,16},{12,20},{16,24},{20,28},{24,0},{28,4},{1,9},{5... | collective-permute-start | bytes 811016 | tf_op jit(solution)/shard_map/ppermute | solution.py:396
  54.0 24.3 %collective-permute-start.3 = (bf16[2,256,512]{2,1,0:T(8,128)(2,1)}, bf16[2,256,512]{2,1,0:T(8,128)(2,1)S(1)}, u32[]{:S(2)}, u32[]{:S(2)}) collective-permute-start(bf16[2,256,512]{2,1,0:T(8,128)(2,1)} %get-tuple-element.21), channel_id=1, source_target_pairs={{0,1},{1,2},{2,3},{3,0},{4,5},{5,6},{6,7},{7,4},{8,9},{9,10},{10,1... | collective-permute-start | bytes 1572872 | tf_op jit(solution)/shard_map/ppermute | solution.py:396
  54.7 16.3 %copy-start.15 = (bf16[2,256,512]{2,1,0:T(8,128)(2,1)S(1)}, bf16[2,256,512]{2,1,0:T(8,128)(2,1)}, u32[]{:S(2)}) copy-start(bf16[2,256,512]{2,1,0:T(8,128)(2,1)} %get-tuple-element.22) | copy-start | bytes 1572868
  54.7 19.7 %copy-start.14 = (bf16[2,256,512]{2,1,0:T(8,128)(2,1)S(1)}, bf16[2,256,512]{2,1,0:T(8,128)(2,1)}, u32[]{:S(2)}) copy-start(bf16[2,256,512]{2,1,0:T(8,128)(2,1)} %get-tuple-element.23) | copy-start | bytes 1572868
  71.0 7.3 %copy-start.16 = (bf16[528,256]{1,0:T(8,128)(2,1)}, bf16[528,256]{1,0:T(8,128)(2,1)S(1)}, u32[]{:S(2)}) copy-start(bf16[528,256]{1,0:T(8,128)(2,1)S(1)} %collective-permute-done.6.near0) | copy-start | bytes 811012
  71.0 48.2 %collective-permute-start.4 = (bf16[2,256,512]{2,1,0:T(8,128)(2,1)S(1)}, bf16[2,256,512]{2,1,0:T(8,128)(2,1)S(1)}, u32[]{:S(2)}, u32[]{:S(2)}) collective-permute-start(bf16[2,256,512]{2,1,0:T(8,128)(2,1)S(1)} %copy-done.15), channel_id=1, source_target_pairs={{0,2},{1,3},{2,0},{3,1},{4,6},{5,7},{6,4},{7,5},{8,10},{9,11},{10,... | collective-permute-start | bytes 1572872 | tf_op jit(solution)/shard_map/ppermute | solution.py:396
  74.4 4.0 %copy-start.17 = (bf16[528,256]{1,0:T(8,128)(2,1)}, bf16[528,256]{1,0:T(8,128)(2,1)S(1)}, u32[]{:S(2)}) copy-start(bf16[528,256]{1,0:T(8,128)(2,1)S(1)} %collective-permute-done.7.near1) | copy-start | bytes 811012
  74.4 46.1 %collective-permute-start.5 = (bf16[2,256,512]{2,1,0:T(8,128)(2,1)S(1)}, bf16[2,256,512]{2,1,0:T(8,128)(2,1)S(1)}, u32[]{:S(2)}, u32[]{:S(2)}) collective-permute-start(bf16[2,256,512]{2,1,0:T(8,128)(2,1)S(1)} %copy-done.14), channel_id=1, source_target_pairs={{0,3},{1,0},{2,1},{3,2},{4,7},{5,4},{6,5},{7,6},{8,11},{9,8},{10,9... | collective-permute-start | bytes 1572872 | tf_op jit(solution)/shard_map/ppermute | solution.py:396
  75.8 2.6 %copy-start.20 = (bf16[528,256]{1,0:T(8,128)(2,1)}, bf16[528,256]{1,0:T(8,128)(2,1)S(1)}, u32[]{:S(2)}) copy-start(bf16[528,256]{1,0:T(8,128)(2,1)S(1)} %collective-permute-done.8.near2) | copy-start | bytes 811012
  75.8 52.2 %collective-permute-start.13 = (bf16[1,256,512]{2,1,0:T(8,128)(2,1)}, bf16[1,256,512]{2,1,0:T(8,128)(2,1)S(1)}, u32[]{:S(2)}, u32[]{:S(2)}) collective-permute-start(bf16[1,256,512]{2,1,0:T(8,128)(2,1)} %get-tuple-element.33), channel_id=1, source_target_pairs={{0,1},{1,2},{2,3},{3,0},{4,5},{5,6},{6,7},{7,4},{8,9},{9,10},{10,1... | collective-permute-start | bytes 786440 | tf_op jit(solution)/shard_map/ppermute | solution.py:396
  76.5 1.9 %copy-start.21 = (bf16[528,256]{1,0:T(8,128)(2,1)}, bf16[528,256]{1,0:T(8,128)(2,1)S(1)}, u32[]{:S(2)}) copy-start(bf16[528,256]{1,0:T(8,128)(2,1)S(1)} %collective-permute-done.9.near3) | copy-start | bytes 811012
  76.5 53.9 %collective-permute-start.14 = (bf16[1,256,512]{2,1,0:T(8,128)(2,1)}, bf16[1,256,512]{2,1,0:T(8,128)(2,1)S(1)}, u32[]{:S(2)}, u32[]{:S(2)}) collective-permute-start(bf16[1,256,512]{2,1,0:T(8,128)(2,1)} %get-tuple-element.34), channel_id=1, source_target_pairs={{0,2},{1,3},{2,0},{3,1},{4,6},{5,7},{6,4},{7,5},{8,10},{9,11},{10,... | collective-permute-start | bytes 786440 | tf_op jit(solution)/shard_map/ppermute | solution.py:396
  78.3 13.5 %copy-start.1 = (bf16[2,256,512]{2,1,0:T(8,128)(2,1)}, bf16[2,256,512]{2,1,0:T(8,128)(2,1)S(1)}, u32[]{:S(2)}) copy-start(bf16[2,256,512]{2,1,0:T(8,128)(2,1)S(1)} %collective-permute-done.3.refs_1_) | copy-start | bytes 1572868
  78.3 52.9 %collective-permute-start.15 = (bf16[1,256,512]{2,1,0:T(8,128)(2,1)}, bf16[1,256,512]{2,1,0:T(8,128)(2,1)S(1)}, u32[]{:S(2)}, u32[]{:S(2)}) collective-permute-start(bf16[1,256,512]{2,1,0:T(8,128)(2,1)} %get-tuple-element.35), channel_id=1, source_target_pairs={{0,3},{1,0},{2,1},{3,2},{4,7},{5,4},{6,5},{7,6},{8,11},{9,8},{10,9... | collective-permute-start | bytes 786440 | tf_op jit(solution)/shard_map/ppermute | solution.py:396
  128.0 3.3 %copy-start.7 = (bf16[1,256,512]{2,1,0:T(8,128)(2,1)}, bf16[1,256,512]{2,1,0:T(8,128)(2,1)S(1)}, u32[]{:S(2)}) copy-start(bf16[1,256,512]{2,1,0:T(8,128)(2,1)S(1)} %collective-permute-done.13.refs_1_) | copy-start | bytes 786436
  (9 other events, 9.1 us)

commit v2 on v1

--- a/solution.py
+++ b/solution.py
@@ -18,7 +18,8 @@
 PENALTY = 0.02
 OFFSETS = (1, 2, -1, -2)
 MSG = 256
-VMEM_LIMIT = 56 * 1024 * 1024
+MIB = 1024 * 1024
+PLANES_LIMIT = 56
 
 F32 = jnp.float32
 BF16 = jnp.bfloat16
@@ -90,28 +91,67 @@
     return dot(jnp.concatenate([high, low, high], axis=1), table)
 
 
-def planes_kernel(
-    modes, advected, me_ref, *refs
-):
-    pieces = refs[:modes]
-    (s_ref, sz_ref, t_ref, tz_ref, visc_ref, mass_ref, rx_ref, ry_ref, kx_ref, ky_ref) = refs[
-        modes : modes + 10
-    ]
+def planes_kernel(modes, chunk, advected, me_ref, *refs):
+    own_ref, pieces = refs[0], refs[1:modes]
+    s_in, sz_in, t_in, tz_in, *node_in = refs[modes : modes + 8]
+    visc_in, mass_ref = refs[modes + 8 : modes + 10]
     refs = refs[modes + 10 :]
     if advected:
-        adv_ref = refs[0]
-        refs = refs[1:]
+        adv_in, refs = refs[0], refs[1:]
     outs = refs[:modes]
-    spec, flat, flux = refs[modes : modes + 3]
-    moved = refs[modes + 3] if advected else None
+    spec, flat, flux, s_ref, sz_ref, t_ref, tz_ref, visc_ref = refs[modes : modes + 8]
+    rx_ref, ry_ref, kx_ref, ky_ref = node_refs = refs[modes + 8 : modes + 12]
+    held, step_sem, node_sem, own_sem, back_sem, out_sem = refs[modes + 12 : modes + 18]
+    if advected:
+        moved, adv_ref = refs[modes + 18 :]
     me = me_ref[0]
-    rows = pieces[0].shape[0]
+    rows = own_ref.shape[0]
     total, width = visc_ref.shape
     group = ry_ref.shape[1]
-    for d in range(modes):
-        block = lax.rem(me - d + modes, modes)
-        spec[pl.ds(pl.multiple_of(block * rows, rows), rows), :] = pieces[d][...]
-    chunk = min(256, total)
+    steps = total // chunk
+
+    own_copy = pltpu.make_async_copy(
+        own_ref.at[:, pl.ds(pl.multiple_of(me * width, width), width)],
+        spec.at[pl.ds(pl.multiple_of(me * rows, rows), rows), :],
+        own_sem,
+    )
+    node_copies = [
+        pltpu.make_async_copy(source, target, node_sem.at[i])
+        for i, (source, target) in enumerate(zip(node_in, node_refs))
+    ]
+    back_copies = [
+        pltpu.make_async_copy(t_in, t_ref, back_sem.at[0]),
+        pltpu.make_async_copy(tz_in, tz_ref, back_sem.at[1]),
+    ]
+
+    def plane_copies(step):
+        at = pl.ds(pl.multiple_of(step * chunk, chunk), chunk)
+        pairs = [(s_in, s_ref), (sz_in, sz_ref), (visc_in, visc_ref)]
+        copies = [
+            pltpu.make_async_copy(source.at[at, :], target.at[at, :], step_sem.at[step, i])
+            for i, (source, target) in enumerate(pairs)
+        ]
+        if advected:
+            copies.append(
+                pltpu.make_async_copy(
+                    adv_in.at[:, at, :], adv_ref.at[:, at, :], step_sem.at[step, 3]
+                )
+            )
+        return copies
+
+    own_copy.start()
+    first = plane_copies(0)
+    for copy in first[:2] + node_copies[:2] + first[2:] + node_copies[2:]:
+        copy.start()
+    for step in range(1, steps):
+        for copy in plane_copies(step):
+            copy.start()
+    for copy in back_copies:
+        copy.start()
+    for d in range(1, modes):
+        at = pl.ds(pl.multiple_of(jnp.bitwise_xor(me, d) * rows, rows), rows)
+        spec[at, :] = pieces[d - 1][...]
+    own_copy.wait()
 
     def grouped(value, ref):
         parts = [
@@ -121,9 +161,20 @@
 
     def forward(step, carry):
         at = pl.ds(pl.multiple_of(step * chunk, chunk), chunk)
+        copies = plane_copies(step)
+        for copy in copies[:2]:
+            copy.wait()
         coeffs = spec[...]
         plain = dot(s_ref[at, :], coeffs)
         along = dot(sz_ref[at, :], coeffs)
+
+        @pl.when(step == 0)
+        def _():
+            for copy in node_copies:
+                copy.wait()
+
+        for copy in copies[2:]:
+            copy.wait()
         grad_x = dot_split(plain, rx_ref[...])
         grad_y = grouped(plain, ry_ref)
         weighted = mass_ref[...] * visc_ref[at, :].astype(F32)
@@ -138,38 +189,62 @@
         flat[at, :] = flat_sum.astype(BF16)
         return carry
 
-    lax.fori_loop(0, total // chunk, forward, 0)
-
-    for d in range(modes):
-        block = lax.rem(me + d, modes)
-        at = pl.ds(pl.multiple_of(block * rows, rows), rows)
+    lax.fori_loop(0, steps, forward, 0)
+
+    for copy in back_copies:
+        copy.wait()
+    stores = [pltpu.make_async_copy(held.at[d], outs[d], out_sem.at[d]) for d in range(modes)]
+    for d in [*range(1, modes), 0]:
+        at = pl.ds(pl.multiple_of(jnp.bitwise_xor(me, d) * rows, rows), rows)
         volume = dot(t_ref[at, :], flat[...]) + dot(tz_ref[at, :], flux[...])
         if advected:
-            outs[d][0] = dot(t_ref[at, :], moved[...]).astype(BF16)
-            outs[d][1] = volume.astype(BF16)
+            held[d, 0] = dot(t_ref[at, :], moved[...]).astype(BF16)
+            held[d, 1] = volume.astype(BF16)
         else:
-            outs[d][0] = volume.astype(BF16)
-
-
-def planes(pieces, tables, visc, adv, me):
+            held[d, 0] = volume.astype(BF16)
+        stores[d].start()
+    for store in stores:
+        store.wait()
+
+
+def planes(pieces, tables, visc, mass, adv, me):
     modes = len(pieces)
-    rows, width = pieces[0].shape
-    total = visc.shape[0]
+    rows = pieces[0].shape[0]
+    total, width = visc.shape
+    group = tables[5].shape[1]
+    chunk = min(256, total)
     advected = adv is not None
     fields = 2 if advected else 1
-    operands = [me, *pieces, *tables[:4], visc, *tables[4:]]
-    if advected:
-        operands.append(adv)
-    scratch = [pltpu.VMEM((total, width), BF16)] * (4 if advected else 3)
+    operands = [me, *pieces, *tables, visc, mass] + ([adv] if advected else [])
     flops = 2 * total * total * width * (2 + 2 + (1 if advected else 0))
     flops += 2 * total * width * width * 9
+    far = pl.BlockSpec(memory_space=pltpu.HBM)
+    plane = pltpu.VMEM((total, width), BF16)
+    square = pltpu.VMEM((total, total), BF16)
+    node_x = pltpu.VMEM((3 * width, width), BF16)
+    node_y = pltpu.VMEM((3 * group, group), BF16)
+    scratch = [plane] * 3 + [square] * 4 + [plane, node_x, node_y, node_x, node_y]
+    scratch += [
+        pltpu.VMEM((modes, fields, rows, width), BF16),
+        pltpu.SemaphoreType.DMA((total // chunk, 4)),
+        pltpu.SemaphoreType.DMA((4,)),
+        pltpu.SemaphoreType.DMA,
+        pltpu.SemaphoreType.DMA((2,)),
+        pltpu.SemaphoreType.DMA((modes,)),
+    ]
+    if advected:
+        scratch += [plane, pltpu.VMEM(adv.shape, BF16)]
     return pl.pallas_call(
-        functools.partial(planes_kernel, modes, advected),
+        functools.partial(planes_kernel, modes, chunk, advected),
         out_shape=[jax.ShapeDtypeStruct((fields, rows, width), BF16)] * modes,
-        in_specs=[SMEM] + [VMEM] * (len(operands) - 1),
-        out_specs=[VMEM] * modes,
+        in_specs=[SMEM, far]
+        + [VMEM] * (modes - 1)
+        + [far] * (len(tables) + 1)
+        + [VMEM]
+        + [far] * (1 if advected else 0),
+        out_specs=[far] * modes,
         scratch_shapes=scratch,
-        compiler_params=pltpu.CompilerParams(vmem_limit_bytes=VMEM_LIMIT),
+        compiler_params=pltpu.CompilerParams(vmem_limit_bytes=PLANES_LIMIT * MIB),
         cost_estimate=pl.CostEstimate(
             flops=flops, bytes_accessed=12 * total * total, transcendentals=0
         ),
@@ -206,7 +281,15 @@
     return across(jnp.where(mine, value, 0))
 
 
-def traces_kernel(parts, block_elements, me_ref, u_ref, d_ref, row_ref, col_ref, deg_ref, *outs):
+def fetch(source, target, sem):
+    return pltpu.make_async_copy(source, target, sem)
+
+
+def traces_kernel(parts, block_elements, me_ref, u_in, d_in, row_ref, col_ref, deg_ref, *refs):
+    out, u_ref, d_ref, sem = refs
+    copies = [fetch(u_in, u_ref, sem.at[0]), fetch(d_in, d_ref, sem.at[1])]
+    for copy in copies:
+        copy.start()
     me = me_ref[0]
     rows, columns = u_ref.shape
     side_col = col_ref[:, 0:1]
@@ -222,7 +305,9 @@
     place = lax.shift_right_logical(lane, 3)
     line = base + step * jnp.bitwise_and(lane, 7) + 1
     chunk = min(512, columns)
-    for out, offset in zip(outs, OFFSETS):
+    for copy in copies:
+        copy.wait()
+    for offset in OFFSETS:
         peer = lax.rem(me + offset + parts, parts)
         rank = across(jnp.where((peer_row == peer) & before, 1, 0)).astype(jnp.int32)
         chosen = (peer_col == peer) & (rank == place)
@@ -234,34 +319,42 @@
             pick = jnp.where(here == target, 1.0, 0.0).astype(BF16)
             total_u += dot(u_ref[:, start : start + chunk], pick)
             total_d += dot(d_ref[:, start : start + chunk], pick)
-        out[0:rows, :] = total_u.astype(BF16)
-        out[rows : 2 * rows, :] = total_d.astype(BF16)
+        out[peer, 0:rows, :] = total_u.astype(BF16)
+        out[peer, rows : 2 * rows, :] = total_d.astype(BF16)
         degrees = down(jnp.where(chosen, degree, 0.0))
-        out[2 * rows :, :] = jnp.broadcast_to(degrees, (16, MSG)).astype(BF16)
+        out[peer, 2 * rows :, :] = jnp.broadcast_to(degrees, (16, MSG)).astype(BF16)
 
 
 def penalty_kernel(
     parts,
     block_elements,
     me_ref,
-    u_ref,
-    d_ref,
+    u_in,
+    d_in,
     row_ref,
     col_ref,
     deg_ref,
     degt_ref,
     weight_ref,
     mass_ref,
-    near0,
-    near1,
-    near2,
-    near3,
+    near_in,
     out_u,
     out_d,
     others,
+    u_ref,
+    d_ref,
+    sem,
+    near,
+    near_sem,
 ):
-    near = (near0, near1, near2, near3)
     me = me_ref[0]
+    near_copies = [
+        fetch(near_in.at[lax.rem(me + offset + parts, parts)], near.at[i], near_sem.at[i])
+        for i, offset in enumerate(OFFSETS)
+    ]
+    copies = [fetch(u_in, u_ref, sem.at[0]), fetch(d_in, d_ref, sem.at[1])]
+    for copy in near_copies + copies:
+        copy.start()
     rows, columns = u_ref.shape
     side_col, flag_col, peer_col, slot_col = (col_ref[:, i : i + 1] for i in range(4))
     side_row, peer_row, slot_row = row_ref[0:1, :], row_ref[2:3, :], row_ref[3:4, :]
@@ -284,6 +377,8 @@
     rank = across(jnp.where((peer_row == peer_col) & (slot_row < slot_col), 1, 0)).astype(
         jnp.int32
     )
+    for copy in near_copies:
+        copy.wait()
     source = partner_base
     source_step = partner_step
     other_degree = inner_degree
@@ -291,7 +386,7 @@
     at_rank = lane_msg == rank * NQ
     for index, offset in enumerate(OFFSETS):
         from_here = peer_col == lax.rem(me + offset + parts, parts)
-        far_degree = near[index][2 * rows : 2 * rows + 16, :].astype(F32)[0:1, :]
+        far_degree = near[index, 2 * rows : 2 * rows + 16, :].astype(F32)[0:1, :]
         source = jnp.where(from_here, columns + index * MSG + rank * NQ, source)
         source_step = jnp.where(from_here, 1, source_step)
         other_degree = jnp.where(
@@ -316,6 +411,8 @@
     factor_low = factor - factor_high
 
     chunk = min(512, columns)
+    for copy in copies:
+        copy.wait()
     total_u = jnp.zeros((rows, nodes), F32)
     total_d = jnp.zeros((rows, nodes), F32)
     for start in range(0, columns, chunk):
@@ -326,8 +423,8 @@
     for index in range(len(OFFSETS)):
         here = lax.broadcasted_iota(jnp.int32, (MSG, nodes), 0) + (columns + index * MSG)
         pick = jnp.where(here == far_line, 1.0, 0.0).astype(BF16)
-        total_u += dot(near[index][0:rows, :], pick)
-        total_d += dot(near[index][rows : 2 * rows, :], pick)
+        total_u += dot(near[index, 0:rows, :], pick)
+        total_d += dot(near[index, rows : 2 * rows, :], pick)
     others[0:rows, :] = total_u.astype(BF16)
     others[rows : 2 * rows, :] = total_d.astype(BF16)
     others[2 * rows :, :] = jnp.ones((16, nodes), BF16)
@@ -346,54 +443,68 @@
         out_d[:, at] = scale * d_ref[:, at].astype(F32) - pulled[rows : 2 * rows, :]
 
 
-def finish_kernel(modes, plane, me_ref, *refs):
+def finish_kernel(modes, rows, width, with_local, me_ref, *refs):
+    fields = len(with_local)
     pieces = refs[:modes]
-    local = refs[modes] if len(refs) == modes + 2 else None
-    out = refs[-1]
+    refs = refs[modes:]
+    count = sum(with_local)
+    locals_in = refs[:count]
+    outs = refs[count : count + fields]
+    held, result, in_sem, out_sem = refs[count + fields :]
     me = me_ref[0]
-    width = pieces[0].shape[2]
+
+    def at(d):
+        return pl.ds(pl.multiple_of(jnp.bitwise_xor(me, d) * width, width), width)
+
+    def load(i, d):
+        return pltpu.make_async_copy(locals_in[i].at[:, at(d)], held.at[i, d], in_sem.at[i, d])
+
+    def store(f, d):
+        return pltpu.make_async_copy(result.at[f, d], outs[f].at[:, at(d)], out_sem.at[f, d])
+
     for d in range(modes):
-        block = lax.rem(me - d + modes, modes)
-        at = pl.ds(pl.multiple_of(block * width, width), width)
-        value = pieces[d][plane].astype(F32)
-        if local is not None:
-            value = value + local[:, at]
-        out[:, at] = value
-
-
-def finish(pieces, plane, local, me):
+        for i in range(count):
+            load(i, d).start()
+    for d in range(modes):
+        seen = 0
+        for f in range(fields):
+            value = pieces[d][f].astype(F32)
+            if with_local[f]:
+                load(seen, d).wait()
+                value = value + held[seen, d]
+                seen += 1
+            result[f, d] = value
+            store(f, d).start()
+    for d in range(modes):
+        for f in range(fields):
+            store(f, d).wait()
+
+
+def finish(pieces, local, me):
     modes = len(pieces)
-    rows, width = pieces[0].shape[1:]
-    operands = [me, *pieces] + ([] if local is None else [local])
-    return pl.pallas_call(
-        functools.partial(finish_kernel, modes, plane),
-        out_shape=jax.ShapeDtypeStruct((rows, modes * width), F32),
-        in_specs=[SMEM] + [VMEM] * (len(operands) - 1),
-        out_specs=VMEM,
-        compiler_params=pltpu.CompilerParams(vmem_limit_bytes=VMEM_LIMIT),
-        name="finish",
-    )(*operands)
-
-
-def pass_kernel(*refs):
-    del refs
-
-
-def after(values, others):
+    fields, rows, width = pieces[0].shape
+    with_local = tuple(part is not None for part in local)
+    present = [part for part in local if part is not None]
     anywhere = pl.BlockSpec(memory_space=pl.ANY)
     return pl.pallas_call(
-        pass_kernel,
-        out_shape=[jax.ShapeDtypeStruct(v.shape, v.dtype) for v in values],
-        in_specs=[anywhere] * (len(values) + len(others)),
-        out_specs=[anywhere] * len(values),
-        input_output_aliases={i: i for i in range(len(values))},
-        name="after",
-    )(*values, *others)
-
-
-def shift_by(block, axis, distance):
+        functools.partial(finish_kernel, modes, rows, width, with_local),
+        out_shape=[jax.ShapeDtypeStruct((rows, modes * width), F32)] * fields,
+        in_specs=[SMEM] + [VMEM] * modes + [anywhere] * len(present),
+        out_specs=[anywhere] * fields,
+        scratch_shapes=[
+            pltpu.VMEM((len(present), modes, rows, width), F32),
+            pltpu.VMEM((fields, modes, rows, width), F32),
+            pltpu.SemaphoreType.DMA((len(present), modes)),
+            pltpu.SemaphoreType.DMA((fields, modes)),
+        ],
+        compiler_params=pltpu.CompilerParams(vmem_limit_bytes=16 * MIB),
+        name="finish",
+    )(me, *pieces, *present)
+
+
+def swap_with(block, axis, distance):
     count = lax.axis_size(axis)
-    return lax.ppermute(block, axis, [(i, (i + distance) % count) for i in range(count)])
+    return lax.ppermute(block, axis, [(i, i ^ distance) for i in range(count)])
 
 
 def on_device(u_spec, dir_spec, advecting, viscosity, degrees, edge_side, edge_link):
@@ -423,51 +534,70 @@
             sloped,
             np.ascontiguousarray(synthesis.T),
             np.ascontiguousarray(sloped.T),
-            mass.astype(np.float32)[None, :],
             split_pair(kron_x.T),
             split_pair(kron_y.T),
             split_pair(kron_x),
             split_pair(kron_y),
         )
     ]
+    mass_row = jnp.asarray(mass.astype(np.float32)[None, :])
 
     def cut(field):
         return [
-            lax.dynamic_slice_in_dim(field, lax.rem(my_mode + d, modes) * width, width, axis=1)
-            for d in range(modes)
+            lax.dynamic_slice_in_dim(
+                field, jnp.bitwise_xor(my_mode, d) * width, width, axis=1
+            )
+            for d in range(1, modes)
         ]
 
+    order = [*range(2, modes), 1]
     u_cut = cut(u_spec)
-    u_pieces = [u_cut[0]] + [shift_by(u_cut[d], "mode", d) for d in range(1, modes)]
-    d_cut = cut(dir_spec)
-    d_send = after(d_cut[1:], u_pieces[1:])
-    d_pieces = [d_cut[0]] + [shift_by(d_send[d - 1], "mode", d) for d in range(1, modes)]
-
+    far = pl.BlockSpec(memory_space=pltpu.HBM)
+    fields_held = [pltpu.VMEM((rows, columns), BF16)] * 2 + [pltpu.SemaphoreType.DMA((2,))]
     table_row = jnp.concatenate([edge_side[None, :], edge_link], axis=0)
     table_col = table_row.T
-    near = pl.pallas_call(
+    table_row, table_col, u_cut = lax.optimization_barrier((table_row, table_col, u_cut))
+    messages = pl.pallas_call(
         functools.partial(traces_kernel, parts, block_elements),
-        out_shape=[jax.ShapeDtypeStruct((2 * rows + 16, MSG), BF16)] * len(OFFSETS),
-        in_specs=[SMEM] + [VMEM] * 5,
-        out_specs=[VMEM] * len(OFFSETS),
-        compiler_params=pltpu.CompilerParams(vmem_limit_bytes=VMEM_LIMIT),
+        out_shape=jax.ShapeDtypeStruct((parts, 2 * rows + 16, MSG), BF16),
+        in_specs=[SMEM, far, far] + [VMEM] * 3,
+        out_specs=VMEM,
+        scratch_shapes=fields_held,
+        compiler_params=pltpu.CompilerParams(vmem_limit_bytes=20 * MIB),
         name="traces",
     )(part_id, u_spec, dir_spec, table_row, table_col, degrees)
-    by_offset = {o: shift_by(block, "elem", o) for o, block in zip(OFFSETS, near)}
-    near = [by_offset[-o] for o in OFFSETS]
-
-    u_back = planes(u_pieces, tables, viscosity, advecting, mode_id)
-    d_back = planes(d_pieces, tables, viscosity, None, mode_id)
+
+    u_pieces = [u_spec] + [None] * (modes - 1)
+    for d in order:
+        u_pieces[d] = swap_with(u_cut[d - 1], "mode", d)
+    d_cut, u_pieces[1] = lax.optimization_barrier((cut(dir_spec), u_pieces[1]))
+    d_pieces = [dir_spec] + [None] * (modes - 1)
+    for d in order:
+        d_pieces[d] = swap_with(d_cut[d - 1], "mode", d)
+
+    u_pieces[1], messages = lax.optimization_barrier((u_pieces[1], messages))
+    near = lax.all_to_all(messages, "elem", split_axis=0, concat_axis=0, tiled=True)
+    u_back = planes(u_pieces, tables, viscosity, mass_row, advecting, mode_id)
+    d_pieces[1], u_back = lax.optimization_barrier((d_pieces[1], list(u_back)))
+    u_returned = [u_back[0]] + [None] * (modes - 1)
+    for d in order:
+        u_returned[d] = swap_with(u_back[d], "mode", d)
+    d_back = planes(d_pieces, tables, viscosity, mass_row, None, mode_id)
 
     edge_weight = np.tile(LENGTH * weights, slots).astype(np.float32)[None, :]
     mass_local = np.tile(mass, modes).astype(np.float32)[None, :]
     local_u, local_d = pl.pallas_call(
         functools.partial(penalty_kernel, parts, block_elements),
         out_shape=[jax.ShapeDtypeStruct((rows, columns), F32)] * 2,
-        in_specs=[SMEM] + [VMEM] * 12,
+        in_specs=[SMEM, far, far] + [VMEM] * 6 + [far],
         out_specs=[VMEM] * 2,
-        scratch_shapes=[pltpu.VMEM((2 * rows + 16, slots * NQ), BF16)],
-        compiler_params=pltpu.CompilerParams(vmem_limit_bytes=VMEM_LIMIT),
+        scratch_shapes=[pltpu.VMEM((2 * rows + 16, slots * NQ), BF16)]
+        + fields_held
+        + [
+            pltpu.VMEM((len(OFFSETS), 2 * rows + 16, MSG), BF16),
+            pltpu.SemaphoreType.DMA((len(OFFSETS),)),
+        ],
+        compiler_params=pltpu.CompilerParams(vmem_limit_bytes=32 * MIB),
         cost_estimate=pl.CostEstimate(
             flops=2 * 2 * rows * slots * NQ * 3 * columns,
             bytes_accessed=20 * rows * columns,
@@ -484,17 +614,15 @@
         degrees.T,
         jnp.asarray(edge_weight),
         jnp.asarray(mass_local),
-        *near,
+        near,
     )
 
-    def returned(back):
-        return [back[0]] + [shift_by(back[d], "mode", d) for d in range(1, modes)]
-
-    u_returned = returned(u_back)
-    d_returned = returned(d_back)
-    advect = finish(u_returned, 0, None, mode_id)
-    helm_velocity = finish(u_returned, 1, local_u, mode_id)
-    helm_direction = finish(d_returned, 0, local_d, mode_id)
+    d_back, u_returned[1], local_d = lax.optimization_barrier((d_back, u_returned[1], local_d))
+    d_returned = [d_back[0]] + [None] * (modes - 1)
+    for d in order:
+        d_returned[d] = swap_with(d_back[d], "mode", d)
+    advect, helm_velocity = finish(u_returned, [None, local_u], mode_id)
+    (helm_direction,) = finish(d_returned, [local_d], mode_id)
     return (advect, helm_velocity, helm_direction)
 
 

time: 136 us -> 121 us (0.89)
  waiting for transfers between devices: 44.7 us -> 35.7 us
  Pallas kernels: 63.6 us -> 55.3 us
  starting transfers between devices: 18.7 us -> 21 us
    ppermute x16 -> x12, waiting for transfers between devices: 44.7 us -> 35.7 us  [swap_with(): return lax.ppermute(block, axis, [(i, i ^ distance) for i in range(count)])]
    pallas_call x6 -> x4, Pallas kernels: 45.3 us -> 40.4 us  [the longest x2 35.4 us: planes(): pl.pallas_call(functools.partial(planes_kernel, modes, chunk, advected),...]
    all_to_all x0 -> x1, starting transfers between devices: none -> 4.61 us  [on_device(): lax.all_to_all(messages, 'elem', split_axis=0, concat_axis=0, tiled=True)]
    pallas_call x1, Pallas kernels: 13.4 us -> 10.6 us  [on_device(): pl.pallas_call(functools.partial(penalty_kernel, parts, block_elements),...]
    ppermute x16 -> x12, starting transfers between devices: 18.7 us -> 16.3 us  [swap_with(): return lax.ppermute(block, axis, [(i, i ^ distance) for i in range(count)])]
    unnamed x51 -> x39, local copies, waits for them, and re-layouts: 3.65 us -> 4.9 us
  transfers between devices with their start and end apart: 16 -> 13, of which waited for: 8 -> 4; matrix products, arithmetic and copies ran while one was open for 2% -> 1% of each run, Pallas kernels for 44% -> 44%
where the time goes in v2:
time: 121 us
  Pallas kernels  55.3 us (46%)
  waiting for transfers between devices  35.7 us (30%)
  starting transfers between devices  21 us (17%)
  local copies, waits for them, and re-layouts  6.98 us (6%)
    ppermute x12, waiting for transfers between devices, swap_with(): return lax.ppermute(block, axis, [(i, i ^ distance) for i in range(count)])  35.7 us
    pallas_call x2, Pallas kernels, planes(): pl.pallas_call(functools.partial(planes_kernel, modes, chunk, advected),...  35.4 us
    ppermute x12, starting transfers between devices, swap_with(): return lax.ppermute(block, axis, [(i, i ^ distance) for i in range(count)])  16.3 us
    pallas_call x1, Pallas kernels, on_device(): pl.pallas_call(functools.partial(penalty_kernel, parts, block_elements),...  10.6 us
    pallas_call x2, Pallas kernels, finish(): pl.pallas_call(functools.partial(finish_kernel, modes, rows, width, with_...  4.97 us
    unnamed x39, local copies, waits for them, and re-layouts  4.9 us
    all_to_all x1, starting transfers between devices, on_device(): lax.all_to_all(messages, 'elem', split_axis=0, concat_axis=0, tiled=True)  4.61 us
    pallas_call x1, Pallas kernels, on_device(): pl.pallas_call(functools.partial(traces_kernel, parts, block_elements), o...  4.34 us
  transfers between devices with their start and end apart: 13, of which 4 were waited for; matrix products, arithmetic and copies ran while one was open for 1% of the time, Pallas kernels for 44%

profile of v2, /device:TPU:10, one launch (start us, length us, event | category | flops | bytes accessed | tf_op | source)
XLA Modules:
  0.0 120.8 jit_solution(3352950085521445775)
XLA Ops:
  0.7 0.8 pad_add_fusion.row_ref
  1.4 0.1 copy.26
  1.6 1.2 constant_dynamic-slice_fusion
  2.7 0.5 collective-permute-start
  3.3 2.6 %collective-permute-start.2 = (bf16[256,512]{1,0:T(8,128)(2,1)S(1)}, bf16[256,512]{1,0:T(8,128)(2,1)S(1)}, u32[]{:S(2)}, u32[]{:S(2)}) collective-permute-start(bf16[256,512]{1,0:T(8,128)(2,1)S(1)} %get-tuple-element.43), channel_id=1, source_target_pairs={{0,2},{1,3},{2,0},{3,1},{4,6},{5,7},{6,4},{7,5},{8,10},{9,11},{10,... | collective-permute-start | bytes 786440 | tf_op jit(solution)/shard_map/ppermute | solution.py:507
  5.8 0.5 collective-permute-start.3
  6.3 1.2 %copy-done.2 = bf16[256,2048]{1,0:T(8,128)(2,1)S(1)} copy-done((bf16[256,2048]{1,0:T(8,128)(2,1)S(1)}, bf16[256,2048]{1,0:T(8,128)(2,1)}, u32[]{:S(2)}) %copy-start.2) | copy-done | bytes 1048600
  7.5 0.7 copy-done.6
  8.2 4.3 %traces.1 = bf16[8,528,256]{2,1,0:T(8,128)(2,1)} custom-call(s32[1]{0:T(128)} %bitcast.3.me_ref, bf16[256,2048]{1,0:T(8,128)(2,1)S(1)} %copy-done, bf16[256,2048]{1,0:T(8,128)(2,1)S(1)} %copy-done.2, s32[4,128]{1,0:T(4,128)S(1)} %pad_add_fusion.row_ref, s32[128,4]{1,0:T(8,128)S(1)} %bitcast.5, s32[2,32]{1,0:T(2,128)S(1)} %copy-done.6), custom_call_target="tpu_custom_call" | custom-call | tf_op jit(solution)/shard_map/traces/pallas_call | solution.py:560
  12.5 0.8 constant_dynamic-slice_fusion.3
  13.3 0.3 collective-permute-done.refs_1_
  13.7 0.7 copy-done.14
  14.4 4.6 %all-to-all-start = ((bf16[8,528,256]{2,1,0:T(8,128)(2,1)}), bf16[8,528,256]{2,1,0:T(8,128)(2,1)}, u32[]{:S(2)}, u32[]{:S(2)}) async-start(bf16[8,528,256]{2,1,0:T(8,128)(2,1)} %traces.1), calls=%async_computation | async-start | bytes 4325376 | tf_op jit(solution)/shard_map/all_to_all | solution.py:579
  19.1 2.5 %collective-permute-start.1 = (bf16[256,512]{1,0:T(8,128)(2,1)S(1)}, bf16[256,512]{1,0:T(8,128)(2,1)S(1)}, u32[]{:S(2)}, u32[]{:S(2)}) collective-permute-start(bf16[256,512]{1,0:T(8,128)(2,1)S(1)} %get-tuple-element.38), channel_id=1, source_target_pairs={{0,1},{1,0},{2,3},{3,2},{4,5},{5,4},{6,7},{7,6},{8,9},{9,8},{10,11... | collective-permute-start | bytes 786440 | tf_op jit(solution)/shard_map/ppermute | solution.py:507
  21.6 1.8 %collective-permute-start.4 = (bf16[256,512]{1,0:T(8,128)(2,1)}, bf16[256,512]{1,0:T(8,128)(2,1)S(1)}, u32[]{:S(2)}, u32[]{:S(2)}) collective-permute-start(bf16[256,512]{1,0:T(8,128)(2,1)} %get-tuple-element.51), channel_id=1, source_target_pairs={{0,2},{1,3},{2,0},{3,1},{4,6},{5,7},{6,4},{7,5},{8,10},{9,11},{10,... | collective-permute-start | bytes 786440 | tf_op jit(solution)/shard_map/ppermute | solution.py:507
  23.4 0.5 collective-permute-start.5
  23.9 17.7 %collective-permute-done.3.refs_3_ = bf16[256,512]{1,0:T(8,128)(2,1)S(1)} collective-permute-done((bf16[256,512]{1,0:T(8,128)(2,1)S(1)}, bf16[256,512]{1,0:T(8,128)(2,1)S(1)}, u32[]{:S(2)}, u32[]{:S(2)}) %collective-permute-start.3) | collective-permute-done | bytes 262176 | tf_op jit(solution)/shard_map/ppermute | solution.py:507
  41.6 0.7 copy-done.18
  42.3 18.8 %planes_moved.1 = (bf16[2,256,512]{2,1,0:T(8,128)(2,1)}, bf16[2,256,512]{2,1,0:T(8,128)(2,1)}, bf16[2,256,512]{2,1,0:T(8,128)(2,1)}, bf16[2,256,512]{2,1,0:T(8,128)(2,1)}) custom-call(s32[1]{0:T(128)} %bitcast.me_ref, bf16[256,2048]{1,0:T(8,128)(2,1)} %u_in.3, bf16[256,512]{1,0:T(8,128)(2,1)} %copy-done.14, bf16[256,512]{1,0:T(8,128)(2,1)} %copy-done.16, ...), custom_call_target="tpu_custom_call" | custom-call | flops 10200547328 | bytes 12582912 | tf_op jit(solution)/shard_map/planes_moved/pallas_call | solution.py:237
  61.3 3.0 %collective-permute-start.7 = (bf16[2,256,512]{2,1,0:T(8,128)(2,1)}, bf16[2,256,512]{2,1,0:T(8,128)(2,1)S(1)}, u32[]{:S(2)}, u32[]{:S(2)}) collective-permute-start(bf16[2,256,512]{2,1,0:T(8,128)(2,1)} %get-tuple-element.61), channel_id=1, source_target_pairs={{0,2},{1,3},{2,0},{3,1},{4,6},{5,7},{6,4},{7,5},{8,10},{9,11},{10,... | collective-permute-start | bytes 1572872 | tf_op jit(solution)/shard_map/ppermute | solution.py:507
  64.3 0.4 collective-permute-start.8
  64.8 0.7 copy-done.15
  65.5 0.7 copy-done.17
  66.2 16.6 %planes_plain.1 = (bf16[1,256,512]{2,1,0:T(8,128)(2,1)}, bf16[1,256,512]{2,1,0:T(8,128)(2,1)}, bf16[1,256,512]{2,1,0:T(8,128)(2,1)}, bf16[1,256,512]{2,1,0:T(8,128)(2,1)}) custom-call(s32[1]{0:T(128)} %bitcast.me_ref, bf16[256,2048]{1,0:T(8,128)(2,1)} %d_in.3, bf16[256,512]{1,0:T(8,128)(2,1)} %copy-done.13, bf16[256,512]{1,0:T(8,128)(2,1)} %copy-done.15, ...), custom_call_target="tpu_custom_call" | custom-call | flops 9126805504 | bytes 12582912 | tf_op jit(solution)/shard_map/planes_plain/pallas_call | solution.py:237
  82.9 10.6 %penalty.1 = (f32[256,2048]{1,0:T(8,128)S(1)}, f32[256,2048]{1,0:T(8,128)S(1)}) custom-call(s32[1]{0:T(128)} %bitcast.3.me_ref, bf16[256,2048]{1,0:T(8,128)(2,1)S(1)} %copy-done.1, bf16[256,2048]{1,0:T(8,128)(2,1)S(1)} %copy-done.3, s32[4,128]{1,0:T(4,128)S(1)} %pad_add_fusion.row_ref, s32[128,4]{1,0:T(8,128)S(1)} %bitcast.6, s32[2,32]{1,0:T(2,128)S(1)} %copy-done.7, ...), custom_call_target="tpu_custom_call" | custom-call | flops 6442450944 | bytes 10485760 | tf_op jit(solution)/shard_map/penalty/pallas_call | solution.py:589
  93.5 2.0 %collective-permute-start.10 = (bf16[1,256,512]{2,1,0:T(8,128)(2,1)S(1)}, bf16[1,256,512]{2,1,0:T(8,128)(2,1)S(1)}, u32[]{:S(2)}, u32[]{:S(2)}) collective-permute-start(bf16[1,256,512]{2,1,0:T(8,128)(2,1)S(1)} %copy-done.12), channel_id=1, source_target_pairs={{0,2},{1,3},{2,0},{3,1},{4,6},{5,7},{6,4},{7,5},{8,10},{9,11},{10,... | collective-permute-start | bytes 786440 | tf_op jit(solution)/shard_map/ppermute | solution.py:507
  95.6 0.5 collective-permute-start.11
  96.1 1.9 %collective-permute-start.9 = (bf16[1,256,512]{2,1,0:T(8,128)(2,1)S(1)}, bf16[1,256,512]{2,1,0:T(8,128)(2,1)S(1)}, u32[]{:S(2)}, u32[]{:S(2)}) collective-permute-start(bf16[1,256,512]{2,1,0:T(8,128)(2,1)S(1)} %copy-done.10), channel_id=1, source_target_pairs={{0,1},{1,0},{2,3},{3,2},{4,5},{5,4},{6,7},{7,6},{8,9},{9,8},{10,11... | collective-permute-start | bytes 786440 | tf_op jit(solution)/shard_map/ppermute | solution.py:507
  98.0 15.5 %collective-permute-done.8.refs_3_ = bf16[2,256,512]{2,1,0:T(8,128)(2,1)} collective-permute-done((bf16[2,256,512]{2,1,0:T(8,128)(2,1)}, bf16[2,256,512]{2,1,0:T(8,128)(2,1)}, u32[]{:S(2)}, u32[]{:S(2)}) %collective-permute-start.8) | collective-permute-done | bytes 524320 | tf_op jit(solution)/shard_map/ppermute | solution.py:507
  113.5 3.4 %finish.2 = (f32[256,2048]{1,0:T(8,128)}, f32[256,2048]{1,0:T(8,128)}) custom-call(s32[1]{0:T(128)} %bitcast.me_ref, bf16[2,256,512]{2,1,0:T(8,128)(2,1)S(1)} %copy-done.4, bf16[2,256,512]{2,1,0:T(8,128)(2,1)S(1)} %collective-permute-done.6.refs_1_, bf16[2,256,512]{2,1,0:T(8,128)(2,1)S(1)} %collective-permute-done.7.refs_2_, ...), custom_call_target="tpu_custom_call" | custom-call | tf_op jit(solution)/shard_map/finish/pallas_call | solution.py:489
  116.9 2.1 %collective-permute-done.11.refs_3_ = bf16[1,256,512]{2,1,0:T(8,128)(2,1)S(1)} collective-permute-done((bf16[1,256,512]{2,1,0:T(8,128)(2,1)S(1)}, bf16[1,256,512]{2,1,0:T(8,128)(2,1)S(1)}, u32[]{:S(2)}, u32[]{:S(2)}) %collective-permute-start.11) | collective-permute-done | bytes 262176 | tf_op jit(solution)/shard_map/ppermute | solution.py:507
  119.0 1.6 %finish.3 = f32[256,2048]{1,0:T(8,128)} custom-call(s32[1]{0:T(128)} %bitcast.me_ref, bf16[1,256,512]{2,1,0:T(8,128)(2,1)S(1)} %copy-done.5, bf16[1,256,512]{2,1,0:T(8,128)(2,1)S(1)} %collective-permute-done.9.refs_1_, bf16[1,256,512]{2,1,0:T(8,128)(2,1)S(1)} %collective-permute-done.10.refs_2_, bf16[1,256,512]{2,1,0:T(8,128)(2,1)S(1)} %collective-permute-done.11.refs_3_, ...), custom_call_target="tpu_custom_call" | custom-call | tf_op jit(solution)/shard_map/finish/pallas_call | solution.py:489
  (43 shorter events, 0.3 us)
Async XLA Ops:
  0.6 5.7 %copy-start = (bf16[256,2048]{1,0:T(8,128)(2,1)S(1)}, bf16[256,2048]{1,0:T(8,128)(2,1)}, u32[]{:S(2)}) copy-start(bf16[256,2048]{1,0:T(8,128)(2,1)} %u_in.3) | copy-start | bytes 3145732
  2.7 10.9 %collective-permute-start = (bf16[256,512]{1,0:T(8,128)(2,1)S(1)}, bf16[256,512]{1,0:T(8,128)(2,1)S(1)}, u32[]{:S(2)}, u32[]{:S(2)}) collective-permute-start(bf16[256,512]{1,0:T(8,128)(2,1)S(1)} %get-tuple-element.37), channel_id=1, source_target_pairs={{0,1},{1,0},{2,3},{3,2},{4,5},{5,4},{6,7},{7,6},{8,9},{9,8},{10,11... | collective-permute-start | bytes 786440 | tf_op jit(solution)/shard_map/ppermute | solution.py:507
  3.3 20.6 %collective-permute-start.2 = (bf16[256,512]{1,0:T(8,128)(2,1)S(1)}, bf16[256,512]{1,0:T(8,128)(2,1)S(1)}, u32[]{:S(2)}, u32[]{:S(2)}) collective-permute-start(bf16[256,512]{1,0:T(8,128)(2,1)S(1)} %get-tuple-element.43), channel_id=1, source_target_pairs={{0,2},{1,3},{2,0},{3,1},{4,6},{5,7},{6,4},{7,5},{8,10},{9,11},{10,... | collective-permute-start | bytes 786440 | tf_op jit(solution)/shard_map/ppermute | solution.py:507
  5.8 35.7 %collective-permute-start.3 = (bf16[256,512]{1,0:T(8,128)(2,1)S(1)}, bf16[256,512]{1,0:T(8,128)(2,1)S(1)}, u32[]{:S(2)}, u32[]{:S(2)}) collective-permute-start(bf16[256,512]{1,0:T(8,128)(2,1)S(1)} %get-tuple-element.44), channel_id=1, source_target_pairs={{0,3},{1,2},{2,1},{3,0},{4,7},{5,6},{6,5},{7,4},{8,11},{9,10},{10,... | collective-permute-start | bytes 786440 | tf_op jit(solution)/shard_map/ppermute | solution.py:507
  6.3 1.2 %copy-start.2 = (bf16[256,2048]{1,0:T(8,128)(2,1)S(1)}, bf16[256,2048]{1,0:T(8,128)(2,1)}, u32[]{:S(2)}) copy-start(bf16[256,2048]{1,0:T(8,128)(2,1)} %d_in.3) | copy-start | bytes 3145732
  7.5 0.7 copy-start.6
  13.7 0.7 copy-start.14
  13.7 5.3 %copy-start.7 = (s32[2,32]{1,0:T(2,128)S(1)}, s32[2,32]{1,0:T(2,128)}, u32[]{:S(2)}) copy-start(s32[2,32]{1,0:T(2,128)} %deg_ref.3) | copy-start | bytes 772
  14.4 68.4 %all-to-all-start = ((bf16[8,528,256]{2,1,0:T(8,128)(2,1)}), bf16[8,528,256]{2,1,0:T(8,128)(2,1)}, u32[]{:S(2)}, u32[]{:S(2)}) async-start(bf16[8,528,256]{2,1,0:T(8,128)(2,1)} %traces.1), calls=%async_computation | async-start | bytes 4325376 | tf_op jit(solution)/shard_map/all_to_all | solution.py:579
  19.1 42.0 %collective-permute-start.1 = (bf16[256,512]{1,0:T(8,128)(2,1)S(1)}, bf16[256,512]{1,0:T(8,128)(2,1)S(1)}, u32[]{:S(2)}, u32[]{:S(2)}) collective-permute-start(bf16[256,512]{1,0:T(8,128)(2,1)S(1)} %get-tuple-element.38), channel_id=1, source_target_pairs={{0,1},{1,0},{2,3},{3,2},{4,5},{5,4},{6,7},{7,6},{8,9},{9,8},{10,11... | collective-permute-start | bytes 786440 | tf_op jit(solution)/shard_map/ppermute | solution.py:507
  21.6 43.2 %collective-permute-start.4 = (bf16[256,512]{1,0:T(8,128)(2,1)}, bf16[256,512]{1,0:T(8,128)(2,1)S(1)}, u32[]{:S(2)}, u32[]{:S(2)}) collective-permute-start(bf16[256,512]{1,0:T(8,128)(2,1)} %get-tuple-element.51), channel_id=1, source_target_pairs={{0,2},{1,3},{2,0},{3,1},{4,6},{5,7},{6,4},{7,5},{8,10},{9,11},{10,... | collective-permute-start | bytes 786440 | tf_op jit(solution)/shard_map/ppermute | solution.py:507
  23.4 41.4 %collective-permute-start.5 = (bf16[256,512]{1,0:T(8,128)(2,1)S(1)}, bf16[256,512]{1,0:T(8,128)(2,1)S(1)}, u32[]{:S(2)}, u32[]{:S(2)}) collective-permute-start(bf16[256,512]{1,0:T(8,128)(2,1)S(1)} %get-tuple-element.52), channel_id=1, source_target_pairs={{0,3},{1,2},{2,1},{3,0},{4,7},{5,6},{6,5},{7,4},{8,11},{9,10},{10,... | collective-permute-start | bytes 786440 | tf_op jit(solution)/shard_map/ppermute | solution.py:507
  23.9 17.7 %copy-start.16 = (bf16[256,512]{1,0:T(8,128)(2,1)}, bf16[256,512]{1,0:T(8,128)(2,1)S(1)}, u32[]{:S(2)}) copy-start(bf16[256,512]{1,0:T(8,128)(2,1)S(1)} %collective-permute-done.2.refs_2_) | copy-start | bytes 786436
  41.6 0.7 copy-start.18
  61.1 3.6 %copy-start.13 = (bf16[256,512]{1,0:T(8,128)(2,1)}, bf16[256,512]{1,0:T(8,128)(2,1)S(1)}, u32[]{:S(2)}) copy-start(bf16[256,512]{1,0:T(8,128)(2,1)S(1)} %collective-permute-done.1.refs_1_) | copy-start | bytes 786436
  61.2 21.6 %copy-start.1 = (bf16[256,2048]{1,0:T(8,128)(2,1)S(1)}, bf16[256,2048]{1,0:T(8,128)(2,1)}, u32[]{:S(2)}) copy-start(bf16[256,2048]{1,0:T(8,128)(2,1)} %u_in.3) | copy-start | bytes 3145732
  61.2 21.6 %copy-start.3 = (bf16[256,2048]{1,0:T(8,128)(2,1)S(1)}, bf16[256,2048]{1,0:T(8,128)(2,1)}, u32[]{:S(2)}) copy-start(bf16[256,2048]{1,0:T(8,128)(2,1)} %d_in.3) | copy-start | bytes 3145732
  61.2 21.6 %copy-start.8 = (f32[1,2048]{1,0:T(1,128)S(1)}, f32[1,2048]{1,0:T(1,128)}, u32[]{:S(2)}) copy-start(f32[1,2048]{1,0:T(1,128)} %constant.53.clone.mass_ref) | copy-start | bytes 24580
  61.2 21.6 %copy-start.9 = (f32[1,1024]{1,0:T(1,128)S(1)}, f32[1,1024]{1,0:T(1,128)}, u32[]{:S(2)}) copy-start(f32[1,1024]{1,0:T(1,128)} %constant.52.clone.weight_ref) | copy-start | bytes 12292
  61.2 32.3 %collective-permute-start.6 = (bf16[2,256,512]{2,1,0:T(8,128)(2,1)}, bf16[2,256,512]{2,1,0:T(8,128)(2,1)S(1)}, u32[]{:S(2)}, u32[]{:S(2)}) collective-permute-start(bf16[2,256,512]{2,1,0:T(8,128)(2,1)} %get-tuple-element.57), channel_id=1, source_target_pairs={{0,1},{1,0},{2,3},{3,2},{4,5},{5,4},{6,7},{7,6},{8,9},{9,8},{10,11... | collective-permute-start | bytes 1572872 | tf_op jit(solution)/shard_map/ppermute | solution.py:507
  61.3 36.7 %collective-permute-start.7 = (bf16[2,256,512]{2,1,0:T(8,128)(2,1)}, bf16[2,256,512]{2,1,0:T(8,128)(2,1)S(1)}, u32[]{:S(2)}, u32[]{:S(2)}) collective-permute-start(bf16[2,256,512]{2,1,0:T(8,128)(2,1)} %get-tuple-element.61), channel_id=1, source_target_pairs={{0,2},{1,3},{2,0},{3,1},{4,6},{5,7},{6,4},{7,5},{8,10},{9,11},{10,... | collective-permute-start | bytes 1572872 | tf_op jit(solution)/shard_map/ppermute | solution.py:507
  64.3 49.2 %collective-permute-start.8 = (bf16[2,256,512]{2,1,0:T(8,128)(2,1)}, bf16[2,256,512]{2,1,0:T(8,128)(2,1)}, u32[]{:S(2)}, u32[]{:S(2)}) collective-permute-start(bf16[2,256,512]{2,1,0:T(8,128)(2,1)} %get-tuple-element.62), channel_id=1, source_target_pairs={{0,3},{1,2},{2,1},{3,0},{4,7},{5,6},{6,5},{7,4},{8,11},{9,10},{10,... | collective-permute-start | bytes 1572872 | tf_op jit(solution)/shard_map/ppermute | solution.py:507
  64.8 0.7 copy-start.15
  65.5 0.7 copy-start.17
  82.8 10.7 %copy-start.12 = (bf16[1,256,512]{2,1,0:T(8,128)(2,1)S(1)}, bf16[1,256,512]{2,1,0:T(8,128)(2,1)}, u32[]{:S(2)}) copy-start(bf16[1,256,512]{2,1,0:T(8,128)(2,1)} %get-tuple-element.68) | copy-start | bytes 786436
  82.8 12.7 %copy-start.11 = (bf16[1,256,512]{2,1,0:T(8,128)(2,1)S(1)}, bf16[1,256,512]{2,1,0:T(8,128)(2,1)}, u32[]{:S(2)}) copy-start(bf16[1,256,512]{2,1,0:T(8,128)(2,1)} %get-tuple-element.69) | copy-start | bytes 786436
  82.9 13.2 %copy-start.10 = (bf16[1,256,512]{2,1,0:T(8,128)(2,1)S(1)}, bf16[1,256,512]{2,1,0:T(8,128)(2,1)}, u32[]{:S(2)}) copy-start(bf16[1,256,512]{2,1,0:T(8,128)(2,1)} %get-tuple-element.67) | copy-start | bytes 786436
  82.9 30.6 %copy-start.4 = (bf16[2,256,512]{2,1,0:T(8,128)(2,1)S(1)}, bf16[2,256,512]{2,1,0:T(8,128)(2,1)}, u32[]{:S(2)}) copy-start(bf16[2,256,512]{2,1,0:T(8,128)(2,1)} %get-tuple-element.49.refs_0_) | copy-start | bytes 1572868
  93.5 23.4 %collective-permute-start.10 = (bf16[1,256,512]{2,1,0:T(8,128)(2,1)S(1)}, bf16[1,256,512]{2,1,0:T(8,128)(2,1)S(1)}, u32[]{:S(2)}, u32[]{:S(2)}) collective-permute-start(bf16[1,256,512]{2,1,0:T(8,128)(2,1)S(1)} %copy-done.12), channel_id=1, source_target_pairs={{0,2},{1,3},{2,0},{3,1},{4,6},{5,7},{6,4},{7,5},{8,10},{9,11},{10,... | collective-permute-start | bytes 786440 | tf_op jit(solution)/shard_map/ppermute | solution.py:507
  95.6 23.4 %collective-permute-start.11 = (bf16[1,256,512]{2,1,0:T(8,128)(2,1)S(1)}, bf16[1,256,512]{2,1,0:T(8,128)(2,1)S(1)}, u32[]{:S(2)}, u32[]{:S(2)}) collective-permute-start(bf16[1,256,512]{2,1,0:T(8,128)(2,1)S(1)} %copy-done.11), channel_id=1, source_target_pairs={{0,3},{1,2},{2,1},{3,0},{4,7},{5,6},{6,5},{7,4},{8,11},{9,10},{10,... | collective-permute-start | bytes 786440 | tf_op jit(solution)/shard_map/ppermute | solution.py:507
  96.1 22.9 %collective-permute-start.9 = (bf16[1,256,512]{2,1,0:T(8,128)(2,1)S(1)}, bf16[1,256,512]{2,1,0:T(8,128)(2,1)S(1)}, u32[]{:S(2)}, u32[]{:S(2)}) collective-permute-start(bf16[1,256,512]{2,1,0:T(8,128)(2,1)S(1)} %copy-done.10), channel_id=1, source_target_pairs={{0,1},{1,0},{2,3},{3,2},{4,5},{5,4},{6,7},{7,6},{8,9},{9,8},{10,11... | collective-permute-start | bytes 786440 | tf_op jit(solution)/shard_map/ppermute | solution.py:507
  113.5 5.5 %copy-start.5 = (bf16[1,256,512]{2,1,0:T(8,128)(2,1)S(1)}, bf16[1,256,512]{2,1,0:T(8,128)(2,1)}, u32[]{:S(2)}) copy-start(bf16[1,256,512]{2,1,0:T(8,128)(2,1)} %get-tuple-element.66.refs_0_) | copy-start | bytes 786436

commit v3 on v2

--- a/solution.py
+++ b/solution.py
@@ -443,41 +443,30 @@
         out_d[:, at] = scale * d_ref[:, at].astype(F32) - pulled[rows : 2 * rows, :]
 
 
-def finish_kernel(modes, rows, width, with_local, me_ref, *refs):
+def finish_kernel(modes, width, with_local, me_ref, *refs):
     fields = len(with_local)
-    pieces = refs[:modes]
-    refs = refs[modes:]
     count = sum(with_local)
-    locals_in = refs[:count]
-    outs = refs[count : count + fields]
-    held, result, in_sem, out_sem = refs[count + fields :]
+    pieces, refs = refs[:modes], refs[modes:]
+    locals_in, outs = refs[:count], refs[count : count + fields]
+    result, sem = refs[count + fields :]
     me = me_ref[0]
 
     def at(d):
         return pl.ds(pl.multiple_of(jnp.bitwise_xor(me, d) * width, width), width)
 
-    def load(i, d):
-        return pltpu.make_async_copy(locals_in[i].at[:, at(d)], held.at[i, d], in_sem.at[i, d])
-
-    def store(f, d):
-        return pltpu.make_async_copy(result.at[f, d], outs[f].at[:, at(d)], out_sem.at[f, d])
-
-    for d in range(modes):
-        for i in range(count):
-            load(i, d).start()
+    stores = []
     for d in range(modes):
         seen = 0
         for f in range(fields):
             value = pieces[d][f].astype(F32)
             if with_local[f]:
-                load(seen, d).wait()
-                value = value + held[seen, d]
+                value = value + locals_in[seen][:, at(d)]
                 seen += 1
             result[f, d] = value
-            store(f, d).start()
-    for d in range(modes):
-        for f in range(fields):
-            store(f, d).wait()
+            stores.append(pltpu.make_async_copy(result.at[f, d], outs[f].at[:, at(d)], sem.at[f, d]))
+            stores[-1].start()
+    for store in stores:
+        store.wait()
 
 
 def finish(pieces, local, me):
@@ -485,16 +474,13 @@
     fields, rows, width = pieces[0].shape
     with_local = tuple(part is not None for part in local)
     present = [part for part in local if part is not None]
-    anywhere = pl.BlockSpec(memory_space=pl.ANY)
     return pl.pallas_call(
-        functools.partial(finish_kernel, modes, rows, width, with_local),
+        functools.partial(finish_kernel, modes, width, with_local),
         out_shape=[jax.ShapeDtypeStruct((rows, modes * width), F32)] * fields,
-        in_specs=[SMEM] + [VMEM] * modes + [anywhere] * len(present),
-        out_specs=[anywhere] * fields,
+        in_specs=[SMEM] + [VMEM] * (modes + len(present)),
+        out_specs=[pl.BlockSpec(memory_space=pl.ANY)] * fields,
         scratch_shapes=[
-            pltpu.VMEM((len(present), modes, rows, width), F32),
             pltpu.VMEM((fields, modes, rows, width), F32),
-            pltpu.SemaphoreType.DMA((len(present), modes)),
             pltpu.SemaphoreType.DMA((fields, modes)),
         ],
         compiler_params=pltpu.CompilerParams(vmem_limit_bytes=16 * MIB),
@@ -554,9 +540,9 @@
     u_cut = cut(u_spec)
     far = pl.BlockSpec(memory_space=pltpu.HBM)
     fields_held = [pltpu.VMEM((rows, columns), BF16)] * 2 + [pltpu.SemaphoreType.DMA((2,))]
+    edge_side, edge_link, u_cut = lax.optimization_barrier((edge_side, edge_link, u_cut))
     table_row = jnp.concatenate([edge_side[None, :], edge_link], axis=0)
     table_col = table_row.T
-    table_row, table_col, u_cut = lax.optimization_barrier((table_row, table_col, u_cut))
     messages = pl.pallas_call(
         functools.partial(traces_kernel, parts, block_elements),
         out_shape=jax.ShapeDtypeStruct((parts, 2 * rows + 16, MSG), BF16),

time: 121 us -> 120 us (level)
  transfers between devices with their start and end apart: 13 -> 13, of which waited for: 4 -> 3; matrix products, arithmetic and copies ran while one was open for 1% -> 1% of each run, Pallas kernels for 44% -> 45%
where the time goes in v3:
time: 120 us
  Pallas kernels  55 us (46%)
  waiting for transfers between devices  35.5 us (30%)
  starting transfers between devices  20.5 us (17%)
  local copies, waits for them, and re-layouts  7.05 us (6%)
    ppermute x12, waiting for transfers between devices, swap_with(): return lax.ppermute(block, axis, [(i, i ^ distance) for i in range(count)])  35.5 us
    pallas_call x2, Pallas kernels, planes(): pl.pallas_call(functools.partial(planes_kernel, modes, chunk, advected),...  35.4 us
    ppermute x12, starting transfers between devices, swap_with(): return lax.ppermute(block, axis, [(i, i ^ distance) for i in range(count)])  15.7 us
    pallas_call x1, Pallas kernels, on_device(): pl.pallas_call(functools.partial(penalty_kernel, parts, block_elements),...  10.6 us
    unnamed x39, local copies, waits for them, and re-layouts  4.89 us
    all_to_all x1, starting transfers between devices, on_device(): lax.all_to_all(messages, 'elem', split_axis=0, concat_axis=0, tiled=True)  4.79 us
    pallas_call x2, Pallas kernels, finish(): pl.pallas_call(functools.partial(finish_kernel, modes, width, with_local)...  4.6 us
    pallas_call x1, Pallas kernels, on_device(): pl.pallas_call(functools.partial(traces_kernel, parts, block_elements), o...  4.34 us
  transfers between devices with their start and end apart: 13, of which 3 were waited for; matrix products, arithmetic and copies ran while one was open for 1% of the time, Pallas kernels for 45%

profile of v3, /device:TPU:10, one launch (start us, length us, event | category | flops | bytes accessed | tf_op | source)
XLA Modules:
  0.0 119.7 jit_solution(6414613712089140078)
XLA Ops:
  0.7 1.3 %constant_dynamic-slice_fusion = (bf16[256,512]{1,0:T(8,128)(2,1)S(1)}, bf16[256,512]{1,0:T(8,128)(2,1)S(1)}, bf16[256,512]{1,0:T(8,128)(2,1)S(1)}) fusion(bf16[256,2048]{1,0:T(8,128)(2,1)} %u_in.3, s32[]{:T(128)S(6)} %select_n.14, s32[]{:T(128)S(6)} %select_n.13, s32[]{:T(128)S(6)} %select_n.12), kind=kLoop, calls=%fused_computation.1 | loop fusion | bytes 1572876 | tf_op jit(solution)/shard_map/dynamic_slice | solution.py:533
  1.9 0.5 collective-permute-start
  2.4 2.6 %collective-permute-start.2 = (bf16[256,512]{1,0:T(8,128)(2,1)S(1)}, bf16[256,512]{1,0:T(8,128)(2,1)S(1)}, u32[]{:S(2)}, u32[]{:S(2)}) collective-permute-start(bf16[256,512]{1,0:T(8,128)(2,1)S(1)} %get-tuple-element.43), channel_id=1, source_target_pairs={{0,2},{1,3},{2,0},{3,1},{4,6},{5,7},{6,4},{7,5},{8,10},{9,11},{10,... | collective-permute-start | bytes 786440 | tf_op jit(solution)/shard_map/ppermute | solution.py:493
  5.0 0.5 collective-permute-start.3
  5.5 0.7 pad_add_fusion.row_ref
  6.2 0.1 copy.26
  6.3 1.2 %copy-done.2 = bf16[256,2048]{1,0:T(8,128)(2,1)S(1)} copy-done((bf16[256,2048]{1,0:T(8,128)(2,1)S(1)}, bf16[256,2048]{1,0:T(8,128)(2,1)}, u32[]{:S(2)}) %copy-start.2) | copy-done | bytes 1048600
  7.5 0.7 copy-done.6
  8.2 4.3 %traces.1 = bf16[8,528,256]{2,1,0:T(8,128)(2,1)} custom-call(s32[1]{0:T(128)} %bitcast.1.me_ref, bf16[256,2048]{1,0:T(8,128)(2,1)S(1)} %copy-done, bf16[256,2048]{1,0:T(8,128)(2,1)S(1)} %copy-done.2, s32[4,128]{1,0:T(4,128)S(1)} %pad_add_fusion.row_ref, s32[128,4]{1,0:T(8,128)S(1)} %bitcast.5, s32[2,32]{1,0:T(2,128)S(1)} %copy-done.6), custom_call_target="tpu_custom_call" | custom-call | tf_op jit(solution)/shard_map/traces/pallas_call | solution.py:546
  12.5 0.8 constant_dynamic-slice_fusion.3
  13.3 0.7 copy-done.14
  14.1 4.8 %all-to-all-start = ((bf16[8,528,256]{2,1,0:T(8,128)(2,1)}), bf16[8,528,256]{2,1,0:T(8,128)(2,1)}, u32[]{:S(2)}, u32[]{:S(2)}) async-start(bf16[8,528,256]{2,1,0:T(8,128)(2,1)} %traces.1), calls=%async_computation | async-start | bytes 4325376 | tf_op jit(solution)/shard_map/all_to_all | solution.py:565
  18.9 0.1 copy.27
  18.9 1.8 %collective-permute-start.1 = (bf16[256,512]{1,0:T(8,128)(2,1)S(1)}, bf16[256,512]{1,0:T(8,128)(2,1)S(1)}, u32[]{:S(2)}, u32[]{:S(2)}) collective-permute-start(bf16[256,512]{1,0:T(8,128)(2,1)S(1)} %get-tuple-element.38), channel_id=1, source_target_pairs={{0,1},{1,0},{2,3},{3,2},{4,5},{5,4},{6,7},{7,6},{8,9},{9,8},{10,11... | collective-permute-start | bytes 786440 | tf_op jit(solution)/shard_map/ppermute | solution.py:493
  20.8 1.8 %collective-permute-start.4 = (bf16[256,512]{1,0:T(8,128)(2,1)}, bf16[256,512]{1,0:T(8,128)(2,1)S(1)}, u32[]{:S(2)}, u32[]{:S(2)}) collective-permute-start(bf16[256,512]{1,0:T(8,128)(2,1)} %get-tuple-element.51), channel_id=1, source_target_pairs={{0,2},{1,3},{2,0},{3,1},{4,6},{5,7},{6,4},{7,5},{8,10},{9,11},{10,... | collective-permute-start | bytes 786440 | tf_op jit(solution)/shard_map/ppermute | solution.py:493
  22.6 0.5 collective-permute-start.5
  23.1 17.7 %collective-permute-done.3.refs_3_ = bf16[256,512]{1,0:T(8,128)(2,1)S(1)} collective-permute-done((bf16[256,512]{1,0:T(8,128)(2,1)S(1)}, bf16[256,512]{1,0:T(8,128)(2,1)S(1)}, u32[]{:S(2)}, u32[]{:S(2)}) %collective-permute-start.3) | collective-permute-done | bytes 262176 | tf_op jit(solution)/shard_map/ppermute | solution.py:493
  40.8 0.7 copy-done.18
  41.5 18.8 %planes_moved.1 = (bf16[2,256,512]{2,1,0:T(8,128)(2,1)}, bf16[2,256,512]{2,1,0:T(8,128)(2,1)}, bf16[2,256,512]{2,1,0:T(8,128)(2,1)}, bf16[2,256,512]{2,1,0:T(8,128)(2,1)}) custom-call(s32[1]{0:T(128)} %bitcast.me_ref, bf16[256,2048]{1,0:T(8,128)(2,1)} %u_in.3, bf16[256,512]{1,0:T(8,128)(2,1)} %copy-done.14, bf16[256,512]{1,0:T(8,128)(2,1)} %copy-done.16, ...), custom_call_target="tpu_custom_call" | custom-call | flops 10200547328 | bytes 12582912 | tf_op jit(solution)/shard_map/planes_moved/pallas_call | solution.py:237
  60.5 3.0 %collective-permute-start.7 = (bf16[2,256,512]{2,1,0:T(8,128)(2,1)}, bf16[2,256,512]{2,1,0:T(8,128)(2,1)S(1)}, u32[]{:S(2)}, u32[]{:S(2)}) collective-permute-start(bf16[2,256,512]{2,1,0:T(8,128)(2,1)} %get-tuple-element.61), channel_id=1, source_target_pairs={{0,2},{1,3},{2,0},{3,1},{4,6},{5,7},{6,4},{7,5},{8,10},{9,11},{10,... | collective-permute-start | bytes 1572872 | tf_op jit(solution)/shard_map/ppermute | solution.py:493
  63.5 0.5 collective-permute-start.8
  64.0 0.7 copy-done.15
  64.7 0.7 copy-done.17
  65.4 16.6 %planes_plain.1 = (bf16[1,256,512]{2,1,0:T(8,128)(2,1)}, bf16[1,256,512]{2,1,0:T(8,128)(2,1)}, bf16[1,256,512]{2,1,0:T(8,128)(2,1)}, bf16[1,256,512]{2,1,0:T(8,128)(2,1)}) custom-call(s32[1]{0:T(128)} %bitcast.me_ref, bf16[256,2048]{1,0:T(8,128)(2,1)} %d_in.3, bf16[256,512]{1,0:T(8,128)(2,1)} %copy-done.13, bf16[256,512]{1,0:T(8,128)(2,1)} %copy-done.15, ...), custom_call_target="tpu_custom_call" | custom-call | flops 9126805504 | bytes 12582912 | tf_op jit(solution)/shard_map/planes_plain/pallas_call | solution.py:237
  82.1 10.6 %penalty.1 = (f32[256,2048]{1,0:T(8,128)S(1)}, f32[256,2048]{1,0:T(8,128)S(1)}) custom-call(s32[1]{0:T(128)} %bitcast.1.me_ref, bf16[256,2048]{1,0:T(8,128)(2,1)S(1)} %copy-done.1, bf16[256,2048]{1,0:T(8,128)(2,1)S(1)} %copy-done.3, s32[4,128]{1,0:T(4,128)S(1)} %pad_add_fusion.row_ref, s32[128,4]{1,0:T(8,128)S(1)} %bitcast.6, s32[2,32]{1,0:T(2,128)S(1)} %copy-done.7, ...), custom_call_target="tpu_custom_call" | custom-call | flops 6442450944 | bytes 10485760 | tf_op jit(solution)/shard_map/penalty/pallas_call | solution.py:575
  92.7 2.0 %collective-permute-start.10 = (bf16[1,256,512]{2,1,0:T(8,128)(2,1)S(1)}, bf16[1,256,512]{2,1,0:T(8,128)(2,1)S(1)}, u32[]{:S(2)}, u32[]{:S(2)}) collective-permute-start(bf16[1,256,512]{2,1,0:T(8,128)(2,1)S(1)} %copy-done.12), channel_id=1, source_target_pairs={{0,2},{1,3},{2,0},{3,1},{4,6},{5,7},{6,4},{7,5},{8,10},{9,11},{10,... | collective-permute-start | bytes 786440 | tf_op jit(solution)/shard_map/ppermute | solution.py:493
  94.7 0.5 collective-permute-start.11
  95.2 1.9 %collective-permute-start.9 = (bf16[1,256,512]{2,1,0:T(8,128)(2,1)S(1)}, bf16[1,256,512]{2,1,0:T(8,128)(2,1)S(1)}, u32[]{:S(2)}, u32[]{:S(2)}) collective-permute-start(bf16[1,256,512]{2,1,0:T(8,128)(2,1)S(1)} %copy-done.10), channel_id=1, source_target_pairs={{0,1},{1,0},{2,3},{3,2},{4,5},{5,4},{6,7},{7,6},{8,9},{9,8},{10,11... | collective-permute-start | bytes 786440 | tf_op jit(solution)/shard_map/ppermute | solution.py:493
  97.2 15.5 %collective-permute-done.8.refs_3_ = bf16[2,256,512]{2,1,0:T(8,128)(2,1)} collective-permute-done((bf16[2,256,512]{2,1,0:T(8,128)(2,1)}, bf16[2,256,512]{2,1,0:T(8,128)(2,1)}, u32[]{:S(2)}, u32[]{:S(2)}) %collective-permute-start.8) | collective-permute-done | bytes 524320 | tf_op jit(solution)/shard_map/ppermute | solution.py:493
  112.6 3.2 %finish.2 = (f32[256,2048]{1,0:T(8,128)}, f32[256,2048]{1,0:T(8,128)}) custom-call(s32[1]{0:T(128)} %bitcast.me_ref, bf16[2,256,512]{2,1,0:T(8,128)(2,1)S(1)} %copy-done.4, bf16[2,256,512]{2,1,0:T(8,128)(2,1)S(1)} %collective-permute-done.6.refs_1_, bf16[2,256,512]{2,1,0:T(8,128)(2,1)S(1)} %collective-permute-done.7.refs_2_, ...), custom_call_target="tpu_custom_call" | custom-call | tf_op jit(solution)/shard_map/finish/pallas_call | solution.py:477
  115.8 2.3 %collective-permute-done.11.refs_3_ = bf16[1,256,512]{2,1,0:T(8,128)(2,1)S(1)} collective-permute-done((bf16[1,256,512]{2,1,0:T(8,128)(2,1)S(1)}, bf16[1,256,512]{2,1,0:T(8,128)(2,1)S(1)}, u32[]{:S(2)}, u32[]{:S(2)}) %collective-permute-start.11) | collective-permute-done | bytes 262176 | tf_op jit(solution)/shard_map/ppermute | solution.py:493
  118.1 1.4 %finish.3 = f32[256,2048]{1,0:T(8,128)} custom-call(s32[1]{0:T(128)} %bitcast.me_ref, bf16[1,256,512]{2,1,0:T(8,128)(2,1)S(1)} %copy-done.5, bf16[1,256,512]{2,1,0:T(8,128)(2,1)S(1)} %collective-permute-done.9.refs_1_, bf16[1,256,512]{2,1,0:T(8,128)(2,1)S(1)} %collective-permute-done.10.refs_2_, bf16[1,256,512]{2,1,0:T(8,128)(2,1)S(1)} %collective-permute-done.11.refs_3_, ...), custom_call_target="tpu_custom_call" | custom-call | tf_op jit(solution)/shard_map/finish/pallas_call | solution.py:477
  (43 shorter events, 0.2 us)
Async XLA Ops:
  0.6 5.7 %copy-start = (bf16[256,2048]{1,0:T(8,128)(2,1)S(1)}, bf16[256,2048]{1,0:T(8,128)(2,1)}, u32[]{:S(2)}) copy-start(bf16[256,2048]{1,0:T(8,128)(2,1)} %u_in.3) | copy-start | bytes 3145732
  1.9 11.4 %collective-permute-start = (bf16[256,512]{1,0:T(8,128)(2,1)S(1)}, bf16[256,512]{1,0:T(8,128)(2,1)S(1)}, u32[]{:S(2)}, u32[]{:S(2)}) collective-permute-start(bf16[256,512]{1,0:T(8,128)(2,1)S(1)} %get-tuple-element.37), channel_id=1, source_target_pairs={{0,1},{1,0},{2,3},{3,2},{4,5},{5,4},{6,7},{7,6},{8,9},{9,8},{10,11... | collective-permute-start | bytes 786440 | tf_op jit(solution)/shard_map/ppermute | solution.py:493
  2.4 20.6 %collective-permute-start.2 = (bf16[256,512]{1,0:T(8,128)(2,1)S(1)}, bf16[256,512]{1,0:T(8,128)(2,1)S(1)}, u32[]{:S(2)}, u32[]{:S(2)}) collective-permute-start(bf16[256,512]{1,0:T(8,128)(2,1)S(1)} %get-tuple-element.43), channel_id=1, source_target_pairs={{0,2},{1,3},{2,0},{3,1},{4,6},{5,7},{6,4},{7,5},{8,10},{9,11},{10,... | collective-permute-start | bytes 786440 | tf_op jit(solution)/shard_map/ppermute | solution.py:493
  5.0 35.7 %collective-permute-start.3 = (bf16[256,512]{1,0:T(8,128)(2,1)S(1)}, bf16[256,512]{1,0:T(8,128)(2,1)S(1)}, u32[]{:S(2)}, u32[]{:S(2)}) collective-permute-start(bf16[256,512]{1,0:T(8,128)(2,1)S(1)} %get-tuple-element.44), channel_id=1, source_target_pairs={{0,3},{1,2},{2,1},{3,0},{4,7},{5,6},{6,5},{7,4},{8,11},{9,10},{10,... | collective-permute-start | bytes 786440 | tf_op jit(solution)/shard_map/ppermute | solution.py:493
  6.3 1.2 %copy-start.2 = (bf16[256,2048]{1,0:T(8,128)(2,1)S(1)}, bf16[256,2048]{1,0:T(8,128)(2,1)}, u32[]{:S(2)}) copy-start(bf16[256,2048]{1,0:T(8,128)(2,1)} %d_in.3) | copy-start | bytes 3145732
  7.5 0.7 copy-start.6
  13.3 0.7 copy-start.14
  13.3 5.5 %copy-start.7 = (s32[2,32]{1,0:T(2,128)S(1)}, s32[2,32]{1,0:T(2,128)}, u32[]{:S(2)}) copy-start(s32[2,32]{1,0:T(2,128)} %deg_ref.3) | copy-start | bytes 772
  14.1 67.9 %all-to-all-start = ((bf16[8,528,256]{2,1,0:T(8,128)(2,1)}), bf16[8,528,256]{2,1,0:T(8,128)(2,1)}, u32[]{:S(2)}, u32[]{:S(2)}) async-start(bf16[8,528,256]{2,1,0:T(8,128)(2,1)} %traces.1), calls=%async_computation | async-start | bytes 4325376 | tf_op jit(solution)/shard_map/all_to_all | solution.py:565
  18.9 41.4 %collective-permute-start.1 = (bf16[256,512]{1,0:T(8,128)(2,1)S(1)}, bf16[256,512]{1,0:T(8,128)(2,1)S(1)}, u32[]{:S(2)}, u32[]{:S(2)}) collective-permute-start(bf16[256,512]{1,0:T(8,128)(2,1)S(1)} %get-tuple-element.38), channel_id=1, source_target_pairs={{0,1},{1,0},{2,3},{3,2},{4,5},{5,4},{6,7},{7,6},{8,9},{9,8},{10,11... | collective-permute-start | bytes 786440 | tf_op jit(solution)/shard_map/ppermute | solution.py:493
  20.8 43.2 %collective-permute-start.4 = (bf16[256,512]{1,0:T(8,128)(2,1)}, bf16[256,512]{1,0:T(8,128)(2,1)S(1)}, u32[]{:S(2)}, u32[]{:S(2)}) collective-permute-start(bf16[256,512]{1,0:T(8,128)(2,1)} %get-tuple-element.51), channel_id=1, source_target_pairs={{0,2},{1,3},{2,0},{3,1},{4,6},{5,7},{6,4},{7,5},{8,10},{9,11},{10,... | collective-permute-start | bytes 786440 | tf_op jit(solution)/shard_map/ppermute | solution.py:493
  22.6 41.4 %collective-permute-start.5 = (bf16[256,512]{1,0:T(8,128)(2,1)S(1)}, bf16[256,512]{1,0:T(8,128)(2,1)S(1)}, u32[]{:S(2)}, u32[]{:S(2)}) collective-permute-start(bf16[256,512]{1,0:T(8,128)(2,1)S(1)} %get-tuple-element.52), channel_id=1, source_target_pairs={{0,3},{1,2},{2,1},{3,0},{4,7},{5,6},{6,5},{7,4},{8,11},{9,10},{10,... | collective-permute-start | bytes 786440 | tf_op jit(solution)/shard_map/ppermute | solution.py:493
  23.1 17.7 %copy-start.16 = (bf16[256,512]{1,0:T(8,128)(2,1)}, bf16[256,512]{1,0:T(8,128)(2,1)S(1)}, u32[]{:S(2)}) copy-start(bf16[256,512]{1,0:T(8,128)(2,1)S(1)} %collective-permute-done.2.refs_2_) | copy-start | bytes 786436
  40.8 0.7 copy-start.18
  60.3 3.6 %copy-start.13 = (bf16[256,512]{1,0:T(8,128)(2,1)}, bf16[256,512]{1,0:T(8,128)(2,1)S(1)}, u32[]{:S(2)}) copy-start(bf16[256,512]{1,0:T(8,128)(2,1)S(1)} %collective-permute-done.1.refs_1_) | copy-start | bytes 786436
  60.3 21.6 %copy-start.1 = (bf16[256,2048]{1,0:T(8,128)(2,1)S(1)}, bf16[256,2048]{1,0:T(8,128)(2,1)}, u32[]{:S(2)}) copy-start(bf16[256,2048]{1,0:T(8,128)(2,1)} %u_in.3) | copy-start | bytes 3145732
  60.3 21.6 %copy-start.3 = (bf16[256,2048]{1,0:T(8,128)(2,1)S(1)}, bf16[256,2048]{1,0:T(8,128)(2,1)}, u32[]{:S(2)}) copy-start(bf16[256,2048]{1,0:T(8,128)(2,1)} %d_in.3) | copy-start | bytes 3145732
  60.4 21.6 %copy-start.8 = (f32[1,2048]{1,0:T(1,128)S(1)}, f32[1,2048]{1,0:T(1,128)}, u32[]{:S(2)}) copy-start(f32[1,2048]{1,0:T(1,128)} %constant.53.clone.mass_ref) | copy-start | bytes 24580
  60.4 21.6 %copy-start.9 = (f32[1,1024]{1,0:T(1,128)S(1)}, f32[1,1024]{1,0:T(1,128)}, u32[]{:S(2)}) copy-start(f32[1,1024]{1,0:T(1,128)} %constant.52.clone.weight_ref) | copy-start | bytes 12292
  60.4 32.3 %collective-permute-start.6 = (bf16[2,256,512]{2,1,0:T(8,128)(2,1)}, bf16[2,256,512]{2,1,0:T(8,128)(2,1)S(1)}, u32[]{:S(2)}, u32[]{:S(2)}) collective-permute-start(bf16[2,256,512]{2,1,0:T(8,128)(2,1)} %get-tuple-element.57), channel_id=1, source_target_pairs={{0,1},{1,0},{2,3},{3,2},{4,5},{5,4},{6,7},{7,6},{8,9},{9,8},{10,11... | collective-permute-start | bytes 1572872 | tf_op jit(solution)/shard_map/ppermute | solution.py:493
  60.5 36.7 %collective-permute-start.7 = (bf16[2,256,512]{2,1,0:T(8,128)(2,1)}, bf16[2,256,512]{2,1,0:T(8,128)(2,1)S(1)}, u32[]{:S(2)}, u32[]{:S(2)}) collective-permute-start(bf16[2,256,512]{2,1,0:T(8,128)(2,1)} %get-tuple-element.61), channel_id=1, source_target_pairs={{0,2},{1,3},{2,0},{3,1},{4,6},{5,7},{6,4},{7,5},{8,10},{9,11},{10,... | collective-permute-start | bytes 1572872 | tf_op jit(solution)/shard_map/ppermute | solution.py:493
  63.5 49.1 %collective-permute-start.8 = (bf16[2,256,512]{2,1,0:T(8,128)(2,1)}, bf16[2,256,512]{2,1,0:T(8,128)(2,1)}, u32[]{:S(2)}, u32[]{:S(2)}) collective-permute-start(bf16[2,256,512]{2,1,0:T(8,128)(2,1)} %get-tuple-element.62), channel_id=1, source_target_pairs={{0,3},{1,2},{2,1},{3,0},{4,7},{5,6},{6,5},{7,4},{8,11},{9,10},{10,... | collective-permute-start | bytes 1572872 | tf_op jit(solution)/shard_map/ppermute | solution.py:493
  63.9 0.7 copy-start.15
  64.7 0.7 copy-start.17
  82.0 10.7 %copy-start.12 = (bf16[1,256,512]{2,1,0:T(8,128)(2,1)S(1)}, bf16[1,256,512]{2,1,0:T(8,128)(2,1)}, u32[]{:S(2)}) copy-start(bf16[1,256,512]{2,1,0:T(8,128)(2,1)} %get-tuple-element.68) | copy-start | bytes 786436
  82.0 12.7 %copy-start.11 = (bf16[1,256,512]{2,1,0:T(8,128)(2,1)S(1)}, bf16[1,256,512]{2,1,0:T(8,128)(2,1)}, u32[]{:S(2)}) copy-start(bf16[1,256,512]{2,1,0:T(8,128)(2,1)} %get-tuple-element.69) | copy-start | bytes 786436
  82.0 13.2 %copy-start.10 = (bf16[1,256,512]{2,1,0:T(8,128)(2,1)S(1)}, bf16[1,256,512]{2,1,0:T(8,128)(2,1)}, u32[]{:S(2)}) copy-start(bf16[1,256,512]{2,1,0:T(8,128)(2,1)} %get-tuple-element.67) | copy-start | bytes 786436
  82.0 30.6 %copy-start.4 = (bf16[2,256,512]{2,1,0:T(8,128)(2,1)S(1)}, bf16[2,256,512]{2,1,0:T(8,128)(2,1)}, u32[]{:S(2)}) copy-start(bf16[2,256,512]{2,1,0:T(8,128)(2,1)} %get-tuple-element.49.refs_0_) | copy-start | bytes 1572868
  92.7 23.1 %collective-permute-start.10 = (bf16[1,256,512]{2,1,0:T(8,128)(2,1)S(1)}, bf16[1,256,512]{2,1,0:T(8,128)(2,1)S(1)}, u32[]{:S(2)}, u32[]{:S(2)}) collective-permute-start(bf16[1,256,512]{2,1,0:T(8,128)(2,1)S(1)} %copy-done.12), channel_id=1, source_target_pairs={{0,2},{1,3},{2,0},{3,1},{4,6},{5,7},{6,4},{7,5},{8,10},{9,11},{10,... | collective-permute-start | bytes 786440 | tf_op jit(solution)/shard_map/ppermute | solution.py:493
  94.7 23.4 %collective-permute-start.11 = (bf16[1,256,512]{2,1,0:T(8,128)(2,1)S(1)}, bf16[1,256,512]{2,1,0:T(8,128)(2,1)S(1)}, u32[]{:S(2)}, u32[]{:S(2)}) collective-permute-start(bf16[1,256,512]{2,1,0:T(8,128)(2,1)S(1)} %copy-done.11), channel_id=1, source_target_pairs={{0,3},{1,2},{2,1},{3,0},{4,7},{5,6},{6,5},{7,4},{8,11},{9,10},{10,... | collective-permute-start | bytes 786440 | tf_op jit(solution)/shard_map/ppermute | solution.py:493
  95.2 22.9 %collective-permute-start.9 = (bf16[1,256,512]{2,1,0:T(8,128)(2,1)S(1)}, bf16[1,256,512]{2,1,0:T(8,128)(2,1)S(1)}, u32[]{:S(2)}, u32[]{:S(2)}) collective-permute-start(bf16[1,256,512]{2,1,0:T(8,128)(2,1)S(1)} %copy-done.10), channel_id=1, source_target_pairs={{0,1},{1,0},{2,3},{3,2},{4,5},{5,4},{6,7},{7,6},{8,9},{9,8},{10,11... | collective-permute-start | bytes 786440 | tf_op jit(solution)/shard_map/ppermute | solution.py:493
  112.6 5.5 %copy-start.5 = (bf16[1,256,512]{2,1,0:T(8,128)(2,1)S(1)}, bf16[1,256,512]{2,1,0:T(8,128)(2,1)}, u32[]{:S(2)}) copy-start(bf16[1,256,512]{2,1,0:T(8,128)(2,1)} %get-tuple-element.66.refs_0_) | copy-start | bytes 786436

commit v4 on v3

--- a/solution.py
+++ b/solution.py
@@ -89,6 +89,19 @@
     high = value.astype(BF16)
     low = (value - high.astype(F32)).astype(BF16)
     return dot(jnp.concatenate([high, low, high], axis=1), table)
+
+
+def cut_kernel(modes, me_ref, field, *refs):
+    pieces, sem = refs[:-1], refs[-1]
+    me = me_ref[0]
+    width = pieces[0].shape[1]
+    copies = []
+    for d in range(1, modes):
+        at = pl.ds(pl.multiple_of(jnp.bitwise_xor(me, d) * width, width), width)
+        copies.append(pltpu.make_async_copy(field.at[:, at], pieces[d - 1], sem.at[d - 1]))
+        copies[-1].start()
+    for copy in copies:
+        copy.wait()
 
 
 def planes_kernel(modes, chunk, advected, me_ref, *refs):
@@ -443,49 +456,52 @@
         out_d[:, at] = scale * d_ref[:, at].astype(F32) - pulled[rows : 2 * rows, :]
 
 
-def finish_kernel(modes, width, with_local, me_ref, *refs):
+def finish_kernel(near, width, with_local, me_ref, *refs):
     fields = len(with_local)
     count = sum(with_local)
-    pieces, refs = refs[:modes], refs[modes:]
-    locals_in, outs = refs[:count], refs[count : count + fields]
-    result, sem = refs[count + fields :]
+    pieces, refs = refs[: len(near)], refs[len(near) :]
+    locals_in, outs = refs[:count], refs[-fields - 2 : -2]
+    result, sem = refs[-2:]
     me = me_ref[0]
-
-    def at(d):
-        return pl.ds(pl.multiple_of(jnp.bitwise_xor(me, d) * width, width), width)
-
     stores = []
-    for d in range(modes):
+    for n, d in enumerate(near):
+        at = pl.ds(pl.multiple_of(jnp.bitwise_xor(me, d) * width, width), width)
         seen = 0
         for f in range(fields):
-            value = pieces[d][f].astype(F32)
+            value = pieces[n][f].astype(F32)
             if with_local[f]:
-                value = value + locals_in[seen][:, at(d)]
+                value = value + locals_in[seen][:, at]
                 seen += 1
-            result[f, d] = value
-            stores.append(pltpu.make_async_copy(result.at[f, d], outs[f].at[:, at(d)], sem.at[f, d]))
+            result[f, n] = value
+            stores.append(pltpu.make_async_copy(result.at[f, n], outs[f].at[:, at], sem.at[f, n]))
             stores[-1].start()
     for store in stores:
         store.wait()
 
 
-def finish(pieces, local, me):
+def finish(pieces, near, local, me, begun=None):
     modes = len(pieces)
     fields, rows, width = pieces[0].shape
     with_local = tuple(part is not None for part in local)
     present = [part for part in local if part is not None]
+    operands = [me, *[pieces[d] for d in near], *present, *(begun or [])]
+    anywhere = pl.BlockSpec(memory_space=pl.ANY)
+    begin = len(operands) - fields
     return pl.pallas_call(
-        functools.partial(finish_kernel, modes, width, with_local),
+        functools.partial(finish_kernel, tuple(near), width, with_local),
         out_shape=[jax.ShapeDtypeStruct((rows, modes * width), F32)] * fields,
-        in_specs=[SMEM] + [VMEM] * (modes + len(present)),
-        out_specs=[pl.BlockSpec(memory_space=pl.ANY)] * fields,
+        in_specs=[SMEM]
+        + [VMEM] * (len(near) + len(present))
+        + [anywhere] * (fields if begun else 0),
+        out_specs=[anywhere] * fields,
+        input_output_aliases={begin + f: f for f in range(fields)} if begun else {},
         scratch_shapes=[
-            pltpu.VMEM((fields, modes, rows, width), F32),
-            pltpu.SemaphoreType.DMA((fields, modes)),
+            pltpu.VMEM((fields, len(near), rows, width), F32),
+            pltpu.SemaphoreType.DMA((fields, len(near))),
         ],
         compiler_params=pltpu.CompilerParams(vmem_limit_bytes=16 * MIB),
-        name="finish",
-    )(me, *pieces, *present)
+        name="finish_rest" if begun else "finish",
+    )(*operands)
 
 
 def swap_with(block, axis, distance):
@@ -529,12 +545,15 @@
     mass_row = jnp.asarray(mass.astype(np.float32)[None, :])
 
     def cut(field):
-        return [
-            lax.dynamic_slice_in_dim(
-                field, jnp.bitwise_xor(my_mode, d) * width, width, axis=1
-            )
-            for d in range(1, modes)
-        ]
+        return pl.pallas_call(
+            functools.partial(cut_kernel, modes),
+            out_shape=[jax.ShapeDtypeStruct((rows, width), BF16)] * (modes - 1),
+            in_specs=[SMEM, pl.BlockSpec(memory_space=pltpu.HBM)],
+            out_specs=[VMEM] * (modes - 1),
+            scratch_shapes=[pltpu.SemaphoreType.DMA((modes - 1,))],
+            compiler_params=pltpu.CompilerParams(vmem_limit_bytes=8 * MIB),
+            name="cut",
+        )(mode_id, field)
 
     order = [*range(2, modes), 1]
     u_cut = cut(u_spec)
@@ -607,8 +626,9 @@
     d_returned = [d_back[0]] + [None] * (modes - 1)
     for d in order:
         d_returned[d] = swap_with(d_back[d], "mode", d)
-    advect, helm_velocity = finish(u_returned, [None, local_u], mode_id)
-    (helm_direction,) = finish(d_returned, [local_d], mode_id)
+    advect, helm_velocity = finish(u_returned, range(modes), [None, local_u], mode_id)
+    begun = finish(d_returned, [0], [local_d], mode_id)
+    (helm_direction,) = finish(d_returned, range(1, modes), [local_d], mode_id, list(begun))
     return (advect, helm_velocity, helm_direction)
 
 

time: 120 us -> 120 us (level)
  waiting for transfers between devices: 35.5 us -> 33.8 us
  Pallas kernels: 55 us -> 56.4 us
    dynamic_slice x2 -> x0, local copies, waits for them, and re-layouts: 2.05 us -> none  [cut(): lax.dynamic_slice_in_dim(field, jnp.bitwise_xor(my_mode, d) * width, widt...]
    unnamed x39 -> x41, local copies, waits for them, and re-layouts: 4.89 us -> 6.6 us
    ppermute x12, waiting for transfers between devices: 35.5 us -> 33.8 us  [swap_with(): return lax.ppermute(block, axis, [(i, i ^ distance) for i in range(count)])]
    pallas_call x2 -> x5, Pallas kernels: 4.6 us -> 6.11 us  [the longest x3 5.22 us: finish(): pl.pallas_call(functools.partial(finish_kernel, tuple(near), width, with_...]
  transfers between devices with their start and end apart: 13 -> 13, of which waited for: 3 -> 3; matrix products, arithmetic and copies ran while one was open for 1% -> 1% of each run, Pallas kernels for 45% -> 46%
where the time goes in v4:
time: 120 us
  Pallas kernels  56.4 us (47%)
  waiting for transfers between devices  33.8 us (28%)
  starting transfers between devices  20.8 us (17%)
  local copies, waits for them, and re-layouts  6.71 us (6%)
    pallas_call x2, Pallas kernels, planes(): pl.pallas_call(functools.partial(planes_kernel, modes, chunk, advected),...  35.4 us
    ppermute x12, waiting for transfers between devices, swap_with(): return lax.ppermute(block, axis, [(i, i ^ distance) for i in range(count)])  33.8 us
    ppermute x12, starting transfers between devices, swap_with(): return lax.ppermute(block, axis, [(i, i ^ distance) for i in range(count)])  16.1 us
    pallas_call x1, Pallas kernels, on_device(): pl.pallas_call(functools.partial(penalty_kernel, parts, block_elements),...  10.6 us
    unnamed x41, local copies, waits for them, and re-layouts  6.6 us
    pallas_call x3, Pallas kernels, finish(): pl.pallas_call(functools.partial(finish_kernel, tuple(near), width, with_...  5.22 us
    all_to_all x1, starting transfers between devices, on_device(): lax.all_to_all(messages, 'elem', split_axis=0, concat_axis=0, tiled=True)  4.76 us
    pallas_call x1, Pallas kernels, on_device(): pl.pallas_call(functools.partial(traces_kernel, parts, block_elements), o...  4.32 us
  transfers between devices with their start and end apart: 13, of which 3 were waited for; matrix products, arithmetic and copies ran while one was open for 1% of the time, Pallas kernels for 46%

profile of v4, /device:TPU:10, one launch (start us, length us, event | category | flops | bytes accessed | tf_op | source)
XLA Modules:
  0.0 119.6 jit_solution(9094125286669221807)
XLA Ops:
  0.7 1.2 %copy-done = bf16[256,2048]{1,0:T(8,128)(2,1)S(1)} copy-done((bf16[256,2048]{1,0:T(8,128)(2,1)S(1)}, bf16[256,2048]{1,0:T(8,128)(2,1)}, u32[]{:S(2)}) %copy-start) | copy-done | bytes 1048600
  1.9 0.1 cut.3
  2.0 0.5 collective-permute-start
  2.5 2.6 %collective-permute-start.2 = (bf16[256,512]{1,0:T(8,128)(2,1)S(1)}, bf16[256,512]{1,0:T(8,128)(2,1)S(1)}, u32[]{:S(2)}, u32[]{:S(2)}) collective-permute-start(bf16[256,512]{1,0:T(8,128)(2,1)S(1)} %get-tuple-element.55), channel_id=1, source_target_pairs={{0,2},{1,3},{2,0},{3,1},{4,6},{5,7},{6,4},{7,5},{8,10},{9,11},{10,... | collective-permute-start | bytes 786440 | tf_op jit(solution)/shard_map/ppermute | solution.py:509
  5.1 0.4 collective-permute-start.3
  5.5 0.7 pad_add_fusion.row_ref
  6.2 0.1 copy.27
  6.3 1.2 %copy-done.3 = bf16[256,2048]{1,0:T(8,128)(2,1)S(1)} copy-done((bf16[256,2048]{1,0:T(8,128)(2,1)S(1)}, bf16[256,2048]{1,0:T(8,128)(2,1)}, u32[]{:S(2)}) %copy-start.3) | copy-done | bytes 1048600
  7.6 0.8 cut.2
  8.4 1.2 %copy-done.4 = bf16[256,2048]{1,0:T(8,128)(2,1)S(1)} copy-done((bf16[256,2048]{1,0:T(8,128)(2,1)S(1)}, bf16[256,2048]{1,0:T(8,128)(2,1)}, u32[]{:S(2)}) %copy-start.4) | copy-done | bytes 1048600
  9.6 4.3 %traces.1 = bf16[8,528,256]{2,1,0:T(8,128)(2,1)} custom-call(s32[1]{0:T(128)} %bitcast.1.me_ref, bf16[256,2048]{1,0:T(8,128)(2,1)S(1)} %copy-done.1, bf16[256,2048]{1,0:T(8,128)(2,1)S(1)} %copy-done.4, s32[4,128]{1,0:T(4,128)S(1)} %pad_add_fusion.row_ref, s32[128,4]{1,0:T(8,128)S(1)} %bitcast.5, s32[2,32]{1,0:T(2,128)S(1)} %copy-done.8), custom_call_target="tpu_custom_call" | custom-call | tf_op jit(solution)/shard_map/traces/pallas_call | solution.py:565
  14.0 0.7 copy-done.16
  14.7 4.8 %all-to-all-start = ((bf16[8,528,256]{2,1,0:T(8,128)(2,1)}), bf16[8,528,256]{2,1,0:T(8,128)(2,1)}, u32[]{:S(2)}, u32[]{:S(2)}) async-start(bf16[8,528,256]{2,1,0:T(8,128)(2,1)} %traces.1), calls=%async_computation | async-start | bytes 4325376 | tf_op jit(solution)/shard_map/all_to_all | solution.py:584
  19.5 1.3 %collective-permute-start.1 = (bf16[256,512]{1,0:T(8,128)(2,1)S(1)}, bf16[256,512]{1,0:T(8,128)(2,1)S(1)}, u32[]{:S(2)}, u32[]{:S(2)}) collective-permute-start(bf16[256,512]{1,0:T(8,128)(2,1)S(1)} %get-tuple-element.50), channel_id=1, source_target_pairs={{0,1},{1,0},{2,3},{3,2},{4,5},{5,4},{6,7},{7,6},{8,9},{9,8},{10,11... | collective-permute-start | bytes 786440 | tf_op jit(solution)/shard_map/ppermute | solution.py:509
  20.8 2.3 %collective-permute-start.4 = (bf16[256,512]{1,0:T(8,128)(2,1)}, bf16[256,512]{1,0:T(8,128)(2,1)S(1)}, u32[]{:S(2)}, u32[]{:S(2)}) collective-permute-start(bf16[256,512]{1,0:T(8,128)(2,1)} %get-tuple-element.63), channel_id=1, source_target_pairs={{0,2},{1,3},{2,0},{3,1},{4,6},{5,7},{6,4},{7,5},{8,10},{9,11},{10,... | collective-permute-start | bytes 786440 | tf_op jit(solution)/shard_map/ppermute | solution.py:509
  23.1 0.5 collective-permute-start.5
  23.6 16.3 %collective-permute-done.3.refs_3_ = bf16[256,512]{1,0:T(8,128)(2,1)S(1)} collective-permute-done((bf16[256,512]{1,0:T(8,128)(2,1)S(1)}, bf16[256,512]{1,0:T(8,128)(2,1)S(1)}, u32[]{:S(2)}, u32[]{:S(2)}) %collective-permute-start.3) | collective-permute-done | bytes 262176 | tf_op jit(solution)/shard_map/ppermute | solution.py:509
  39.9 0.7 copy-done.19
  40.6 18.8 %planes_moved.1 = (bf16[2,256,512]{2,1,0:T(8,128)(2,1)}, bf16[2,256,512]{2,1,0:T(8,128)(2,1)}, bf16[2,256,512]{2,1,0:T(8,128)(2,1)}, bf16[2,256,512]{2,1,0:T(8,128)(2,1)}) custom-call(s32[1]{0:T(128)} %bitcast.me_ref, bf16[256,2048]{1,0:T(8,128)(2,1)} %u_in.3, bf16[256,512]{1,0:T(8,128)(2,1)} %copy-done.16, bf16[256,512]{1,0:T(8,128)(2,1)} %copy-done.18, ...), custom_call_target="tpu_custom_call" | custom-call | flops 10200547328 | bytes 12582912 | tf_op jit(solution)/shard_map/planes_moved/pallas_call | solution.py:250
  59.6 3.9 %collective-permute-start.7 = (bf16[2,256,512]{2,1,0:T(8,128)(2,1)}, bf16[2,256,512]{2,1,0:T(8,128)(2,1)S(1)}, u32[]{:S(2)}, u32[]{:S(2)}) collective-permute-start(bf16[2,256,512]{2,1,0:T(8,128)(2,1)} %get-tuple-element.73), channel_id=1, source_target_pairs={{0,2},{1,3},{2,0},{3,1},{4,6},{5,7},{6,4},{7,5},{8,10},{9,11},{10,... | collective-permute-start | bytes 1572872 | tf_op jit(solution)/shard_map/ppermute | solution.py:509
  63.6 0.7 copy-done.15
  64.3 0.7 copy-done.17
  64.9 16.6 %planes_plain.1 = (bf16[1,256,512]{2,1,0:T(8,128)(2,1)}, bf16[1,256,512]{2,1,0:T(8,128)(2,1)}, bf16[1,256,512]{2,1,0:T(8,128)(2,1)}, bf16[1,256,512]{2,1,0:T(8,128)(2,1)}) custom-call(s32[1]{0:T(128)} %bitcast.me_ref, bf16[256,2048]{1,0:T(8,128)(2,1)} %d_in.3, bf16[256,512]{1,0:T(8,128)(2,1)} %copy-done.14, bf16[256,512]{1,0:T(8,128)(2,1)} %copy-done.15, ...), custom_call_target="tpu_custom_call" | custom-call | flops 9126805504 | bytes 12582912 | tf_op jit(solution)/shard_map/planes_plain/pallas_call | solution.py:250
  81.6 10.6 %penalty.1 = (f32[256,2048]{1,0:T(8,128)S(1)}, f32[256,2048]{1,0:T(8,128)S(1)}) custom-call(s32[1]{0:T(128)} %bitcast.1.me_ref, bf16[256,2048]{1,0:T(8,128)(2,1)S(1)} %copy-done.2, bf16[256,2048]{1,0:T(8,128)(2,1)S(1)} %copy-done.5, s32[4,128]{1,0:T(4,128)S(1)} %pad_add_fusion.row_ref, s32[128,4]{1,0:T(8,128)S(1)} %bitcast.6, s32[2,32]{1,0:T(2,128)S(1)} %copy-done.8, ...), custom_call_target="tpu_custom_call" | custom-call | flops 6442450944 | bytes 10485760 | tf_op jit(solution)/shard_map/penalty/pallas_call | solution.py:594
  92.3 2.5 %collective-permute-start.10 = (bf16[1,256,512]{2,1,0:T(8,128)(2,1)S(1)}, bf16[1,256,512]{2,1,0:T(8,128)(2,1)S(1)}, u32[]{:S(2)}, u32[]{:S(2)}) collective-permute-start(bf16[1,256,512]{2,1,0:T(8,128)(2,1)S(1)} %copy-done.13), channel_id=1, source_target_pairs={{0,2},{1,3},{2,0},{3,1},{4,6},{5,7},{6,4},{7,5},{8,10},{9,11},{10,... | collective-permute-start | bytes 786440 | tf_op jit(solution)/shard_map/ppermute | solution.py:509
  94.7 0.5 collective-permute-start.11
  95.3 1.5 %collective-permute-start.9 = (bf16[1,256,512]{2,1,0:T(8,128)(2,1)S(1)}, bf16[1,256,512]{2,1,0:T(8,128)(2,1)S(1)}, u32[]{:S(2)}, u32[]{:S(2)}) collective-permute-start(bf16[1,256,512]{2,1,0:T(8,128)(2,1)S(1)} %copy-done.11), channel_id=1, source_target_pairs={{0,1},{1,0},{2,3},{3,2},{4,5},{5,4},{6,7},{7,6},{8,9},{9,8},{10,11... | collective-permute-start | bytes 786440 | tf_op jit(solution)/shard_map/ppermute | solution.py:509
  96.7 0.9 finish.3.refs_4_
  97.6 15.1 %collective-permute-done.8.refs_3_ = bf16[2,256,512]{2,1,0:T(8,128)(2,1)} collective-permute-done((bf16[2,256,512]{2,1,0:T(8,128)(2,1)}, bf16[2,256,512]{2,1,0:T(8,128)(2,1)}, u32[]{:S(2)}, u32[]{:S(2)}) %collective-permute-start.8) | collective-permute-done | bytes 524320 | tf_op jit(solution)/shard_map/ppermute | solution.py:509
  112.6 3.1 %finish.2 = (f32[256,2048]{1,0:T(8,128)}, f32[256,2048]{1,0:T(8,128)}) custom-call(s32[1]{0:T(128)} %bitcast.me_ref, bf16[2,256,512]{2,1,0:T(8,128)(2,1)S(1)} %copy-done.6, bf16[2,256,512]{2,1,0:T(8,128)(2,1)S(1)} %collective-permute-done.6.refs_1_, bf16[2,256,512]{2,1,0:T(8,128)(2,1)S(1)} %collective-permute-done.7.refs_2_, ...), custom_call_target="tpu_custom_call" | custom-call | tf_op jit(solution)/shard_map/finish/pallas_call | solution.py:490
  115.8 2.4 %collective-permute-done.11.refs_2_ = bf16[1,256,512]{2,1,0:T(8,128)(2,1)S(1)} collective-permute-done((bf16[1,256,512]{2,1,0:T(8,128)(2,1)S(1)}, bf16[1,256,512]{2,1,0:T(8,128)(2,1)S(1)}, u32[]{:S(2)}, u32[]{:S(2)}) %collective-permute-start.11) | collective-permute-done | bytes 262176 | tf_op jit(solution)/shard_map/ppermute | solution.py:509
  118.2 1.2 %finish_rest.1 = f32[256,2048]{1,0:T(8,128)} custom-call(s32[1]{0:T(128)} %bitcast.me_ref, bf16[1,256,512]{2,1,0:T(8,128)(2,1)S(1)} %collective-permute-done.9.refs_0_, bf16[1,256,512]{2,1,0:T(8,128)(2,1)S(1)} %collective-permute-done.10.refs_1_, bf16[1,256,512]{2,1,0:T(8,128)(2,1)S(1)} %collective-permute-done.11.refs_2_, ...), custom_call_target="tpu_custom_call", output_to_operand_aliasing={{}: (5, {})} | custom-call | tf_op jit(solution)/shard_map/finish_rest/pallas_call | solution.py:490
  (46 shorter events, 0.3 us)
Async XLA Ops:
  0.6 7.7 %copy-start.8 = (s32[2,32]{1,0:T(2,128)S(1)}, s32[2,32]{1,0:T(2,128)}, u32[]{:S(2)}) copy-start(s32[2,32]{1,0:T(2,128)} %deg_ref.3) | copy-start | bytes 772
  0.6 1.2 %copy-start = (bf16[256,2048]{1,0:T(8,128)(2,1)S(1)}, bf16[256,2048]{1,0:T(8,128)(2,1)}, u32[]{:S(2)}) copy-start(bf16[256,2048]{1,0:T(8,128)(2,1)} %u_in.3) | copy-start | bytes 3145732
  1.9 6.5 %copy-start.1 = (bf16[256,2048]{1,0:T(8,128)(2,1)S(1)}, bf16[256,2048]{1,0:T(8,128)(2,1)}, u32[]{:S(2)}) copy-start(bf16[256,2048]{1,0:T(8,128)(2,1)} %u_in.3) | copy-start | bytes 3145732
  2.0 12.0 %collective-permute-start = (bf16[256,512]{1,0:T(8,128)(2,1)S(1)}, bf16[256,512]{1,0:T(8,128)(2,1)S(1)}, u32[]{:S(2)}, u32[]{:S(2)}) collective-permute-start(bf16[256,512]{1,0:T(8,128)(2,1)S(1)} %get-tuple-element.49), channel_id=1, source_target_pairs={{0,1},{1,0},{2,3},{3,2},{4,5},{5,4},{6,7},{7,6},{8,9},{9,8},{10,11... | collective-permute-start | bytes 786440 | tf_op jit(solution)/shard_map/ppermute | solution.py:509
  2.5 21.1 %collective-permute-start.2 = (bf16[256,512]{1,0:T(8,128)(2,1)S(1)}, bf16[256,512]{1,0:T(8,128)(2,1)S(1)}, u32[]{:S(2)}, u32[]{:S(2)}) collective-permute-start(bf16[256,512]{1,0:T(8,128)(2,1)S(1)} %get-tuple-element.55), channel_id=1, source_target_pairs={{0,2},{1,3},{2,0},{3,1},{4,6},{5,7},{6,4},{7,5},{8,10},{9,11},{10,... | collective-permute-start | bytes 786440 | tf_op jit(solution)/shard_map/ppermute | solution.py:509
  5.1 34.8 %collective-permute-start.3 = (bf16[256,512]{1,0:T(8,128)(2,1)S(1)}, bf16[256,512]{1,0:T(8,128)(2,1)S(1)}, u32[]{:S(2)}, u32[]{:S(2)}) collective-permute-start(bf16[256,512]{1,0:T(8,128)(2,1)S(1)} %get-tuple-element.56), channel_id=1, source_target_pairs={{0,3},{1,2},{2,1},{3,0},{4,7},{5,6},{6,5},{7,4},{8,11},{9,10},{10,... | collective-permute-start | bytes 786440 | tf_op jit(solution)/shard_map/ppermute | solution.py:509
  6.3 1.2 %copy-start.3 = (bf16[256,2048]{1,0:T(8,128)(2,1)S(1)}, bf16[256,2048]{1,0:T(8,128)(2,1)}, u32[]{:S(2)}) copy-start(bf16[256,2048]{1,0:T(8,128)(2,1)} %d_in.3) | copy-start | bytes 3145732
  8.4 1.2 %copy-start.4 = (bf16[256,2048]{1,0:T(8,128)(2,1)S(1)}, bf16[256,2048]{1,0:T(8,128)(2,1)}, u32[]{:S(2)}) copy-start(bf16[256,2048]{1,0:T(8,128)(2,1)} %d_in.3) | copy-start | bytes 3145732
  14.0 0.7 copy-start.16
  14.7 66.9 %all-to-all-start = ((bf16[8,528,256]{2,1,0:T(8,128)(2,1)}), bf16[8,528,256]{2,1,0:T(8,128)(2,1)}, u32[]{:S(2)}, u32[]{:S(2)}) async-start(bf16[8,528,256]{2,1,0:T(8,128)(2,1)} %traces.1), calls=%async_computation | async-start | bytes 4325376 | tf_op jit(solution)/shard_map/all_to_all | solution.py:584
  19.5 39.9 %collective-permute-start.1 = (bf16[256,512]{1,0:T(8,128)(2,1)S(1)}, bf16[256,512]{1,0:T(8,128)(2,1)S(1)}, u32[]{:S(2)}, u32[]{:S(2)}) collective-permute-start(bf16[256,512]{1,0:T(8,128)(2,1)S(1)} %get-tuple-element.50), channel_id=1, source_target_pairs={{0,1},{1,0},{2,3},{3,2},{4,5},{5,4},{6,7},{7,6},{8,9},{9,8},{10,11... | collective-permute-start | bytes 786440 | tf_op jit(solution)/shard_map/ppermute | solution.py:509
  20.8 42.8 %collective-permute-start.4 = (bf16[256,512]{1,0:T(8,128)(2,1)}, bf16[256,512]{1,0:T(8,128)(2,1)S(1)}, u32[]{:S(2)}, u32[]{:S(2)}) collective-permute-start(bf16[256,512]{1,0:T(8,128)(2,1)} %get-tuple-element.63), channel_id=1, source_target_pairs={{0,2},{1,3},{2,0},{3,1},{4,6},{5,7},{6,4},{7,5},{8,10},{9,11},{10,... | collective-permute-start | bytes 786440 | tf_op jit(solution)/shard_map/ppermute | solution.py:509
  23.1 40.5 %collective-permute-start.5 = (bf16[256,512]{1,0:T(8,128)(2,1)S(1)}, bf16[256,512]{1,0:T(8,128)(2,1)S(1)}, u32[]{:S(2)}, u32[]{:S(2)}) collective-permute-start(bf16[256,512]{1,0:T(8,128)(2,1)S(1)} %get-tuple-element.64), channel_id=1, source_target_pairs={{0,3},{1,2},{2,1},{3,0},{4,7},{5,6},{6,5},{7,4},{8,11},{9,10},{10,... | collective-permute-start | bytes 786440 | tf_op jit(solution)/shard_map/ppermute | solution.py:509
  23.6 16.3 %copy-start.18 = (bf16[256,512]{1,0:T(8,128)(2,1)}, bf16[256,512]{1,0:T(8,128)(2,1)S(1)}, u32[]{:S(2)}) copy-start(bf16[256,512]{1,0:T(8,128)(2,1)S(1)} %collective-permute-done.2.refs_2_) | copy-start | bytes 786436
  39.9 0.7 copy-start.19
  59.5 4.1 %copy-start.14 = (bf16[256,512]{1,0:T(8,128)(2,1)}, bf16[256,512]{1,0:T(8,128)(2,1)S(1)}, u32[]{:S(2)}) copy-start(bf16[256,512]{1,0:T(8,128)(2,1)S(1)} %collective-permute-done.1.refs_1_) | copy-start | bytes 786436
  59.5 22.1 %copy-start.2 = (bf16[256,2048]{1,0:T(8,128)(2,1)S(1)}, bf16[256,2048]{1,0:T(8,128)(2,1)}, u32[]{:S(2)}) copy-start(bf16[256,2048]{1,0:T(8,128)(2,1)} %u_in.3) | copy-start | bytes 3145732
  59.5 22.1 %copy-start.5 = (bf16[256,2048]{1,0:T(8,128)(2,1)S(1)}, bf16[256,2048]{1,0:T(8,128)(2,1)}, u32[]{:S(2)}) copy-start(bf16[256,2048]{1,0:T(8,128)(2,1)} %d_in.3) | copy-start | bytes 3145732
  59.5 22.1 %copy-start.9 = (f32[1,2048]{1,0:T(1,128)S(1)}, f32[1,2048]{1,0:T(1,128)}, u32[]{:S(2)}) copy-start(f32[1,2048]{1,0:T(1,128)} %constant.41.clone.mass_ref) | copy-start | bytes 24580
  59.5 22.1 %copy-start.10 = (f32[1,1024]{1,0:T(1,128)S(1)}, f32[1,1024]{1,0:T(1,128)}, u32[]{:S(2)}) copy-start(f32[1,1024]{1,0:T(1,128)} %constant.40.clone.weight_ref) | copy-start | bytes 12292
  59.5 32.7 %collective-permute-start.6 = (bf16[2,256,512]{2,1,0:T(8,128)(2,1)}, bf16[2,256,512]{2,1,0:T(8,128)(2,1)S(1)}, u32[]{:S(2)}, u32[]{:S(2)}) collective-permute-start(bf16[2,256,512]{2,1,0:T(8,128)(2,1)} %get-tuple-element.69), channel_id=1, source_target_pairs={{0,1},{1,0},{2,3},{3,2},{4,5},{5,4},{6,7},{7,6},{8,9},{9,8},{10,11... | collective-permute-start | bytes 1572872 | tf_op jit(solution)/shard_map/ppermute | solution.py:509
  59.6 38.0 %collective-permute-start.7 = (bf16[2,256,512]{2,1,0:T(8,128)(2,1)}, bf16[2,256,512]{2,1,0:T(8,128)(2,1)S(1)}, u32[]{:S(2)}, u32[]{:S(2)}) collective-permute-start(bf16[2,256,512]{2,1,0:T(8,128)(2,1)} %get-tuple-element.73), channel_id=1, source_target_pairs={{0,2},{1,3},{2,0},{3,1},{4,6},{5,7},{6,4},{7,5},{8,10},{9,11},{10,... | collective-permute-start | bytes 1572872 | tf_op jit(solution)/shard_map/ppermute | solution.py:509
  63.6 49.1 %collective-permute-start.8 = (bf16[2,256,512]{2,1,0:T(8,128)(2,1)}, bf16[2,256,512]{2,1,0:T(8,128)(2,1)}, u32[]{:S(2)}, u32[]{:S(2)}) collective-permute-start(bf16[2,256,512]{2,1,0:T(8,128)(2,1)} %get-tuple-element.74), channel_id=1, source_target_pairs={{0,3},{1,2},{2,1},{3,0},{4,7},{5,6},{6,5},{7,4},{8,11},{9,10},{10,... | collective-permute-start | bytes 1572872 | tf_op jit(solution)/shard_map/ppermute | solution.py:509
  63.6 0.7 copy-start.15
  81.6 10.6 %copy-start.13 = (bf16[1,256,512]{2,1,0:T(8,128)(2,1)S(1)}, bf16[1,256,512]{2,1,0:T(8,128)(2,1)}, u32[]{:S(2)}) copy-start(bf16[1,256,512]{2,1,0:T(8,128)(2,1)} %get-tuple-element.79) | copy-start | bytes 786436
  81.6 13.1 %copy-start.12 = (bf16[1,256,512]{2,1,0:T(8,128)(2,1)S(1)}, bf16[1,256,512]{2,1,0:T(8,128)(2,1)}, u32[]{:S(2)}) copy-start(bf16[1,256,512]{2,1,0:T(8,128)(2,1)} %get-tuple-element.80) | copy-start | bytes 786436
  81.6 13.6 %copy-start.11 = (bf16[1,256,512]{2,1,0:T(8,128)(2,1)S(1)}, bf16[1,256,512]{2,1,0:T(8,128)(2,1)}, u32[]{:S(2)}) copy-start(bf16[1,256,512]{2,1,0:T(8,128)(2,1)} %get-tuple-element.78) | copy-start | bytes 786436
  81.6 15.1 %copy-start.7 = (bf16[1,256,512]{2,1,0:T(8,128)(2,1)S(1)}, bf16[1,256,512]{2,1,0:T(8,128)(2,1)}, u32[]{:S(2)}) copy-start(bf16[1,256,512]{2,1,0:T(8,128)(2,1)} %get-tuple-element.82.refs_0_) | copy-start | bytes 786436
  92.2 20.4 %copy-start.6 = (bf16[2,256,512]{2,1,0:T(8,128)(2,1)S(1)}, bf16[2,256,512]{2,1,0:T(8,128)(2,1)}, u32[]{:S(2)}) copy-start(bf16[2,256,512]{2,1,0:T(8,128)(2,1)} %get-tuple-element.61.refs_0_) | copy-start | bytes 1572868
  92.3 23.6 %collective-permute-start.10 = (bf16[1,256,512]{2,1,0:T(8,128)(2,1)S(1)}, bf16[1,256,512]{2,1,0:T(8,128)(2,1)S(1)}, u32[]{:S(2)}, u32[]{:S(2)}) collective-permute-start(bf16[1,256,512]{2,1,0:T(8,128)(2,1)S(1)} %copy-done.13), channel_id=1, source_target_pairs={{0,2},{1,3},{2,0},{3,1},{4,6},{5,7},{6,4},{7,5},{8,10},{9,11},{10,... | collective-permute-start | bytes 786440 | tf_op jit(solution)/shard_map/ppermute | solution.py:509
  94.7 23.5 %collective-permute-start.11 = (bf16[1,256,512]{2,1,0:T(8,128)(2,1)S(1)}, bf16[1,256,512]{2,1,0:T(8,128)(2,1)S(1)}, u32[]{:S(2)}, u32[]{:S(2)}) collective-permute-start(bf16[1,256,512]{2,1,0:T(8,128)(2,1)S(1)} %copy-done.12), channel_id=1, source_target_pairs={{0,3},{1,2},{2,1},{3,0},{4,7},{5,6},{6,5},{7,4},{8,11},{9,10},{10,... | collective-permute-start | bytes 786440 | tf_op jit(solution)/shard_map/ppermute | solution.py:509
  95.3 23.0 %collective-permute-start.9 = (bf16[1,256,512]{2,1,0:T(8,128)(2,1)S(1)}, bf16[1,256,512]{2,1,0:T(8,128)(2,1)S(1)}, u32[]{:S(2)}, u32[]{:S(2)}) collective-permute-start(bf16[1,256,512]{2,1,0:T(8,128)(2,1)S(1)} %copy-done.11), channel_id=1, source_target_pairs={{0,1},{1,0},{2,3},{3,2},{4,5},{5,4},{6,7},{7,6},{8,9},{9,8},{10,11... | collective-permute-start | bytes 786440 | tf_op jit(solution)/shard_map/ppermute | solution.py:509
  (1 other events, 0.7 us)

commit v5 on v4

--- a/solution.py
+++ b/solution.py
@@ -622,7 +622,7 @@
         near,
     )
 
-    d_back, u_returned[1], local_d = lax.optimization_barrier((d_back, u_returned[1], local_d))
+    d_back, u_returned[1] = lax.optimization_barrier((d_back, u_returned[1]))
     d_returned = [d_back[0]] + [None] * (modes - 1)
     for d in order:
         d_returned[d] = swap_with(d_back[d], "mode", d)

time: 120 us -> 124 us (1.033)
  waiting for transfers between devices: 33.8 us -> 37.2 us
    ppermute x12, waiting for transfers between devices: 33.8 us -> 37.2 us  [swap_with(): return lax.ppermute(block, axis, [(i, i ^ distance) for i in range(count)])]
    unnamed x41 -> x35, local copies, waits for them, and re-layouts: 6.6 us -> 6.57 us
  transfers between devices with their start and end apart: 13 -> 13, of which waited for: 3 -> 3; matrix products, arithmetic and copies ran while one was open for 1% -> 1% of each run, Pallas kernels for 46% -> 44%
where the time goes in v5:
time: 124 us
  Pallas kernels  57.4 us (46%)
  waiting for transfers between devices  37.2 us (30%)
  starting transfers between devices  20.8 us (17%)
  local copies, waits for them, and re-layouts  6.68 us (5%)
    ppermute x12, waiting for transfers between devices, swap_with(): return lax.ppermute(block, axis, [(i, i ^ distance) for i in range(count)])  37.2 us
    pallas_call x2, Pallas kernels, planes(): pl.pallas_call(functools.partial(planes_kernel, modes, chunk, advected),...  35.4 us
    ppermute x12, starting transfers between devices, swap_with(): return lax.ppermute(block, axis, [(i, i ^ distance) for i in range(count)])  16.1 us
    pallas_call x1, Pallas kernels, on_device(): pl.pallas_call(functools.partial(penalty_kernel, parts, block_elements),...  10.5 us
    unnamed x35, local copies, waits for them, and re-layouts  6.57 us
    pallas_call x3, Pallas kernels, finish(): pl.pallas_call(functools.partial(finish_kernel, tuple(near), width, with_...  6.25 us
    all_to_all x1, starting transfers between devices, on_device(): lax.all_to_all(messages, 'elem', split_axis=0, concat_axis=0, tiled=True)  4.78 us
    pallas_call x1, Pallas kernels, on_device(): pl.pallas_call(functools.partial(traces_kernel, parts, block_elements), o...  4.29 us
  transfers between devices with their start and end apart: 13, of which 3 were waited for; matrix products, arithmetic and copies ran while one was open for 1% of the time, Pallas kernels for 44%

profile of v5, /device:TPU:10, one launch (start us, length us, event | category | flops | bytes accessed | tf_op | source)
XLA Modules:
  0.0 123.9 jit_solution(6518240503018887275)
XLA Ops:
  0.7 1.2 copy-done
  1.9 0.1 cut.3
  2.0 0.5 collective-permute-start
  2.5 2.6 %collective-permute-start.2 = (bf16[256,512]{1,0:T(8,128)(2,1)S(1)}, bf16[256,512]{1,0:T(8,128)(2,1)S(1)}, u32[]{:S(2)}, u32[]{:S(2)}) collective-permute-start(bf16[256,512]{1,0:T(8,128)(2,1)S(1)} %get-tuple-element.54), channel_id=1, source_target_pairs={{0,2},{1,3},{2,0},{3,1},{4,6},{5,7},{6,4},{7,5},{8,10},{9,11},{10,... | collective-permute-start | bytes 786440 | tf_op jit(solution)/shard_map/ppermute | solution.py:509
  5.1 0.4 collective-permute-start.3
  5.5 0.7 pad_add_fusion.row_ref
  6.2 0.1 copy.27
  6.3 1.2 copy-done.3
  7.6 0.8 cut.2
  8.4 1.2 copy-done.4
  9.6 4.3 %traces.1 = bf16[8,528,256]{2,1,0:T(8,128)(2,1)} custom-call(s32[1]{0:T(128)} %bitcast.1.me_ref, bf16[256,2048]{1,0:T(8,128)(2,1)S(1)} %copy-done.1, bf16[256,2048]{1,0:T(8,128)(2,1)S(1)} %copy-done.4, s32[4,128]{1,0:T(4,128)S(1)} %pad_add_fusion.row_ref, s32[128,4]{1,0:T(8,128)S(1)} %bitcast.5, s32[2,32]{1,0:T(2,128)S(1)} %copy-done.8), custom_call_target="tpu_custom_call" | custom-call | tf_op jit(solution)/shard_map/traces/pallas_call | solution.py:565
  13.9 0.7 copy-done.13
  14.6 4.8 %all-to-all-start = ((bf16[8,528,256]{2,1,0:T(8,128)(2,1)}), bf16[8,528,256]{2,1,0:T(8,128)(2,1)}, u32[]{:S(2)}, u32[]{:S(2)}) async-start(bf16[8,528,256]{2,1,0:T(8,128)(2,1)} %traces.1), calls=%async_computation | async-start | bytes 4325376 | tf_op jit(solution)/shard_map/all_to_all | solution.py:584
  19.5 1.3 %collective-permute-start.1 = (bf16[256,512]{1,0:T(8,128)(2,1)S(1)}, bf16[256,512]{1,0:T(8,128)(2,1)S(1)}, u32[]{:S(2)}, u32[]{:S(2)}) collective-permute-start(bf16[256,512]{1,0:T(8,128)(2,1)S(1)} %get-tuple-element.49), channel_id=1, source_target_pairs={{0,1},{1,0},{2,3},{3,2},{4,5},{5,4},{6,7},{7,6},{8,9},{9,8},{10,11... | collective-permute-start | bytes 786440 | tf_op jit(solution)/shard_map/ppermute | solution.py:509
  20.8 2.3 %collective-permute-start.4 = (bf16[256,512]{1,0:T(8,128)(2,1)}, bf16[256,512]{1,0:T(8,128)(2,1)S(1)}, u32[]{:S(2)}, u32[]{:S(2)}) collective-permute-start(bf16[256,512]{1,0:T(8,128)(2,1)} %get-tuple-element.62), channel_id=1, source_target_pairs={{0,2},{1,3},{2,0},{3,1},{4,6},{5,7},{6,4},{7,5},{8,10},{9,11},{10,... | collective-permute-start | bytes 786440 | tf_op jit(solution)/shard_map/ppermute | solution.py:509
  23.1 0.5 collective-permute-start.5
  23.6 16.3 %collective-permute-done.3.refs_3_ = bf16[256,512]{1,0:T(8,128)(2,1)S(1)} collective-permute-done((bf16[256,512]{1,0:T(8,128)(2,1)S(1)}, bf16[256,512]{1,0:T(8,128)(2,1)S(1)}, u32[]{:S(2)}, u32[]{:S(2)}) %collective-permute-start.3) | collective-permute-done | bytes 262176 | tf_op jit(solution)/shard_map/ppermute | solution.py:509
  39.9 0.7 copy-done.16
  40.6 18.8 %planes_moved.1 = (bf16[2,256,512]{2,1,0:T(8,128)(2,1)}, bf16[2,256,512]{2,1,0:T(8,128)(2,1)}, bf16[2,256,512]{2,1,0:T(8,128)(2,1)}, bf16[2,256,512]{2,1,0:T(8,128)(2,1)}) custom-call(s32[1]{0:T(128)} %bitcast.me_ref, bf16[256,2048]{1,0:T(8,128)(2,1)} %u_in.3, bf16[256,512]{1,0:T(8,128)(2,1)} %copy-done.13, bf16[256,512]{1,0:T(8,128)(2,1)} %copy-done.15, ...), custom_call_target="tpu_custom_call" | custom-call | flops 10200547328 | bytes 12582912 | tf_op jit(solution)/shard_map/planes_moved/pallas_call | solution.py:250
  59.6 3.9 %collective-permute-start.7 = (bf16[2,256,512]{2,1,0:T(8,128)(2,1)}, bf16[2,256,512]{2,1,0:T(8,128)(2,1)S(1)}, u32[]{:S(2)}, u32[]{:S(2)}) collective-permute-start(bf16[2,256,512]{2,1,0:T(8,128)(2,1)} %get-tuple-element.70), channel_id=1, source_target_pairs={{0,2},{1,3},{2,0},{3,1},{4,6},{5,7},{6,4},{7,5},{8,10},{9,11},{10,... | collective-permute-start | bytes 1572872 | tf_op jit(solution)/shard_map/ppermute | solution.py:509
  63.6 0.7 copy-done.12
  64.2 0.7 copy-done.14
  64.9 16.6 %planes_plain.1 = (bf16[1,256,512]{2,1,0:T(8,128)(2,1)}, bf16[1,256,512]{2,1,0:T(8,128)(2,1)}, bf16[1,256,512]{2,1,0:T(8,128)(2,1)}, bf16[1,256,512]{2,1,0:T(8,128)(2,1)}) custom-call(s32[1]{0:T(128)} %bitcast.me_ref, bf16[256,2048]{1,0:T(8,128)(2,1)} %d_in.3, bf16[256,512]{1,0:T(8,128)(2,1)} %copy-done.11, bf16[256,512]{1,0:T(8,128)(2,1)} %copy-done.12, ...), custom_call_target="tpu_custom_call" | custom-call | flops 9126805504 | bytes 12582912 | tf_op jit(solution)/shard_map/planes_plain/pallas_call | solution.py:250
  81.5 2.5 %collective-permute-start.10 = (bf16[1,256,512]{2,1,0:T(8,128)(2,1)}, bf16[1,256,512]{2,1,0:T(8,128)(2,1)S(1)}, u32[]{:S(2)}, u32[]{:S(2)}) collective-permute-start(bf16[1,256,512]{2,1,0:T(8,128)(2,1)} %get-tuple-element.77), channel_id=1, source_target_pairs={{0,2},{1,3},{2,0},{3,1},{4,6},{5,7},{6,4},{7,5},{8,10},{9,11},{10,... | collective-permute-start | bytes 786440 | tf_op jit(solution)/shard_map/ppermute | solution.py:509
  84.0 0.5 collective-permute-start.11
  84.5 1.5 %collective-permute-start.9 = (bf16[1,256,512]{2,1,0:T(8,128)(2,1)}, bf16[1,256,512]{2,1,0:T(8,128)(2,1)}, u32[]{:S(2)}, u32[]{:S(2)}) collective-permute-start(bf16[1,256,512]{2,1,0:T(8,128)(2,1)} %get-tuple-element.76), channel_id=1, source_target_pairs={{0,1},{1,0},{2,3},{3,2},{4,5},{5,4},{6,7},{7,6},{8,9},{9,8},{10,11... | collective-permute-start | bytes 786440 | tf_op jit(solution)/shard_map/ppermute | solution.py:509
  86.0 10.5 %penalty.1 = (f32[256,2048]{1,0:T(8,128)S(1)}, f32[256,2048]{1,0:T(8,128)S(1)}) custom-call(s32[1]{0:T(128)} %bitcast.1.me_ref, bf16[256,2048]{1,0:T(8,128)(2,1)S(1)} %copy-done.2, bf16[256,2048]{1,0:T(8,128)(2,1)S(1)} %copy-done.5, s32[4,128]{1,0:T(4,128)S(1)} %pad_add_fusion.row_ref, s32[128,4]{1,0:T(8,128)S(1)} %bitcast.6, s32[2,32]{1,0:T(2,128)S(1)} %copy-done.8, ...), custom_call_target="tpu_custom_call" | custom-call | flops 6442450944 | bytes 10485760 | tf_op jit(solution)/shard_map/penalty/pallas_call | solution.py:594
  96.6 0.9 finish.3.refs_4_
  97.5 17.1 %collective-permute-done.10.refs_1_ = bf16[1,256,512]{2,1,0:T(8,128)(2,1)S(1)} collective-permute-done((bf16[1,256,512]{2,1,0:T(8,128)(2,1)}, bf16[1,256,512]{2,1,0:T(8,128)(2,1)S(1)}, u32[]{:S(2)}, u32[]{:S(2)}) %collective-permute-start.10) | collective-permute-done | bytes 262176 | tf_op jit(solution)/shard_map/ppermute | solution.py:509
  114.6 3.7 %collective-permute-done.11.refs_2_ = bf16[1,256,512]{2,1,0:T(8,128)(2,1)} collective-permute-done((bf16[1,256,512]{2,1,0:T(8,128)(2,1)}, bf16[1,256,512]{2,1,0:T(8,128)(2,1)}, u32[]{:S(2)}, u32[]{:S(2)}) %collective-permute-start.11) | collective-permute-done | bytes 262176 | tf_op jit(solution)/shard_map/ppermute | solution.py:509
  118.3 2.2 %finish_rest.1 = f32[256,2048]{1,0:T(8,128)} custom-call(s32[1]{0:T(128)} %bitcast.me_ref, bf16[1,256,512]{2,1,0:T(8,128)(2,1)} %collective-permute-done.9.refs_0_, bf16[1,256,512]{2,1,0:T(8,128)(2,1)S(1)} %collective-permute-done.10.refs_1_, bf16[1,256,512]{2,1,0:T(8,128)(2,1)} %collective-permute-done.11.refs_2_, ...), custom_call_target="tpu_custom_call", output_to_operand_aliasing={{}: (5, {})} | custom-call | tf_op jit(solution)/shard_map/finish_rest/pallas_call | solution.py:490
  120.6 3.1 %finish.2 = (f32[256,2048]{1,0:T(8,128)}, f32[256,2048]{1,0:T(8,128)}) custom-call(s32[1]{0:T(128)} %bitcast.me_ref, bf16[2,256,512]{2,1,0:T(8,128)(2,1)S(1)} %copy-done.6, bf16[2,256,512]{2,1,0:T(8,128)(2,1)S(1)} %collective-permute-done.6.refs_1_, bf16[2,256,512]{2,1,0:T(8,128)(2,1)S(1)} %collective-permute-done.7.refs_2_, ...), custom_call_target="tpu_custom_call" | custom-call | tf_op jit(solution)/shard_map/finish/pallas_call | solution.py:490
  (40 shorter events, 0.3 us)
Async XLA Ops:
  0.6 7.7 %copy-start.8 = (s32[2,32]{1,0:T(2,128)S(1)}, s32[2,32]{1,0:T(2,128)}, u32[]{:S(2)}) copy-start(s32[2,32]{1,0:T(2,128)} %deg_ref.3) | copy-start | bytes 772
  0.6 1.2 copy-start
  1.9 6.5 %copy-start.1 = (bf16[256,2048]{1,0:T(8,128)(2,1)S(1)}, bf16[256,2048]{1,0:T(8,128)(2,1)}, u32[]{:S(2)}) copy-start(bf16[256,2048]{1,0:T(8,128)(2,1)} %u_in.3) | copy-start | bytes 3145732
  2.0 11.9 %collective-permute-start = (bf16[256,512]{1,0:T(8,128)(2,1)S(1)}, bf16[256,512]{1,0:T(8,128)(2,1)S(1)}, u32[]{:S(2)}, u32[]{:S(2)}) collective-permute-start(bf16[256,512]{1,0:T(8,128)(2,1)S(1)} %get-tuple-element.48), channel_id=1, source_target_pairs={{0,1},{1,0},{2,3},{3,2},{4,5},{5,4},{6,7},{7,6},{8,9},{9,8},{10,11... | collective-permute-start | bytes 786440 | tf_op jit(solution)/shard_map/ppermute | solution.py:509
  2.5 21.1 %collective-permute-start.2 = (bf16[256,512]{1,0:T(8,128)(2,1)S(1)}, bf16[256,512]{1,0:T(8,128)(2,1)S(1)}, u32[]{:S(2)}, u32[]{:S(2)}) collective-permute-start(bf16[256,512]{1,0:T(8,128)(2,1)S(1)} %get-tuple-element.54), channel_id=1, source_target_pairs={{0,2},{1,3},{2,0},{3,1},{4,6},{5,7},{6,4},{7,5},{8,10},{9,11},{10,... | collective-permute-start | bytes 786440 | tf_op jit(solution)/shard_map/ppermute | solution.py:509
  5.1 34.8 %collective-permute-start.3 = (bf16[256,512]{1,0:T(8,128)(2,1)S(1)}, bf16[256,512]{1,0:T(8,128)(2,1)S(1)}, u32[]{:S(2)}, u32[]{:S(2)}) collective-permute-start(bf16[256,512]{1,0:T(8,128)(2,1)S(1)} %get-tuple-element.55), channel_id=1, source_target_pairs={{0,3},{1,2},{2,1},{3,0},{4,7},{5,6},{6,5},{7,4},{8,11},{9,10},{10,... | collective-permute-start | bytes 786440 | tf_op jit(solution)/shard_map/ppermute | solution.py:509
  6.3 1.2 copy-start.3
  8.4 1.2 copy-start.4
  13.9 0.7 copy-start.13
  14.6 71.3 %all-to-all-start = ((bf16[8,528,256]{2,1,0:T(8,128)(2,1)}), bf16[8,528,256]{2,1,0:T(8,128)(2,1)}, u32[]{:S(2)}, u32[]{:S(2)}) async-start(bf16[8,528,256]{2,1,0:T(8,128)(2,1)} %traces.1), calls=%async_computation | async-start | bytes 4325376 | tf_op jit(solution)/shard_map/all_to_all | solution.py:584
  19.5 40.0 %collective-permute-start.1 = (bf16[256,512]{1,0:T(8,128)(2,1)S(1)}, bf16[256,512]{1,0:T(8,128)(2,1)S(1)}, u32[]{:S(2)}, u32[]{:S(2)}) collective-permute-start(bf16[256,512]{1,0:T(8,128)(2,1)S(1)} %get-tuple-element.49), channel_id=1, source_target_pairs={{0,1},{1,0},{2,3},{3,2},{4,5},{5,4},{6,7},{7,6},{8,9},{9,8},{10,11... | collective-permute-start | bytes 786440 | tf_op jit(solution)/shard_map/ppermute | solution.py:509
  20.8 42.7 %collective-permute-start.4 = (bf16[256,512]{1,0:T(8,128)(2,1)}, bf16[256,512]{1,0:T(8,128)(2,1)S(1)}, u32[]{:S(2)}, u32[]{:S(2)}) collective-permute-start(bf16[256,512]{1,0:T(8,128)(2,1)} %get-tuple-element.62), channel_id=1, source_target_pairs={{0,2},{1,3},{2,0},{3,1},{4,6},{5,7},{6,4},{7,5},{8,10},{9,11},{10,... | collective-permute-start | bytes 786440 | tf_op jit(solution)/shard_map/ppermute | solution.py:509
  23.1 40.5 %collective-permute-start.5 = (bf16[256,512]{1,0:T(8,128)(2,1)S(1)}, bf16[256,512]{1,0:T(8,128)(2,1)S(1)}, u32[]{:S(2)}, u32[]{:S(2)}) collective-permute-start(bf16[256,512]{1,0:T(8,128)(2,1)S(1)} %get-tuple-element.63), channel_id=1, source_target_pairs={{0,3},{1,2},{2,1},{3,0},{4,7},{5,6},{6,5},{7,4},{8,11},{9,10},{10,... | collective-permute-start | bytes 786440 | tf_op jit(solution)/shard_map/ppermute | solution.py:509
  23.6 16.3 %copy-start.15 = (bf16[256,512]{1,0:T(8,128)(2,1)}, bf16[256,512]{1,0:T(8,128)(2,1)S(1)}, u32[]{:S(2)}) copy-start(bf16[256,512]{1,0:T(8,128)(2,1)S(1)} %collective-permute-done.2.refs_2_) | copy-start | bytes 786436
  39.9 0.7 copy-start.16
  59.5 4.1 %copy-start.11 = (bf16[256,512]{1,0:T(8,128)(2,1)}, bf16[256,512]{1,0:T(8,128)(2,1)S(1)}, u32[]{:S(2)}) copy-start(bf16[256,512]{1,0:T(8,128)(2,1)S(1)} %collective-permute-done.1.refs_1_) | copy-start | bytes 786436
  59.5 26.5 %copy-start.2 = (bf16[256,2048]{1,0:T(8,128)(2,1)S(1)}, bf16[256,2048]{1,0:T(8,128)(2,1)}, u32[]{:S(2)}) copy-start(bf16[256,2048]{1,0:T(8,128)(2,1)} %u_in.3) | copy-start | bytes 3145732
  59.5 26.5 %copy-start.5 = (bf16[256,2048]{1,0:T(8,128)(2,1)S(1)}, bf16[256,2048]{1,0:T(8,128)(2,1)}, u32[]{:S(2)}) copy-start(bf16[256,2048]{1,0:T(8,128)(2,1)} %d_in.3) | copy-start | bytes 3145732
  59.5 26.5 %copy-start.9 = (f32[1,2048]{1,0:T(1,128)S(1)}, f32[1,2048]{1,0:T(1,128)}, u32[]{:S(2)}) copy-start(f32[1,2048]{1,0:T(1,128)} %constant.41.clone.mass_ref) | copy-start | bytes 24580
  59.5 26.5 %copy-start.10 = (f32[1,1024]{1,0:T(1,128)S(1)}, f32[1,1024]{1,0:T(1,128)}, u32[]{:S(2)}) copy-start(f32[1,1024]{1,0:T(1,128)} %constant.40.clone.weight_ref) | copy-start | bytes 12292
  59.5 22.0 %collective-permute-start.6 = (bf16[2,256,512]{2,1,0:T(8,128)(2,1)}, bf16[2,256,512]{2,1,0:T(8,128)(2,1)S(1)}, u32[]{:S(2)}, u32[]{:S(2)}) collective-permute-start(bf16[2,256,512]{2,1,0:T(8,128)(2,1)} %get-tuple-element.68), channel_id=1, source_target_pairs={{0,1},{1,0},{2,3},{3,2},{4,5},{5,4},{6,7},{7,6},{8,9},{9,8},{10,11... | collective-permute-start | bytes 1572872 | tf_op jit(solution)/shard_map/ppermute | solution.py:509
  59.6 60.9 %collective-permute-start.7 = (bf16[2,256,512]{2,1,0:T(8,128)(2,1)}, bf16[2,256,512]{2,1,0:T(8,128)(2,1)S(1)}, u32[]{:S(2)}, u32[]{:S(2)}) collective-permute-start(bf16[2,256,512]{2,1,0:T(8,128)(2,1)} %get-tuple-element.70), channel_id=1, source_target_pairs={{0,2},{1,3},{2,0},{3,1},{4,6},{5,7},{6,4},{7,5},{8,10},{9,11},{10,... | collective-permute-start | bytes 1572872 | tf_op jit(solution)/shard_map/ppermute | solution.py:509
  63.5 57.0 %collective-permute-start.8 = (bf16[2,256,512]{2,1,0:T(8,128)(2,1)}, bf16[2,256,512]{2,1,0:T(8,128)(2,1)}, u32[]{:S(2)}, u32[]{:S(2)}) collective-permute-start(bf16[2,256,512]{2,1,0:T(8,128)(2,1)} %get-tuple-element.71), channel_id=1, source_target_pairs={{0,3},{1,2},{2,1},{3,0},{4,7},{5,6},{6,5},{7,4},{8,11},{9,10},{10,... | collective-permute-start | bytes 1572872 | tf_op jit(solution)/shard_map/ppermute | solution.py:509
  63.5 0.7 copy-start.12
  64.2 0.7 copy-start.14
  81.5 33.0 %collective-permute-start.10 = (bf16[1,256,512]{2,1,0:T(8,128)(2,1)}, bf16[1,256,512]{2,1,0:T(8,128)(2,1)S(1)}, u32[]{:S(2)}, u32[]{:S(2)}) collective-permute-start(bf16[1,256,512]{2,1,0:T(8,128)(2,1)} %get-tuple-element.77), channel_id=1, source_target_pairs={{0,2},{1,3},{2,0},{3,1},{4,6},{5,7},{6,4},{7,5},{8,10},{9,11},{10,... | collective-permute-start | bytes 786440 | tf_op jit(solution)/shard_map/ppermute | solution.py:509
  84.0 34.3 %collective-permute-start.11 = (bf16[1,256,512]{2,1,0:T(8,128)(2,1)}, bf16[1,256,512]{2,1,0:T(8,128)(2,1)}, u32[]{:S(2)}, u32[]{:S(2)}) collective-permute-start(bf16[1,256,512]{2,1,0:T(8,128)(2,1)} %get-tuple-element.78), channel_id=1, source_target_pairs={{0,3},{1,2},{2,1},{3,0},{4,7},{5,6},{6,5},{7,4},{8,11},{9,10},{10,... | collective-permute-start | bytes 786440 | tf_op jit(solution)/shard_map/ppermute | solution.py:509
  84.5 33.8 %collective-permute-start.9 = (bf16[1,256,512]{2,1,0:T(8,128)(2,1)}, bf16[1,256,512]{2,1,0:T(8,128)(2,1)}, u32[]{:S(2)}, u32[]{:S(2)}) collective-permute-start(bf16[1,256,512]{2,1,0:T(8,128)(2,1)} %get-tuple-element.76), channel_id=1, source_target_pairs={{0,1},{1,0},{2,3},{3,2},{4,5},{5,4},{6,7},{7,6},{8,9},{9,8},{10,11... | collective-permute-start | bytes 786440 | tf_op jit(solution)/shard_map/ppermute | solution.py:509
  86.0 10.6 %copy-start.7 = (bf16[1,256,512]{2,1,0:T(8,128)(2,1)S(1)}, bf16[1,256,512]{2,1,0:T(8,128)(2,1)}, u32[]{:S(2)}) copy-start(bf16[1,256,512]{2,1,0:T(8,128)(2,1)} %get-tuple-element.80.refs_0_) | copy-start | bytes 786436
  97.5 23.1 %copy-start.6 = (bf16[2,256,512]{2,1,0:T(8,128)(2,1)S(1)}, bf16[2,256,512]{2,1,0:T(8,128)(2,1)}, u32[]{:S(2)}) copy-start(bf16[2,256,512]{2,1,0:T(8,128)(2,1)} %get-tuple-element.60.refs_0_) | copy-start | bytes 1572868
